TPU v7x, 32 devices: a whole 2x2x4 slice. The times are simulated.
32 devices in a mesh: seq: 8 (over z, core), mod: 4 (over y, x).
Axes of the slice: x: 2, y: 2, z: 4, core: 2. Of those that a mesh axis runs over, the one named last changes fastest.
Arguments:
- tokens: bfloat16 [4096, 2048], P(('seq', 'mod')), may hold values from -6 to 6
- modality: int32 [4096], P('seq'), may hold values from 0 to 2, as said below
- lengths: int32 [2], replicated, may hold values from 256 to 3840, as said below
- norm_gain: bfloat16 [2048], replicated, may hold values from 0.5 to 1.5
- input_weight: bfloat16 [3, 2048, 2, 4096], P(None, 'seq', None, 'mod'), may hold values from -0.125 to 0.125
- param_weight: bfloat16 [3, 4096, 160], P(None, ('mod', 'seq')), may hold values from -0.09375 to 0.09375
- step_weight: bfloat16 [3, 128, 4096], P(None, None, ('mod', 'seq')), may hold values from -0.5 to 0.5
- step_bias: bfloat16 [3, 4096], P(None, ('mod', 'seq')), may hold values from -14 to -2
- output_weight: bfloat16 [3, 4096, 2048], P(None, 'mod', 'seq'), may hold values from -0.25 to 0.25
- conv_weight: bfloat16 [4, 4096], P(None, ('mod', 'seq')), may hold values from -3 to 3
- conv_bias: bfloat16 [4096], P(('mod', 'seq')), may hold values from -3 to 3
- decay_log: bfloat16 [16, 4096], P(None, ('mod', 'seq')), may hold values from 0 to 1.5
- skip_gain: bfloat16 [4096], P(('mod', 'seq')), may hold values from 0.5 to 1.5
- cotangent: bfloat16 [4096, 2048], P(('seq', 'mod')), may hold values from -6 to 6
Outputs:
- output: bfloat16 [4096, 2048], P(('seq', 'mod'))
- grad_tokens: float32 [4096, 2048], P(('seq', 'mod'))
- grad_norm_gain: float32 [2048], replicated
- grad_input_weight: float32 [3, 2048, 2, 4096], P(None, 'seq', None, 'mod')
- grad_param_weight: float32 [3, 4096, 160], P(None, ('mod', 'seq'))
- grad_step_weight: float32 [3, 128, 4096], P(None, None, ('mod', 'seq'))
- grad_output_weight: float32 [3, 4096, 2048], P(None, 'mod', 'seq')
- grad_conv_weight: float32 [4, 4096], P(None, ('mod', 'seq'))
- grad_conv_bias: float32 [4096], P(('mod', 'seq'))
- grad_decay_log: float32 [16, 4096], P(None, ('mod', 'seq'))
- grad_skip_gain: float32 [4096], P(('mod', 'seq'))
- grad_step_bias: float32 [3, 4096], P(None, ('mod', 'seq'))
Inputs may be any that keep to these rules, and one draw needn't show every extreme that they name: In each aligned block of 128 tokens no modality has more than 48 tokens, and one modality has exactly 48. The two lengths sum to 4096; one of them is shorter than 512.
All inputs are finite; a program needn't handle non-finite values.
Results may differ from a plain program's by a relative error of at most 0.0078.
The roundings to bfloat16 on the way count: a program that leaves them out, or rounds other values in their place, can miss the bound.
Values may be sent and summed in bfloat16 or wider, within the bound.
No kernel may reach another device: no remote copies, remote signals or barrier semaphores. Data moves between devices by JAX's collectives and lax.ppermute only.
A program may use at most 576 MiB of HBM per device.

v0:
```python
import functools
import math

import jax
import jax.numpy as jnp
from jax import lax
from jax.experimental import pallas as pl
from jax.experimental.pallas import tpu as pltpu
from jax.sharding import PartitionSpec as P

N = 16
KW = 4
R = 128
MODS = 3
TOK_DEV = 128
CAPD = 48


EPSILON = 1e-05
SCAN_ROWS = 512

LANES = 128
SEGMENTS = 8
CHUNK = 32
UNROLL = 8
BACK = 4
COLUMNS = 4
FAR = 1e9
VMEM_BYTES = 60 * 1024 * 1024
f32 = jnp.float32
bf16 = jnp.bfloat16


def shifted_2(value, axis, by):
    size = lax.axis_size(axis)
    pairs = [(i, i + by) for i in range(size) if 0 <= i + by < size]
    return lax.ppermute(value, axis, pairs)


def carried_in(value, axis, combine, identity):
    size, here = (lax.axis_size(axis), lax.axis_index(axis))
    everything = jax.tree.map(
        lambda part, kind: lax.all_gather(part.astype(kind), axis),
        value,
        (jnp.bfloat16, jnp.bfloat16),
    )
    start = jax.tree.map(
        lambda part, zero: jnp.broadcast_to(jnp.asarray(zero, part.dtype), part.shape),
        value,
        identity,
    )

    def carried_hop(k, before):
        reached = k < here
        new = combine(
            before, jax.tree.map(lambda part, own: part[k].astype(own.dtype), everything, value)
        )
        return jax.tree.map(lambda a, b: jnp.where(reached, a, b), new, before)

    return lax.fori_loop(0, size, carried_hop, start)


def prefix(value, axis, combine, identity):
    size, here = (lax.axis_size(axis), lax.axis_index(axis))
    everything = jax.tree.map(lambda part: lax.all_gather(part, axis), value)
    start = jax.tree.map(
        lambda part, zero: jnp.broadcast_to(jnp.asarray(zero, part.dtype), part.shape),
        value,
        identity,
    )

    def prefix_hop(k, before):
        at = size - 1 - k
        reached = at > here
        new = combine(before, jax.tree.map(lambda part: part[at], everything))
        return jax.tree.map(lambda a, b: jnp.where(reached, a, b), new, before)

    return lax.fori_loop(0, size, prefix_hop, start)


def split_rows(count_rows):
    return (count_rows // TOK_DEV, TOK_DEV)


def slot_tables(modal_ids, capacity):
    sub_rows = modal_ids.shape[1]
    marked = (modal_ids[:, :, None] == jnp.arange(MODS, dtype=jnp.int32)[None, None, :]).astype(
        jnp.int32
    )
    ranking = jnp.sum((jnp.cumsum(marked, axis=1) - 1) * marked, axis=2)
    slot_ids = modal_ids * capacity + ranking
    positions = jnp.broadcast_to(jnp.arange(sub_rows, dtype=jnp.int32)[None, :], modal_ids.shape)
    unfilled = jnp.full((modal_ids.shape[0], MODS * capacity), sub_rows, jnp.int32)
    tables = jax.vmap(lambda table_row, slot_row, place_row: table_row.at[slot_row].set(place_row))(
        unfilled, slot_ids, positions
    )
    return (tables, slot_ids)


def group_rows(values, tables, capacity):
    padded = jnp.concatenate([values, jnp.zeros_like(values[:, :1])], axis=1)
    picked = jax.vmap(lambda block_values, block_table: block_values[block_table])(padded, tables)
    return picked.reshape(values.shape[0], MODS, capacity, values.shape[2])


def ungroup_rows(grouped, slot_ids):
    flattened = grouped.reshape(grouped.shape[0], MODS * grouped.shape[2], grouped.shape[3])
    return jax.vmap(lambda block_values, block_slots: block_values[block_slots])(
        flattened, slot_ids
    )


def modal_product(values, modal_ids, weight, transpose):
    count_rows = values.shape[0]
    sub_count, sub_rows = split_rows(count_rows)
    capacity = min(CAPD, sub_rows)
    tables, slot_ids = slot_tables(modal_ids.reshape(sub_count, sub_rows), capacity)
    grouped = group_rows(values.reshape(sub_count, sub_rows, values.shape[1]), tables, capacity)
    if transpose:
        result = jnp.einsum("gmcn,mkn->gmck", grouped, weight, preferred_element_type=jnp.float32)
    else:
        result = jnp.einsum("gmck,mkn->gmcn", grouped, weight, preferred_element_type=jnp.float32)
    return ungroup_rows(result, slot_ids).reshape(count_rows, result.shape[3])


def modal_outer(left, right, modal_ids):
    count_rows = left.shape[0]
    sub_count, sub_rows = split_rows(count_rows)
    capacity = min(CAPD, sub_rows)
    tables, slot_ids = slot_tables(modal_ids.reshape(sub_count, sub_rows), capacity)
    left_grouped = group_rows(left.reshape(sub_count, sub_rows, left.shape[1]), tables, capacity)
    right_grouped = group_rows(right.reshape(sub_count, sub_rows, right.shape[1]), tables, capacity)
    return jnp.einsum(
        "gmcl,gmcr->mlr", left_grouped, right_grouped, preferred_element_type=jnp.float32
    )


def modal_table(table, modal_ids):
    picked = jnp.zeros((modal_ids.shape[0], table.shape[1]), jnp.float32)
    for modal_index in range(MODS):
        picked = (
            picked
            + (modal_ids == modal_index).astype(jnp.float32)[:, None] * table[modal_index][None, :]
        )
    return picked


def modal_sums(values, modal_ids):
    return jnp.stack(
        [
            jnp.sum(values * (modal_ids == modal_index).astype(jnp.float32)[:, None], axis=0)
            for modal_index in range(MODS)
        ]
    )


def pair_combine(earlier, later):
    return (earlier[0] * later[0], later[0] * earlier[1] + later[1])


def back_combine(earlier, later):
    return (earlier[0] * later[0], later[1] + later[0] * earlier[1])


def silu_slope(values):
    sigmoid_part = jax.nn.sigmoid(values)
    return sigmoid_part * (1.0 + values * (1.0 - sigmoid_part))


def local(
    tokens,
    modality,
    lengths,
    norm_gain,
    input_weight,
    param_weight,
    step_weight,
    step_bias,
    output_weight,
    conv_weight,
    conv_bias,
    decay_log,
    skip_gain,
    cotangent,
):
    block_rows = modality.shape[0]
    gathered = (
        lax.all_gather(input_weight, "seq", axis=1, tiled=True),
        lax.all_gather(param_weight, "seq", axis=1, tiled=True),
        lax.all_gather(step_weight, "seq", axis=2, tiled=True),
        lax.all_gather(output_weight, "seq", axis=2, tiled=True),
        lax.all_gather(conv_weight, "seq", axis=1, tiled=True),
        lax.all_gather(conv_bias, "seq", axis=0, tiled=True),
        lax.all_gather(decay_log, "seq", axis=1, tiled=True),
        lax.all_gather(skip_gain, "seq", axis=0, tiled=True),
        lax.all_gather(step_bias, "seq", axis=1, tiled=True),
    )
    in_local = gathered[0]
    param_local = gathered[1]
    step_local = gathered[2]
    out_local = gathered[3]
    tap_weights = gathered[4].astype(jnp.float32)
    tap_bias = gathered[5].astype(jnp.float32)
    decay_rate = -jnp.exp(gathered[6].astype(jnp.float32))
    skip_local = gathered[7].astype(jnp.float32)
    bias_local = gathered[8].astype(jnp.float32)
    channels = in_local.shape[3]
    model_width = in_local.shape[1]
    in_flat = in_local.reshape(MODS, model_width, 2 * channels)
    token_vals = tokens.astype(jnp.float32)
    inverse = lax.rsqrt(jnp.mean(token_vals * token_vals, axis=1, keepdims=True) + EPSILON)
    normal_rows = token_vals * inverse
    gain_vals = norm_gain.astype(jnp.float32)
    normed = (normal_rows * gain_vals[None, :]).astype(jnp.bfloat16)
    piece = lax.all_gather(normed, "mod", axis=0, tiled=True)
    piece_ids = modality
    product = modal_product(piece, piece_ids, in_flat, False)
    filled = product
    folded = (filled, piece)
    expanded = folded[0].reshape(block_rows, 2, channels)
    inner = expanded[:, 0]
    gate_pre = expanded[:, 1]
    first_place = lax.axis_index("seq") * block_rows
    places = first_place + jnp.arange(block_rows, dtype=jnp.int32)
    split_place = lengths[0]
    begins = jnp.where(places >= split_place, split_place, 0)
    keeping = (places != begins).astype(jnp.float32)
    inherit = (begins < first_place).astype(jnp.float32)
    halo_rows = shifted_2(inner[block_rows - KW + 1 :], "seq", 1)
    extended = jnp.concatenate([halo_rows, inner], axis=0)
    valid_taps = [
        (places - (KW - 1 - tap_index) >= begins).astype(jnp.float32)[:, None]
        for tap_index in range(KW)
    ]
    conv_pre = jnp.broadcast_to(tap_bias[None, :], inner.shape)
    for tap_index in range(KW):
        conv_pre = (
            conv_pre
            + tap_weights[tap_index][None, :]
            * extended[tap_index : tap_index + block_rows]
            * valid_taps[tap_index]
        )
    activated = jax.nn.silu(conv_pre)
    act_low = activated.astype(jnp.bfloat16)
    feature_part = modal_product(act_low, modality, param_local, False)
    features = lax.psum(feature_part, "mod")
    step_low = features[:, :R].astype(jnp.bfloat16)
    input_mix = features[:, R : R + N]
    output_mix = features[:, R + N :]
    step_pre = modal_product(step_low, modality, step_local, False) + modal_table(
        bias_local, modality
    )
    step_size = jax.nn.softplus(step_pre)
    scan_rows = math.gcd(block_rows, SCAN_ROWS)
    scan_count = block_rows // scan_rows

    def blocked(values):
        return values.reshape((scan_count, scan_rows) + values.shape[1:])

    def block_mult(keep_block, step_block):
        return keep_block[:, None, None] * jnp.exp(step_block[:, None, :] * decay_rate[None])

    def local_step(state_now, inputs):
        keep_block, step_block, act_block, input_block, output_block = inputs
        multiplier = block_mult(keep_block, step_block)
        addition = (step_block * act_block)[:, None, :] * input_block[:, :, None]
        running = lax.associative_scan(pair_combine, (multiplier, addition), axis=0)
        states = running[0] * state_now[None] + running[1]
        return (
            states[-1],
            (jnp.sum(output_block[:, :, None] * states, axis=1), state_now, running[0], running[1]),
        )

    scan_inputs = (
        blocked(keeping),
        blocked(step_size),
        blocked(activated),
        blocked(input_mix),
        blocked(output_mix),
    )
    end_state, (local_out, local_starts, run_mult, run_add) = lax.scan(
        local_step, jnp.zeros((N, channels), jnp.float32), scan_inputs
    )
    device_decay = jnp.exp(decay_rate * jnp.sum(step_size, axis=0)[None, :]) * jnp.min(keeping)
    chained = carried_in(
        (device_decay, end_state),
        "seq",
        pair_combine,
        (jnp.ones_like(device_decay), jnp.zeros_like(end_state)),
    )
    state_in = chained[1]

    def fix_step(carried, inputs):
        total_step, alive = carried
        inherit_block, step_block, output_block = inputs
        start_factor = alive * jnp.exp(decay_rate * total_step[None, :])
        running_step = total_step[None, :] + jnp.cumsum(step_block, axis=0)
        reach = inherit_block[:, None, None] * jnp.exp(running_step[:, None, :] * decay_rate[None])
        extra = jnp.sum(output_block[:, :, None] * reach * state_in[None], axis=1)
        return ((running_step[-1], inherit_block[-1]), (extra, start_factor))

    reach_inputs = (blocked(inherit), blocked(step_size), blocked(output_mix))
    _, (extra_out, start_factors) = lax.scan(
        fix_step, (jnp.zeros((channels,), jnp.float32), jnp.float32(1.0)), reach_inputs
    )
    start_states = local_starts + start_factors * state_in[None]
    scan_out = (local_out + extra_out).reshape(block_rows, channels) + skip_local[
        None, :
    ] * activated
    gate_act = jax.nn.silu(gate_pre)
    gated = (scan_out * gate_act).astype(jnp.bfloat16)
    piece = gated
    piece_ids = modality
    branch = lax.psum_scatter(
        modal_product(piece, piece_ids, out_local, False), "mod", scatter_dimension=0, tiled=True
    )
    output = (token_vals + branch).astype(jnp.bfloat16)
    back_rows = cotangent.astype(jnp.float32)
    piece = lax.all_gather(cotangent, "mod", axis=0, tiled=True)
    piece_ids = modality
    product = modal_product(piece, piece_ids, out_local, True)
    grad_out = modal_outer(gated, piece, piece_ids)
    grad_scan = product * gate_act
    grad_gate = product * scan_out * silu_slope(gate_pre)
    grad_skip = jnp.sum(grad_scan * activated, axis=0)
    grad_act = grad_scan * skip_local[None, :]

    def lead_step(carried, inputs):
        total_step, lead_sum = carried
        inherit_block, step_block, output_block, grad_block = inputs
        running_step = total_step[None, :] + jnp.cumsum(step_block, axis=0)
        reach = inherit_block[:, None, None] * jnp.exp(running_step[:, None, :] * decay_rate[None])
        lead_sum = lead_sum + jnp.sum(
            reach * output_block[:, :, None] * grad_block[:, None, :], axis=0
        )
        return ((running_step[-1], lead_sum), None)

    (_, lead_local), _ = lax.scan(
        lead_step,
        (jnp.zeros((channels,), jnp.float32), jnp.zeros((N, channels), jnp.float32)),
        reach_inputs + (blocked(grad_scan),),
    )
    incoming = prefix(
        (device_decay, lead_local),
        "seq",
        back_combine,
        (jnp.ones_like(device_decay), jnp.zeros_like(lead_local)),
    )[1]

    def back_step(carried, inputs):
        after_block, rate_grad = carried
        (
            keep_block,
            step_block,
            act_block,
            input_block,
            output_block,
            grad_block,
            start_state,
            mult_block,
            add_block,
        ) = inputs
        multiplier = block_mult(keep_block, step_block)
        states = mult_block * start_state[None] + add_block
        previous = jnp.concatenate([start_state[None], states[:-1]], axis=0)
        pushed = output_block[:, :, None] * grad_block[:, None, :]
        pushed = pushed.at[-1].add(after_block)
        shifted = jnp.concatenate([multiplier[1:], jnp.ones_like(multiplier[:1])], axis=0)
        flipped = lax.associative_scan(pair_combine, (shifted[::-1], pushed[::-1]), axis=0)
        grad_state = flipped[1][::-1]
        mult_grad = grad_state * previous * multiplier
        state_input = jnp.sum(grad_state * input_block[:, :, None], axis=1)
        step_grad = jnp.sum(mult_grad * decay_rate[None], axis=1) + state_input * act_block
        rate_grad = rate_grad + jnp.sum(mult_grad * step_block[:, None, :], axis=0)
        input_grad = jnp.sum(grad_state * (step_block * act_block)[:, None, :], axis=2)
        act_grad = state_input * step_block
        output_grad = jnp.sum(states * grad_block[:, None, :], axis=2)
        return (
            (multiplier[0] * grad_state[0], rate_grad),
            (step_grad, input_grad, act_grad, output_grad),
        )

    back_inputs = scan_inputs[:5] + (blocked(grad_scan), start_states, run_mult, run_add)
    (_, rate_total), (step_grads, input_grads, act_grads, output_grads) = lax.scan(
        back_step, (incoming, jnp.zeros((N, channels), jnp.float32)), back_inputs, reverse=True
    )
    step_pre_grad = step_grads.reshape(block_rows, channels) * jax.nn.sigmoid(step_pre)
    grad_bias = modal_sums(step_pre_grad, modality)
    step_grad_low = step_pre_grad.astype(jnp.bfloat16)
    step_in_part = modal_product(step_grad_low, modality, step_local, True)
    grad_step = modal_outer(step_low, step_grad_low, modality)
    summed = lax.psum(
        (step_in_part, input_grads.reshape(block_rows, N), output_grads.reshape(block_rows, N)),
        "mod",
    )
    feature_grad = jnp.concatenate(summed, axis=1).astype(jnp.bfloat16)
    grad_param = modal_outer(act_low, feature_grad, modality)
    act_total = (
        grad_act
        + act_grads.reshape(block_rows, channels)
        + modal_product(feature_grad, modality, param_local, True)
    )
    conv_grad = act_total * silu_slope(conv_pre)
    tap_grads = []
    ext_grad = jnp.zeros((block_rows + KW - 1, channels), jnp.float32)
    for tap_index in range(KW):
        masked = conv_grad * valid_taps[tap_index]
        tap_grads.append(jnp.sum(masked * extended[tap_index : tap_index + block_rows], axis=0))
        ext_grad = ext_grad.at[tap_index : tap_index + block_rows].add(
            masked * tap_weights[tap_index][None, :]
        )
    grad_taps = jnp.stack(tap_grads)
    grad_tap_bias = jnp.sum(conv_grad, axis=0)
    spill = shifted_2(ext_grad[: KW - 1], "seq", -1)
    inner_grad = ext_grad[KW - 1 :].at[block_rows - KW + 1 :].add(spill)
    both_grad = (
        jnp.stack([inner_grad, grad_gate], axis=1)
        .astype(jnp.bfloat16)
        .reshape(block_rows, 2 * channels)
    )
    piece = both_grad
    piece_ids = modality
    normed_grad = lax.psum_scatter(
        modal_product(piece, piece_ids, in_flat, True), "mod", scatter_dimension=0, tiled=True
    )
    grad_in = modal_outer(folded[1], both_grad, modality)
    gain_part = jnp.sum(normed_grad * normal_rows, axis=0)
    hat_grad = normed_grad * gain_vals[None, :]
    token_grad = back_rows + inverse * (
        hat_grad - normal_rows * jnp.mean(hat_grad * normal_rows, axis=1, keepdims=True)
    )
    grad_gain = lax.psum(gain_part, ("seq", "mod"))
    grad_decay = rate_total * decay_rate
    weight_grads = (
        lax.psum_scatter(
            grad_in.reshape(MODS, model_width, 2, channels), "seq", scatter_dimension=1, tiled=True
        ),
        lax.psum_scatter(grad_param, "seq", scatter_dimension=1, tiled=True),
        lax.psum_scatter(grad_step, "seq", scatter_dimension=2, tiled=True),
        lax.psum_scatter(grad_out, "seq", scatter_dimension=2, tiled=True),
        lax.psum_scatter(grad_taps, "seq", scatter_dimension=1, tiled=True),
        lax.psum_scatter(grad_tap_bias, "seq", scatter_dimension=0, tiled=True),
        lax.psum_scatter(grad_decay, "seq", scatter_dimension=1, tiled=True),
        lax.psum_scatter(grad_skip, "seq", scatter_dimension=0, tiled=True),
        lax.psum_scatter(grad_bias, "seq", scatter_dimension=1, tiled=True),
    )
    return (
        output,
        token_grad,
        grad_gain,
        weight_grads[0],
        weight_grads[1],
        weight_grads[2],
        weight_grads[3],
        weight_grads[4],
        weight_grads[5],
        weight_grads[6],
        weight_grads[7],
        weight_grads[8],
    )


def pick(ids, parts):
    return jnp.where(ids == 0, parts[0], jnp.where(ids == 1, parts[1], parts[2]))


def silu(values):
    return values * jax.nn.sigmoid(values)


def softplus(values):
    small = jnp.exp(-jnp.abs(values))
    series = small * (
        1.0 + small * (-1 / 2 + small * (1 / 3 + small * (-1 / 4 + small * (1 / 5 - small / 6))))
    )
    return jnp.maximum(values, 0.0) + jnp.where(small < 0.05, series, jnp.log(1.0 + small))


def dot(left, right, left_dim=1, right_dim=0):
    return lax.dot_general(
        left, right, (((left_dim,), (right_dim,)), ((), ())), preferred_element_type=f32
    )


def row_places(first, rows):
    return first + lax.broadcasted_iota(jnp.int32, (rows, 1), 0)


def lane(values, at):
    return jnp.broadcast_to(values[:, at : at + 1], (SEGMENTS, LANES))


def tile(at):
    return pl.ds(at * LANES, LANES)


def whole(shape):
    return pl.BlockSpec(shape, lambda *_: (0,) * len(shape), pipeline_mode=pl.Buffered(1))


def cost(micros, flops=0):
    return pl.CostEstimate(flops=flops, bytes_accessed=int(micros * 3.69e6), transcendentals=0)


def modal_dot(values, ids, weight):
    part = values[0].shape[1]
    wide = sum(dot(v[...], weight[i * part : (i + 1) * part, :]) for i, v in enumerate(values))
    channels = wide.shape[1] // MODS
    return pick(ids, [wide[:, m * channels : (m + 1) * channels] for m in range(MODS)])


def put_masked(ref, rows, ids, values):
    channels = values.shape[1]
    for m in range(MODS):
        ref[rows, m * channels : (m + 1) * channels] = jnp.where(ids == m, values, 0.0).astype(
            ref.dtype
        )


def arrange(blocks, first, out):
    slab = out.shape[0] // blocks.shape[0]
    channels = blocks.shape[3]
    for at in range(blocks.shape[0]):
        for m in range(MODS):
            out[at * slab : (at + 1) * slab, m * channels : (m + 1) * channels] = blocks[
                at, first + m, 0:slab, :
            ]


def project_kernel(lengths, place, *refs):
    pieces, refs = refs[: 4 * COLUMNS], refs[4 * COLUMNS :]
    ids_ref, ids_rows, blocks, taps, bias, param_t = refs[:6]
    xs, refs = refs[6 : 6 + COLUMNS], refs[6 + COLUMNS :]
    w, w_gate, inner_ref, pre_ref, low_ref, feats, ext = refs
    step = pl.program_id(0)

    @pl.when(step == 0)
    def _():
        arrange(blocks, 0, w)
        arrange(blocks, MODS, w_gate)

    block_rows = pieces[0].shape[3]
    for which in (0, 1):

        @pl.when((place[0] == step % 2) == (which == 0))
        def _():
            for at in range(COLUMNS):
                own_line, other_line = pieces[4 * at + 2 * which : 4 * at + 2 * which + 2]
                here = place[1] if at % 2 == 0 else place[2]
                for near in (0, 1):
                    for line, value in ((here, own_line), (1 - here, other_line)):
                        block = line * 2 + near if at % 2 == 0 else near * 2 + line
                        row = pl.multiple_of(block * block_rows, block_rows)
                        xs[at][pl.ds(row, block_rows), :] = value[near, 0, 0]

    rows = xs[0].shape[0]
    channels = inner_ref.shape[1]
    ids = ids_ref[...]
    inner = modal_dot(xs, ids, w)
    inner_ref[...] = inner

    @pl.when(step == 0)
    def _():
        ext[0:8, :] = jnp.zeros((8, channels), f32)

    @pl.when(step > 0)
    def _():
        ext[0:8, :] = ext[rows : rows + 8, :]

    ext[8 : 8 + rows, :] = inner
    places = row_places(step * rows, rows)
    split = lengths[0]
    begins = jnp.where(places >= split, split, 0)
    pre = jnp.broadcast_to(bias[...], (rows, channels))
    for tap in range(KW):
        lag = KW - 1 - tap
        shifted = ext[8 - lag : 8 - lag + rows, :]
        pre = pre + taps[tap : tap + 1, :] * jnp.where(places - lag >= begins, shifted, 0.0)
    pre_ref[...] = pre
    low = silu(pre).astype(bf16)
    low_ref[...] = low
    across = feats.shape[2]
    ours = jnp.where(place[0] == step % 2, 1, 0)
    for j in range(across):
        block = low[j * block_rows : (j + 1) * block_rows]
        feats[ours, step // 2, j] = pick(
            ids_rows[pl.ds(step * across + j, 1), :],
            [dot(param_t[m], block, 1, 1) for m in range(MODS)],
        )


def project(lengths, place, pieces, ids, ids_rows, blocks, taps, bias, param_t):
    total = ids.shape[0]
    channels = taps.shape[1]
    chips, across = lax.axis_size("z"), lax.axis_size("mod")
    rows = total // (2 * chips)
    width = pieces[0].shape[4]
    by_rows = lambda i: (i, 0)
    feats = (2, chips, across, param_t.shape[1], rows // across)
    smem = pl.BlockSpec(memory_space=pltpu.SMEM)
    return pl.pallas_call(
        project_kernel,
        grid=(total // rows,),
        in_specs=[
            smem,
            smem,
            *[
                pl.BlockSpec((2, 1, 1) + piece.shape[3:], lambda i: (0, i // 2 % 2, i // 4, 0, 0))
                for piece in pieces
            ],
            pl.BlockSpec((rows, 1), by_rows),
            whole(ids_rows.shape),
            whole(blocks.shape),
            whole(taps.shape),
            whole(bias.shape),
            whole(param_t.shape),
        ],
        out_specs=[pl.BlockSpec((rows, width), by_rows)] * COLUMNS
        + [whole((COLUMNS * width, MODS * channels))] * 2
        + [pl.BlockSpec((rows, channels), by_rows)] * 3
        + [whole(feats)],
        out_shape=[jax.ShapeDtypeStruct((total, width), bf16)] * COLUMNS
        + [jax.ShapeDtypeStruct((COLUMNS * width, MODS * channels), bf16)] * 2
        + [jax.ShapeDtypeStruct((total, channels), f32)] * 2
        + [jax.ShapeDtypeStruct((total, channels), bf16)]
        + [jax.ShapeDtypeStruct(feats, f32)],
        scratch_shapes=[pltpu.VMEM((rows + 8, channels), f32)],
        compiler_params=pltpu.CompilerParams(vmem_limit_bytes=VMEM_BYTES),
        cost_estimate=cost(1),
        name="project",
    )(lengths, place, *pieces, ids, ids_rows, blocks, taps, bias, param_t)


def modal_kernel(*refs):
    *xs, ids_ref, w, out = refs
    out[...] = modal_dot(xs, ids_ref[...], w)


def modal_rows(values, ids, weight):
    total = values[0].shape[0]
    channels = weight.shape[1] // MODS
    rows = math.gcd(total, 512)
    by_rows = lambda i: (i, 0)
    return pl.pallas_call(
        modal_kernel,
        grid=(total // rows,),
        in_specs=[
            *[pl.BlockSpec((rows, part.shape[1]), by_rows) for part in values],
            pl.BlockSpec((rows, 1), by_rows),
            whole(weight.shape),
        ],
        out_specs=pl.BlockSpec((rows, channels), by_rows),
        out_shape=jax.ShapeDtypeStruct((total, channels), f32),
        compiler_params=pltpu.CompilerParams(vmem_limit_bytes=VMEM_BYTES),
        cost_estimate=cost(1),
        name="modal_rows",
    )(*values, ids, weight)


def side_kernel(*refs):
    out, columns = refs[-1], refs[0].shape[1]
    for at, part in enumerate(refs[:-1]):
        out[:, at * columns : (at + 1) * columns] = part[...]


def side_by_side(*parts):
    rows, columns = parts[0].shape
    step = math.gcd(rows, 512)
    by_rows = lambda i: (i, 0)
    return pl.pallas_call(
        side_kernel,
        grid=(rows // step,),
        in_specs=[pl.BlockSpec((step, columns), by_rows)] * len(parts),
        out_specs=pl.BlockSpec((step, columns * len(parts)), by_rows),
        out_shape=jax.ShapeDtypeStruct((rows, columns * len(parts)), parts[0].dtype),
        cost_estimate=cost(1),
        name="side_by_side",
    )(*parts)


def gates_kernel(
    cot, ids_ref, blocks, pre, out, w_out, grad_scan, gate_wide, gated_wide, gate_low, gated_low
):
    @pl.when(pl.program_id(0) == 0)
    def _():
        arrange(blocks, 0, w_out)

    ids = ids_ref[...]
    here = pre[...]
    grad = modal_dot([cot], ids, w_out)
    sig = jax.nn.sigmoid(here)
    scanned = out[...]
    grad_scan[...] = grad * (here * sig)
    gate_grad = grad * scanned * (sig * (1.0 + here * (1.0 - sig)))
    gated = scanned * (here * sig)
    gate_low[...] = gate_grad.astype(bf16)
    gated_low[...] = gated.astype(bf16)
    put_masked(gate_wide, slice(None), ids, gate_grad)
    put_masked(gated_wide, slice(None), ids, gated)


def gates(cotangents, ids, blocks, pre, out):
    total, channels = out.shape
    width = cotangents.shape[1]
    rows = total // size_of(SEQ)
    by_rows = lambda i: (i, 0)
    block = pl.BlockSpec((rows, channels), by_rows)
    wide = pl.BlockSpec((rows, MODS * channels), by_rows)
    return pl.pallas_call(
        gates_kernel,
        grid=(total // rows,),
        in_specs=[
            pl.BlockSpec((rows, width), by_rows),
            pl.BlockSpec((rows, 1), by_rows),
            whole(blocks.shape),
            block,
            block,
        ],
        out_specs=[whole((width, MODS * channels)), block, wide, wide, block, block],
        out_shape=[
            jax.ShapeDtypeStruct((width, MODS * channels), bf16),
            jax.ShapeDtypeStruct((total, channels), f32),
            jax.ShapeDtypeStruct((total, MODS * channels), bf16),
            jax.ShapeDtypeStruct((total, MODS * channels), bf16),
            jax.ShapeDtypeStruct((total, channels), bf16),
            jax.ShapeDtypeStruct((total, channels), bf16),
        ],
        compiler_params=pltpu.CompilerParams(vmem_limit_bytes=VMEM_BYTES),
        cost_estimate=cost(1),
        name="gates",
    )(cotangents, ids, blocks, pre, out)


def scan_kernel(
    lengths,
    ids_ref,
    feats,
    pre,
    step_w,
    step_b,
    rate,
    skip,
    states,
    enter,
    step_pre,
    mix,
    scan_out,
    s_turn,
    u_turn,
    mix_turn,
    y_turn,
    held,
):
    chunk = pl.program_id(0)
    total = pre.shape[0]
    length = total // SEGMENTS
    steps = states.shape[0] // SEGMENTS
    split = lengths[0]
    rows_on = UNROLL * SEGMENTS

    def rated(n):
        return jnp.broadcast_to(rate[n : n + 1, :], (SEGMENTS, LANES))

    def cut(values):
        return [values[j * SEGMENTS : (j + 1) * SEGMENTS] for j in range(UNROLL)]

    @pl.when(chunk == 0)
    def _():
        for seg in range(SEGMENTS):
            rows = pl.ds(seg * length, length)
            turned = pl.ds(seg, length, stride=SEGMENTS)
            ids = ids_ref[rows, :]
            block_rows = length // feats.shape[2]
            for j in range(feats.shape[2]):
                block = pl.ds(seg * length + j * block_rows, block_rows)
                block_ids = ids_ref[block, :]
                low = feats[seg % 2, seg // 2, j, 0:R, :]
                step_pre[block, :] = pick(
                    block_ids, [dot(low, step_w[m], 0, 0) for m in range(MODS)]
                ) + pick(block_ids, [step_b[m : m + 1, :] for m in range(MODS)])
                mixed = feats[seg % 2, seg // 2, j, R : R + 2 * N, :].astype(f32)
                mixed = mixed + feats[seg % 2, seg // 2, j, R + 2 * N :, :].astype(f32)
                blank = jnp.zeros((LANES - 2 * N, block_rows), f32)
                mix[block, :] = jnp.transpose(jnp.concatenate([mixed, blank], axis=0))
            step = softplus(step_pre[rows, :])
            places = row_places(seg * length, length)
            start = (places == 0) | (places == split)
            s_turn[turned, :] = jnp.where(start, FAR, step)
            u_turn[turned, :] = step * silu(pre[rows, :])
            mix_turn[turned, :] = mix[rows, :]

        def ahead(i, spent):
            at = pl.ds(pl.multiple_of(i * rows_on, rows_on), rows_on)
            s, u, bc = [cut(v[at, :]) for v in (s_turn, u_turn, mix_turn)]
            for n in range(N):
                rate_n, hidden = rated(n), held[:, tile(n)]
                for j in range(UNROLL):
                    hidden = jnp.exp2(s[j] * rate_n) * hidden + u[j] * lane(bc[j], n)
                held[:, tile(n)] = hidden
            return spent + sum(s)

        zero = jnp.zeros((SEGMENTS, LANES), f32)
        held[...] = jnp.zeros(held.shape, f32)
        spent = lax.fori_loop(0, length // UNROLL, ahead, zero)
        first = lax.broadcasted_iota(jnp.int32, (SEGMENTS, LANES), 0) == 0
        for n in range(N):
            through = jnp.exp2(spent * rated(n))
            end = held[:, tile(n)]
            inside = zero
            for _ in range(SEGMENTS - 1):
                inside = jnp.where(first, 0.0, pltpu.roll(end + through * inside, 1, 0))
            held[:, tile(n)] = inside
            enter[:, tile(n)] = inside

    base = chunk * steps

    def steps_on(i, carried):
        at = pl.ds(pl.multiple_of((base + i * UNROLL) * SEGMENTS, rows_on), rows_on)
        s, u, bc = [cut(v[at, :]) for v in (s_turn, u_turn, mix_turn)]
        result = [0.0] * UNROLL
        for n in range(N):
            rate_n, hidden = rated(n), held[:, tile(n)]
            for j in range(UNROLL):
                hidden = jnp.exp2(s[j] * rate_n) * hidden + u[j] * lane(bc[j], n)
                out = pl.ds(pl.multiple_of((i * UNROLL + j) * SEGMENTS, SEGMENTS), SEGMENTS)
                states[out, tile(n)] = hidden
                result[j] = result[j] + hidden * lane(bc[j], N + n)
            held[:, tile(n)] = hidden
        y_turn[at, :] = jnp.concatenate(result, axis=0)
        return carried

    lax.fori_loop(0, steps // UNROLL, steps_on, 0)

    @pl.when(chunk == pl.num_programs(0) - 1)
    def _():
        for seg in range(SEGMENTS):
            rows = pl.ds(seg * length, length)
            turned = pl.ds(seg, length, stride=SEGMENTS)
            scan_out[rows, :] = y_turn[turned, :] + skip[...] * silu(pre[rows, :])


def scan(lengths, ids, feats, pre, step_w, step_b, rate, skip):
    total, channels = pre.shape
    steps = math.gcd(total // SEGMENTS, CHUNK)
    rows = steps * SEGMENTS
    turn = pltpu.VMEM((total, channels), f32)
    ins = (ids, feats, pre, step_w, step_b, rate, skip)
    return pl.pallas_call(
        scan_kernel,
        grid=(total // rows,),
        in_specs=[pl.BlockSpec(memory_space=pltpu.SMEM)] + [whole(a.shape) for a in ins],
        out_specs=[
            pl.BlockSpec((rows, N * channels), lambda i: (i, 0)),
            whole((SEGMENTS, N * channels)),
            whole((total, channels)),
            whole((total, channels)),
            whole((total, channels)),
        ],
        out_shape=[
            jax.ShapeDtypeStruct((total, N * channels), f32),
            jax.ShapeDtypeStruct((SEGMENTS, N * channels), f32),
            jax.ShapeDtypeStruct((total, channels), f32),
            jax.ShapeDtypeStruct((total, channels), f32),
            jax.ShapeDtypeStruct((total, channels), f32),
        ],
        scratch_shapes=[turn, turn, turn, turn, pltpu.VMEM((SEGMENTS, N * channels), f32)],
        compiler_params=pltpu.CompilerParams(vmem_limit_bytes=VMEM_BYTES),
        cost_estimate=cost(1),
        name="scan",
    )(lengths, *ins)


def back_kernel(
    lengths,
    core,
    ids_ref,
    ids_rows,
    mix,
    pre,
    step_pre,
    grad,
    states,
    before,
    enter,
    step_w,
    rate,
    skip,
    gather_in,
    gather_out,
    act_part,
    step_grad_low,
    feat_part,
    sums,
    rate_out,
    s_turn,
    u_turn,
    g_turn,
    mix_turn,
    step_turn,
    in_turn,
    mix_grad,
    in_terms,
    out_terms,
    held,
    rate_sum,
):
    turn_at = pl.program_id(0)
    chunks = pl.num_programs(0)
    chunk = chunks - 1 - turn_at
    total = pre.shape[0]
    length = total // SEGMENTS
    steps = states.shape[0] // SEGMENTS
    split = lengths[0]
    zero = jnp.zeros((SEGMENTS, LANES), f32)

    def rated(n):
        return jnp.broadcast_to(rate[n : n + 1, :], (SEGMENTS, LANES))

    def cut(values):
        count = values.shape[0] // SEGMENTS
        return [values[j * SEGMENTS : (j + 1) * SEGMENTS] for j in range(count)]

    @pl.when(turn_at == 0)
    def _():
        for seg in range(SEGMENTS):
            rows = pl.ds(seg * length, length)
            turned = pl.ds(seg, length, stride=SEGMENTS)
            step = softplus(step_pre[rows, :])
            places = row_places(seg * length, length)
            start = (places == 0) | (places == split)
            s_turn[turned, :] = jnp.where(start, FAR, step)
            u_turn[turned, :] = step * silu(pre[rows, :])
            mix_turn[turned, :] = mix[rows, :]
            g_turn[turned, :] = grad[rows, :]

        def ahead(i, spent):
            rows_on = UNROLL * SEGMENTS
            first_row = total - (i + 1) * rows_on
            at = pl.ds(pl.multiple_of(first_row, rows_on), rows_on)
            s, g, bc = [cut(v[at, :]) for v in (s_turn, g_turn, mix_turn)]
            for n in range(N):
                rate_n, pulled = rated(n), held[:, tile(n)]
                for j in reversed(range(UNROLL)):
                    pulled = jnp.exp2(s[j] * rate_n) * (pulled + g[j] * lane(bc[j], N + n))
                held[:, tile(n)] = pulled
            return spent + sum(s)

        held[...] = jnp.zeros(held.shape, f32)
        spent = lax.fori_loop(0, length // UNROLL, ahead, zero)
        last = lax.broadcasted_iota(jnp.int32, (SEGMENTS, LANES), 0) == SEGMENTS - 1
        for n in range(N):
            through = jnp.exp2(spent * rated(n))
            end = held[:, tile(n)]
            inside = zero
            for _ in range(SEGMENTS - 1):
                inside = jnp.where(
                    last, 0.0, pltpu.roll(end + through * inside, SEGMENTS - 1, 0)
                )
            held[:, tile(n)] = inside
            rate_sum[:, tile(n)] = zero

    base = chunk * steps

    def steps_back(low_step, earlier):
        rows_on = BACK * SEGMENTS
        at = pl.ds(pl.multiple_of((base + low_step) * SEGMENTS, rows_on), rows_on)
        here = pl.ds(pl.multiple_of(low_step * SEGMENTS, rows_on), rows_on)
        s, u, g, bc = [cut(v[at, :]) for v in (s_turn, u_turn, g_turn, mix_turn)]
        step_sum, in_sum = [0.0] * BACK, [0.0] * BACK
        for n in range(N):
            rate_n, pull, rate_acc = rated(n), held[:, tile(n)], rate_sum[:, tile(n)]
            state = [earlier(n)] + cut(states[here, tile(n)])
            parts_in, parts_out = [None] * BACK, [None] * BACK
            for j in reversed(range(BACK)):
                grad_state = g[j] * lane(bc[j], N + n) + pull
                pull = jnp.exp2(s[j] * rate_n) * grad_state
                mult = pull * state[j]
                step_sum[j] = step_sum[j] + mult * rate_n
                rate_acc = rate_acc + mult * s[j]
                in_sum[j] = in_sum[j] + grad_state * lane(bc[j], n)
                parts_in[j] = grad_state * u[j]
                parts_out[j] = state[j + 1] * g[j]
            in_terms[here, tile(n)] = jnp.concatenate(parts_in, axis=0).astype(bf16)
            out_terms[here, tile(n)] = jnp.concatenate(parts_out, axis=0).astype(bf16)
            held[:, tile(n)] = pull
            rate_sum[:, tile(n)] = rate_acc
        step_turn[at, :] = jnp.concatenate(step_sum, axis=0)
        in_turn[at, :] = jnp.concatenate(in_sum, axis=0)

    def inside(i, carried):
        low_step = steps - BACK * (i + 1)
        prior = pl.ds(pl.multiple_of((low_step - 1) * SEGMENTS, SEGMENTS), SEGMENTS)
        steps_back(low_step, lambda n: states[prior, tile(n)])
        return carried

    def entering(n):
        return jnp.where(chunk == 0, enter[:, tile(n)], before[:, tile(n)])

    lax.fori_loop(0, steps // BACK - 1, inside, 0)
    steps_back(0, entering)
    mix_grad[pl.ds(pl.multiple_of(base * SEGMENTS, SEGMENTS), steps * SEGMENTS), :] = dot(
        in_terms[...], gather_in[...]
    ) + dot(out_terms[...], gather_out[...])

    @pl.when(turn_at == chunks - 1)
    def _():
        sums[...] = jnp.zeros(sums.shape, f32)
        for seg in range(SEGMENTS):
            rows = pl.ds(seg * length, length)
            turned = pl.ds(seg, length, stride=SEGMENTS)
            ids = ids_ref[rows, :]
            act = silu(pre[rows, :])
            step_in = step_pre[rows, :]
            state_in = in_turn[turned, :]
            grad_here = grad[rows, :]
            step_grad = step_turn[turned, :] * math.log(2.0) + state_in * act
            pre_grad = step_grad * jax.nn.sigmoid(step_in)
            low = pre_grad.astype(bf16)
            step_grad_low[rows, :] = low
            act_part[rows, :] = grad_here * skip[...] + state_in * softplus(step_in)
            block_rows = feat_part.shape[4]
            ours = jnp.where(core[0] == seg % 2, 1, 0)
            for j in range(length // block_rows):
                block = seg * (length // block_rows) + j
                block_low = low[j * block_rows : (j + 1) * block_rows]
                feat_part[ours, seg // 2, j, 0:R, :] = pick(
                    ids_rows[block : block + 1, :],
                    [dot(step_w[m], block_low, 1, 1) for m in range(MODS)],
                )
                part = pl.ds(j * block_rows * SEGMENTS + seg, block_rows, stride=SEGMENTS)
                turned_mix = jnp.transpose(mix_grad[part, :])
                feat_part[ours, seg // 2, j, R : R + 2 * N, :] = turned_mix[: 2 * N]
            for m in range(MODS):
                sums[m : m + 1, :] += jnp.sum(
                    jnp.where(ids == m, pre_grad, 0.0), axis=0, keepdims=True
                )
            sums[MODS : MODS + 1, :] += jnp.sum(grad_here * act, axis=0, keepdims=True)
        for n in range(N):
            rate_out[n : n + 1, :] = jnp.sum(rate_sum[:, tile(n)], axis=0, keepdims=True)


def scan_back(
    lengths, core, ids, ids_rows, mix, pre, step_pre, grad, states, enter, step_w, rate, skip
):
    total, channels = pre.shape
    steps = math.gcd(total // SEGMENTS, CHUNK)
    rows = steps * SEGMENTS
    chunks = total // rows
    turn = pltpu.VMEM((total, channels), f32)
    state_lane = jnp.arange(N * channels, dtype=jnp.int32)[:, None] // channels
    column = jnp.arange(LANES, dtype=jnp.int32)[None, :]
    gather_in = (state_lane == column).astype(bf16)
    gather_out = (state_lane + N == column).astype(bf16)
    across = lax.axis_size("mod")
    feats = (2, lax.axis_size("z"), across, R + 2 * N, ids_rows.shape[1])
    first = (ids, ids_rows, mix, pre, step_pre, grad)
    second = (enter, step_w, rate, skip, gather_in, gather_out)
    return pl.pallas_call(
        back_kernel,
        grid=(chunks,),
        in_specs=[pl.BlockSpec(memory_space=pltpu.SMEM)] * 2
        + [whole(a.shape) for a in first]
        + [
            pl.BlockSpec((rows, N * channels), lambda i: (chunks - 1 - i, 0)),
            pl.BlockSpec(
                (SEGMENTS, N * channels),
                lambda i: (jnp.maximum((chunks - 1 - i) * steps - 1, 0), 0),
            ),
        ]
        + [whole(a.shape) for a in second],
        out_specs=[
            whole((total, channels)),
            whole((total, channels)),
            whole(feats),
            whole((SEGMENTS, channels)),
            whole((N, channels)),
        ],
        out_shape=[
            jax.ShapeDtypeStruct((total, channels), f32),
            jax.ShapeDtypeStruct((total, channels), bf16),
            jax.ShapeDtypeStruct(feats, f32),
            jax.ShapeDtypeStruct((SEGMENTS, channels), f32),
            jax.ShapeDtypeStruct((N, channels), f32),
        ],
        scratch_shapes=[turn] * 7
        + [pltpu.VMEM((rows, N * channels), bf16)] * 2
        + [pltpu.VMEM((SEGMENTS, N * channels), f32)] * 2,
        compiler_params=pltpu.CompilerParams(vmem_limit_bytes=VMEM_BYTES),
        cost_estimate=cost(1),
        name="scan_back",
    )(lengths, core, *first, states, states, *second)


def conv_back_kernel(
    seqs,
    lengths,
    ids_ref,
    feat_grad,
    act_part,
    pre,
    inner,
    taps,
    param_t,
    inner_wide,
    inner_low,
    sums,
    ext,
):
    total, channels = pre.shape
    rows = total // seqs
    split = lengths[0]
    ext[total : total + 8, :] = jnp.zeros((8, channels), f32)
    sums[...] = jnp.zeros(sums.shape, f32)

    def through_silu(i, carried):
        at = pl.ds(pl.multiple_of(i * rows, rows), rows)
        for j in range(feat_grad.shape[2]):
            block_rows = feat_grad.shape[4]
            block = pl.ds(pl.multiple_of(i * rows + j * block_rows, block_rows), block_rows)
            low = feat_grad[i % 2, i // 2, j]
            ext[block, :] = pick(
                ids_ref[block, :], [dot(low, param_t[m], 0, 0) for m in range(MODS)]
            )
        act_grad = act_part[at, :] + ext[at, :]
        here = pre[at, :]
        sig = jax.nn.sigmoid(here)
        conv_grad = act_grad * (sig * (1.0 + here * (1.0 - sig)))
        ext[at, :] = conv_grad
        sums[KW : KW + 1, :] += jnp.sum(conv_grad, axis=0, keepdims=True)
        return carried

    lax.fori_loop(0, total // rows, through_silu, 0)

    for block in range(total // rows):
        first = block * rows
        at = pl.ds(first, rows)
        places = row_places(first, rows)
        here = inner[at, :]
        grad = jnp.zeros((rows, channels), f32)
        for tap in range(KW):
            lag = KW - 1 - tap
            kept = (places >= split) | (places + lag < split)
            later = jnp.where(kept, ext[pl.ds(first + lag, rows), :], 0.0)
            grad = grad + taps[tap : tap + 1, :] * later
            sums[tap : tap + 1, :] += jnp.sum(later * here, axis=0, keepdims=True)
        put_masked(inner_wide, at, ids_ref[at, :], grad)
        inner_low[at, :] = grad.astype(bf16)


def conv_back(seqs, lengths, ids, feat_grad, act_part, pre, inner, taps, param_t):
    total, channels = pre.shape
    ins = (ids, feat_grad, act_part, pre, inner, taps, param_t)
    vmem = pl.BlockSpec(memory_space=pltpu.VMEM)
    return pl.pallas_call(
        functools.partial(conv_back_kernel, seqs),
        in_specs=[pl.BlockSpec(memory_space=pltpu.SMEM)] + [vmem] * len(ins),
        out_specs=[vmem, vmem, vmem],
        out_shape=[
            jax.ShapeDtypeStruct((total, MODS * channels), bf16),
            jax.ShapeDtypeStruct((total, channels), bf16),
            jax.ShapeDtypeStruct((8, channels), f32),
        ],
        scratch_shapes=[pltpu.VMEM((total + 8, channels), f32)],
        compiler_params=pltpu.CompilerParams(vmem_limit_bytes=VMEM_BYTES),
        cost_estimate=cost(1),
        name="conv_back",
    )(lengths, *ins)


def flip(axis, bit):
    size = lax.axis_size(axis)
    return lambda value: lax.ppermute(value, axis, [(i, i ^ bit) for i in range(size)])


def taken(values, at, dim):
    return lax.dynamic_index_in_dim(values, at, dim, keepdims=False)


SEQ = ("z", "core")
SAME_CORE = ("z", "mod")


def size_of(axes):
    return math.prod(lax.axis_size(axis) for axis in axes)


def share(values, axes):
    size = size_of(axes)
    return lax.all_to_all(jnp.broadcast_to(values, (size,) + values.shape), axes, 0, 0)


def exchange(blocks, axes):
    return lax.all_to_all(blocks, axes, 0, 0)


def held_back(value, until):
    return lax.optimization_barrier((value, tuple(until)))[0] if until else value


def flip(axis, bit):
    size = lax.axis_size(axis)
    return lambda value: lax.ppermute(value, axis, [(i, i ^ bit) for i in range(size)])


def taken(values, at, dim):
    return lax.dynamic_index_in_dim(values, at, dim, keepdims=False)


def two(bit, mine, got):
    return jnp.where(bit == 0, jnp.stack([mine, got]), jnp.stack([got, mine]))


Z_HIGH, Z_LOW, CORE = ("z", 2), ("z", 1), ("core", 1)
Y, X = ("mod", 2), ("mod", 1)


def place_bit(place):
    axis, bit = place
    return lax.axis_index(axis) // bit % 2


def summed_features(feats, kind=f32):
    feats = (feats[1] + flip(*CORE)(feats[0])).astype(kind)
    feats = feats.reshape((-1,) + feats.shape[2:])
    return jnp.sum(exchange(feats, SAME_CORE).astype(f32), axis=0), feats


def shared_features(block, until=()):
    mine = share(block, SAME_CORE)
    every = two(place_bit(CORE), mine, flip(*CORE)(held_back(mine, until)))
    return every.reshape((2, lax.axis_size("z"), lax.axis_size("mod")) + block.shape)


def core_rows(values, which):
    blocks = values.reshape(lax.axis_size("z"), 2, -1, values.shape[1])
    return taken(blocks, which, 1).reshape(-1, values.shape[1])


def both_cores(low, ids_ours):
    core = place_bit(CORE)
    got = flip(*CORE)(core_rows(low, 1 - core))
    return [masked(core_rows(low, core), ids_ours), masked(got, ids_ours)]


def gathered_columns(shard, between):
    width = shard.shape[1] // COLUMNS
    lines, far = [], []
    for at in range(COLUMNS):
        part = shard[:, at * width : (at + 1) * width]
        far.append(flip(*Z_HIGH)(held_back(part, far[at - 1 : at] if at else ())))
        line = two(place_bit(Z_HIGH), part, far[at])
        given = held_back(line, lines[at - 1 : at] if at else ())
        lines.append(two(place_bit(Z_LOW), line, flip(*Z_LOW)(given)))
    until = between(lines[-1])
    pieces, arrived, halfway = [], [], []
    for at, line in enumerate(lines):
        near, next_ = (X, Y) if at % 2 == 0 else (Y, X)
        halfway.append(flip(*near)(held_back(line, halfway[at - 2 : at - 1] if at > 1 else ())))
        pair = two(place_bit(near), line, halfway[at])
        got = flip(*next_)(held_back(pair, until if at > 1 else ()))
        arrived.append(got)
        pieces += [pair, got, flip(*CORE)(pair), flip(*CORE)(got)]
    return pieces, arrived


def row_parts(left, right, count):
    width = right.shape[0] // count
    return [
        dot(left, right[at * width : (at + 1) * width], 1, 1)
        .astype(bf16)
        .reshape(2, 2, 2, 2, -1, width)
        for at in range(count)
    ]


class SummedRows:
    def __init__(self, parts):
        self.dims = [["zh", "zl", "y", "x"] for _ in parts]
        self.parts = [[part] for part in parts]

    def give(self, at, name, place):
        dim = self.dims[at].index(name)
        bit = place_bit(place)
        away = sum(taken(p, 1 - bit, dim).astype(f32) for p in self.parts[at]).astype(bf16)
        self.parts[at] = [taken(p, bit, dim) for p in self.parts[at]]
        self.dims[at].remove(name)
        return away

    def stage(self, names):
        places = {"x": X, "y": Y, "zl": Z_LOW, "zh": Z_HIGH}
        sent = []
        for at in range(len(self.parts)):
            name = names[at % 2]
            away = self.give(at, name, places[name])
            sent.append(away)
            self.parts[at].append(flip(*places[name])(away))
        return sent

    def merge(self):
        pairs = list(zip(self.parts[::2], self.parts[1::2]))
        self.parts = [
            [jnp.concatenate(both, axis=-1) for both in zip(even, odd)] for even, odd in pairs
        ]
        self.dims = self.dims[::2]

    def arrived(self):
        return [parts[-1] for parts in self.parts]

    def hold(self, until):
        for parts in self.parts:
            parts[-1] = held_back(parts[-1], until)

    def result(self):
        return jnp.concatenate([sum(p.astype(f32) for p in parts) for parts in self.parts], axis=1)


def masked(values, ids):
    return jnp.concatenate(
        [jnp.where(ids == m, values, jnp.zeros_like(values)) for m in range(MODS)], axis=1
    )


def channel_layout(
    tokens,
    modality,
    lengths,
    norm_gain,
    input_weight,
    param_weight,
    step_weight,
    step_bias,
    output_weight,
    conv_weight,
    conv_bias,
    decay_log,
    skip_gain,
    cotangent,
):
    seqs = size_of(SEQ)
    channels = conv_weight.shape[1]
    width = tokens.shape[1]
    features = param_weight.shape[2]
    slab = input_weight.shape[1]

    token_vals = tokens.astype(f32)
    inverse = lax.rsqrt(jnp.mean(token_vals * token_vals, axis=1, keepdims=True) + EPSILON)
    normal_rows = token_vals * inverse
    gain_vals = norm_gain.astype(f32)

    send_in = input_weight.reshape(MODS, slab, 2, seqs, channels)
    send_in = send_in.transpose(3, 2, 0, 1, 4).reshape(seqs, 2 * MODS, slab, channels)
    id_rows = 16
    send_ids = jnp.pad(modality.astype(bf16), (0, id_rows * channels - modality.shape[0]))
    send_ids = jnp.broadcast_to(
        send_ids.reshape(id_rows, channels), (seqs, 2 * MODS, id_rows, channels)
    )
    send_in = jnp.concatenate([send_in, send_ids], axis=2)
    made = []

    def send(line):
        made.append(exchange(held_back(send_in, [line]), SEQ))
        return made

    pieces, arrived = gathered_columns((normal_rows * gain_vals[None, :]).astype(bf16), send)
    inner_blocks = made[0]
    ids = inner_blocks[:, 0, slab:].reshape(seqs, -1)[:, : modality.shape[0]].astype(jnp.int32)
    ids_rows = ids.reshape(-1, tokens.shape[0])
    ids = ids.reshape(-1, 1)
    send_out = output_weight.reshape(MODS, seqs, channels, slab).transpose(1, 0, 3, 2)
    param_t = param_weight.transpose(0, 2, 1)
    core = place_bit(CORE)
    place = jnp.stack([place_bit(at) for at in (CORE, Y, X)]).astype(jnp.int32)
    taps = conv_weight.astype(f32)
    skip = skip_gain.astype(f32)[None, :]
    decay_rate = -jnp.exp(decay_log.astype(f32))
    rate = decay_rate * math.log2(math.e)

    *normed, own_inner, own_gate, inner, conv_pre, act_low, feats = project(
        lengths,
        place,
        pieces,
        ids,
        ids_rows,
        inner_blocks,
        taps,
        conv_bias.astype(f32)[None, :],
        param_t,
    )
    cotangents = lax.all_gather(
        held_back(cotangent, [inner]), SEQ + ("mod",), axis=0, tiled=True
    )
    feats, sent = summed_features(feats)
    gate_pre = modal_rows(normed, held_back(ids, [sent]), own_gate)
    feats = held_back(feats, [gate_pre])
    mix_high = feats[R:].astype(bf16)
    mix_rest = (feats[R:] - mix_high.astype(f32)).astype(bf16)
    feats = jnp.concatenate([feats[:R].astype(bf16), mix_high, mix_rest], axis=0)
    feats = shared_features(feats)

    out_blocks = exchange(held_back(send_out, [feats]), SEQ)
    states, enter, step_pre, mix, scan_out = scan(
        lengths, ids, feats, conv_pre, step_weight, step_bias.astype(f32), rate, skip
    )
    out_blocks, scan_out = lax.optimization_barrier((out_blocks, scan_out))
    own_out, grad_scan, gate_wide, gated_wide, gate_rows, gated_rows = gates(
        cotangents, ids, out_blocks, gate_pre, scan_out
    )

    def token_sums(wide, weight):
        lows, gains = [], []
        for at, part in enumerate(normed):
            rows = part.shape[1]
            grad = dot(part, wide, 0, 0)
            lows.append(grad.astype(bf16))
            gains.append(jnp.sum(grad * weight[at * rows : (at + 1) * rows].astype(f32), axis=1))
        return jnp.concatenate(lows, axis=0), jnp.concatenate(gains, axis=0)

    def by_holder(low):
        return low.reshape(seqs, slab, MODS * channels)

    ids_ours = core_rows(ids, core)
    gated_both = both_cores(gated_rows, ids_ours)
    other_out = flip(*CORE)(own_out)
    gate_low, gate_gain = token_sums(gate_wide, own_gate)
    gated_both, other_out, gated_wide = lax.optimization_barrier(
        (gated_both, other_out, gated_wide)
    )
    out_low = dot(cotangents, gated_wide, 0, 0).astype(bf16)
    gated_both = jnp.concatenate(gated_both, axis=1)
    branch = SummedRows(row_parts(gated_both, side_by_side(own_out, other_out), 2))
    branch_sent = branch.stage(("x", "y"))
    more_low = jnp.concatenate([by_holder(gate_low), by_holder(out_low)], axis=2)
    grad_scan = held_back(grad_scan, branch_sent + [more_low])
    more_low = exchange(more_low, SEQ).reshape(seqs, slab, 2, MODS, channels)
    grad_gate = more_low[:, :, 0].transpose(2, 1, 0, 3)
    grad_out = more_low[:, :, 1].transpose(2, 0, 3, 1)
    grad_out = grad_out.reshape(MODS, seqs * channels, slab).astype(f32)

    act_part, step_grad_low, feat_grad, sums, rate_sum = scan_back(
        lengths,
        place,
        ids,
        ids_rows,
        mix,
        conv_pre,
        step_pre,
        grad_scan,
        states,
        enter,
        step_weight,
        rate,
        skip,
    )

    feat_grad = held_back(feat_grad, [more_low] + branch.arrived())
    gate_rows = held_back(gate_rows, [feat_grad])
    gate_both = both_cores(gate_rows, ids_ours)
    feat_grad, sent = summed_features(feat_grad, bf16)
    own_inner, own_gate = held_back((own_inner, own_gate), [sent])
    pair_in = side_by_side(own_inner, flip(*CORE)(own_inner), own_gate, flip(*CORE)(own_gate))
    feat_grad = held_back(feat_grad.astype(bf16), branch.stage(("y", "x")) + [pair_in])
    feat_grad = shared_features(feat_grad)
    branch.hold([feat_grad])
    branch.merge()

    inner_wide, inner_rows, tap_sums = conv_back(
        seqs,
        lengths,
        ids,
        feat_grad,
        act_part,
        conv_pre,
        inner,
        taps,
        param_t,
    )
    both_wide = jnp.concatenate(both_cores(inner_rows, ids_ours) + gate_both, axis=1)
    products = row_parts(both_wide, pair_in, COLUMNS)
    normed_sums = SummedRows(products)
    sent = normed_sums.stage(("x", "y"))
    branch.hold(sent)
    branch.stage(("zl", "zl"))
    inner_low, inner_gain = token_sums(held_back(inner_wide, sent), own_inner)
    inner_low = exchange(by_holder(inner_low), SEQ).reshape(seqs, slab, MODS, channels)
    branch.stage(("zh", "zh"))
    sent = normed_sums.stage(("y", "x"))
    output = (token_vals + branch.result()).astype(bf16)
    gain_sum, inner_low = lax.optimization_barrier((inner_gain + gate_gain, inner_low))
    grad_gain = jnp.sum(share(gain_sum, SEQ + ("mod",)), axis=0) / gain_vals
    grad_in = jnp.stack([inner_low.transpose(2, 1, 0, 3), grad_gate], axis=2)
    grad_in = grad_in.reshape(MODS, slab, 2, seqs * channels).astype(f32)
    normed_sums.merge()
    normed_sums.stage(("zl", "zl"))
    normed_sums.hold([grad_in, grad_gain])
    normed_sums.stage(("zh", "zh"))
    normed_grad = normed_sums.result()
    step_grad_low, feat_late = held_back((step_grad_low, feat_grad), sent)
    step_t = feats[:, :, :, :R].transpose(3, 1, 0, 2, 4).reshape(R, -1)
    grad_step = dot(step_t, masked(step_grad_low, ids))
    grad_step = grad_step.reshape(R, MODS, channels).transpose(1, 0, 2)
    feat_late = feat_late.transpose(3, 1, 0, 2, 4).reshape(features, -1)
    feat_late = [
        jnp.where(ids_rows.reshape(1, -1) == m, feat_late, jnp.zeros_like(feat_late))
        for m in range(MODS)
    ]
    grad_param = dot(jnp.concatenate(feat_late, axis=0), act_low)
    grad_param = grad_param.reshape(MODS, features, channels).transpose(0, 2, 1)
    hat_grad = normed_grad * gain_vals[None, :]
    token_grad = cotangent.astype(f32) + inverse * (
        hat_grad - normal_rows * jnp.mean(hat_grad * normal_rows, axis=1, keepdims=True)
    )
    return (
        output,
        token_grad,
        grad_gain,
        grad_in,
        grad_param,
        grad_step,
        grad_out,
        tap_sums[:KW],
        tap_sums[KW],
        rate_sum * decay_rate,
        sums[MODS],
        sums[:MODS],
    )


def placed(spec, axes):
    entries = [
        sum((axes[name] for name in ((entry,) if isinstance(entry, str) else entry or ())), ())
        for entry in spec
    ]
    return P(*[entry or None for entry in entries])


def solution(mesh):
    token_rows = P(("seq", "mod"), None)
    in_weight = P(None, "seq", None, "mod")
    out_weight = P(None, "mod", "seq")
    row, column, depth = P(("mod", "seq")), P(None, ("mod", "seq")), P(None, None, ("mod", "seq"))
    middle = P(None, ("mod", "seq"), None)
    ins = (token_rows, P("seq"), P(), P(), in_weight, middle, depth, column, out_weight)
    ins += (column, row, column, row, token_rows)
    outs = (token_rows, token_rows, P(), in_weight, middle, depth, out_weight)
    outs += (column, row, column, row, column)

    def run(*args):
        sizes = (mesh.shape["seq"], mesh.shape["mod"])
        share_of_channels = args[12].shape[0] // (sizes[0] * sizes[1])
        if share_of_channels == LANES and sizes == (8, 4):
            part, over = channel_layout, jax.sharding.Mesh(
                mesh.devices.reshape(sizes[0] // 2, 2, sizes[1]), ("z", "core", "mod")
            )
            axes = {"seq": SEQ, "mod": ("mod",)}
        else:
            part, over = local, mesh
            axes = {"seq": ("seq",), "mod": ("mod",)}
        return jax.shard_map(
            part,
            mesh=over,
            in_specs=tuple(placed(spec, axes) for spec in ins),
            out_specs=tuple(placed(spec, axes) for spec in outs),
            check_vma=False,
        )(*args)

    return run
```

profile of v0, /device:TPU:0, one launch (start us, length us, event | category | flops | bytes accessed | tf_op | source)
XLA Modules:
  0.0 809.9 jit_solution(15337988551779950782)
XLA Ops:
  15.3 6.3 collective-permute-done
  25.9 5.1 collective-permute-done.1
  38.5 6.3 collective-permute-done.2
  49.9 4.6 reshape.1138
  76.6 8.9 %collective-permute-done.8 = bf16[2,2,128,512]{3,2,1,0:T(8,128)(2,1)} collective-permute-done((bf16[2,2,128,512]{3,2,1,0:T(8,128)(2,1)}, bf16[2,2,128,512]{3,2,1,0:T(8,128)(2,1)}, u32[]{:S(2)}, u32[]{:S(2)}) %collective-permute-start.8) | collective-permute-done | bytes 524320 | tf_op jit(solution)/shard_map/ppermute | solution.py:1202
  95.6 8.6 %collective-permute-done.16 = bf16[2,2,128,512]{3,2,1,0:T(8,128)(2,1)S(1)} collective-permute-done((bf16[2,2,128,512]{3,2,1,0:T(8,128)(2,1)S(1)}, bf16[2,2,128,512]{3,2,1,0:T(8,128)(2,1)S(1)}, u32[]{:S(2)}, u32[]{:S(2)}) %collective-permute-start.16) | collective-permute-done | bytes 524320 | tf_op jit(solution)/shard_map/ppermute | solution.py:1202
  105.4 18.4 %collective-permute-done.20 = bf16[2,2,128,512]{3,2,1,0:T(8,128)(2,1)S(1)} collective-permute-done((bf16[2,2,128,512]{3,2,1,0:T(8,128)(2,1)S(1)}, bf16[2,2,128,512]{3,2,1,0:T(8,128)(2,1)S(1)}, u32[]{:S(2)}, u32[]{:S(2)}) %collective-permute-start.20) | collective-permute-done | bytes 524320 | tf_op jit(solution)/shard_map/ppermute | solution.py:1202
  125.0 21.7 %all-to-all-done.refs_18_ = bf16[8,6,272,128]{3,2,1,0:T(8,128)(2,1)S(1)} async-done(((bf16[8,6,272,128]{3,2,1,0:T(8,128)(2,1)}), bf16[8,6,272,128]{3,2,1,0:T(8,128)(2,1)S(1)}, u32[]{:S(2)}, u32[]{:S(2)}) %all-to-all-start) | async-done | bytes 3342368 | tf_op jit(solution)/shard_map/all_to_all | solution.py:1193
  150.2 21.4 %collective-permute-done.21.refs_13_ = bf16[2,2,2,128,512]{4,3,2,1,0:T(8,128)(2,1)} collective-permute-done((bf16[2,2,2,128,512]{4,3,2,1,0:T(8,128)(2,1)}, bf16[2,2,2,128,512]{4,3,2,1,0:T(8,128)(2,1)}, u32[]{:S(2)}, u32[]{:S(2)}) %collective-permute-start.21) | collective-permute-done | bytes 1048608 | tf_op jit(solution)/shard_map/ppermute | solution.py:1202
  177.3 26.4 %project.1 = (bf16[4096,512]{1,0:T(8,128)(2,1)}, bf16[4096,512]{1,0:T(8,128)(2,1)}, bf16[4096,512]{1,0:T(8,128)(2,1)}, bf16[4096,512]{1,0:T(8,128)(2,1)}, bf16[2...) custom-call(s32[2]{0:T(128)} %lengths.7, ...), custom_call_target="tpu_custom_call" | custom-call | bytes 3690000 | tf_op jit(solution)/shard_map/project/pallas_call | solution.py:601
  215.9 14.8 %modal_rows.1.pre = f32[4096,128]{1,0:T(8,128)} custom-call(bf16[4096,512]{1,0:T(8,128)(2,1)} %get-tuple-element.92.refs_0_, bf16[4096,512]{1,0:T(8,128)(2,1)} %get-tuple-element.93.refs_1_, bf16[4096,512]{1,0:T(8,128)(2,1)} %get-tuple-element.94.refs_2_, bf16[4096,512]{1,0:T(8,128)(2,1)} %get-tuple-element.95.refs_3_, s32[4096,1]{1,0:T(8,128)} %copy.126.refs_4_, ...), custom_call_target="tpu_custom_call" | custom-call | bytes 3690000 | tf_op jit(solution)/shard_map/modal_rows/pallas_call | solution.py:644
  230.6 27.8 %all-to-all-done.1 = f32[16,160,128]{2,1,0:T(8,128)S(1)} async-done(((f32[16,160,128]{2,1,0:T(8,128)}), f32[16,160,128]{2,1,0:T(8,128)S(1)}, u32[]{:S(2)}, u32[]{:S(2)}) %all-to-all-start.1) | async-done | bytes 1310752 | tf_op jit(solution)/shard_map/all_to_all | solution.py:1193
  258.7 56.3 %all_to_all.46 = bf16[16,192,128]{2,1,0:T(8,128)(2,1)S(1)} all-to-all(bf16[16,192,128]{2,1,0:T(8,128)(2,1)S(1)} %broadcast_in_dim.131), channel_id=1, replica_groups=mesh['z'=4,'core'=2,'mod'=4] {'z','mod'}, dimensions={0} | all-to-all | bytes 1572864 | tf_op jit(solution)/shard_map/all_to_all | solution.py:1189
  320.3 6.4 all-to-all-start.3
  328.5 57.0 %scan.1 = (f32[4096,2048]{1,0:T(8,128)}, f32[8,2048]{1,0:T(8,128)}, f32[4096,128]{1,0:T(8,128)}, f32[4096,128]{1,0:T(8,128)}, f32[4096,128]{1,0:T(8,128)}) custom-call(s32[2]{0:T(128)} %lengths.7, s32[4096,1]{1,0:T(8,128)} %copy.124.refs_16_.ids_ref, bf16[2,4,4,192,128]{4,3,2,1,0:T(8,128)(2,1)} %maximum_select_fusion.feats, ...), custom_call_target="tpu_custom_call" | custom-call | bytes 3690000 | tf_op jit(solution)/shard_map/scan/pallas_call | solution.py:848
  386.6 18.5 %gates.1 = (bf16[2048,384]{1,0:T(8,128)(2,1)}, f32[4096,128]{1,0:T(8,128)}, bf16[4096,384]{1,0:T(8,128)(2,1)}, bf16[4096,384]{1,0:T(8,128)(2,1)}, bf16[4096,128]{1,0:T(8,128)(2,1)}, /*index=5*/bf16[4096,128]{1,0:T(8,128)(2,1)}) custom-call(bf16[4096,2048]{1,0:T(8,128)(2,1)} %all-gather.2.cloned.1.call-done.cot, s32[4096,1]{1,0:T(8,128)} %copy.124.refs_16_.ids_ref, ...), custom_call_target="tpu_custom_call" | custom-call | bytes 3690000 | tf_op jit(solution)/shard_map/gates/pallas_call | solution.py:709
  405.1 5.7 fusion.67
  428.2 13.4 %convolution_convert_fusion.6 = bf16[2048,384]{1,0:T(8,128)(2,1)} fusion(bf16[4096,2048]{1,0:T(8,128)(2,1)} %all-gather.2.cloned.1.call-done.cot, bf16[4096,384]{1,0:T(8,128)(2,1)S(1)} %copy-done.74), kind=kOutput, calls=%fused_computation.17 | convolution fusion | flops 6443237376 | bytes 21495808 | tf_op jit(solution)/shard_map/dot_general | solution.py:480
  445.2 5.1 all-to-all-start.4
  450.2 4.2 side_by_side.2
  474.9 74.8 %scan_back.1 = (f32[4096,128]{1,0:T(8,128)}, bf16[4096,128]{1,0:T(8,128)(2,1)}, f32[2,4,4,160,128]{4,3,2,1,0:T(8,128)}, f32[8,128]{1,0:T(8,128)}, f32[16,128]{1,0:T(8,128)}) custom-call(s32[2]{0:T(128)} %lengths.7, s32[3]{0:T(128)} %pad_add_fusion.place.core, s32[4096,1]{1,0:T(8,128)} %copy.124.refs_16_.ids_ref, s32[32,128]{1,0:T(8,128)} %reshape.1142.refs_17_.ids_rows, ...), custom_call_target="tpu_custom_call" | custom-call | bytes 3690000 | tf_op jit(solution)/shard_map/scan_back/pallas_call | solution.py:1058
  556.9 6.0 all-to-all-start.5
  569.0 11.7 %all-to-all-done.5 = bf16[16,160,128]{2,1,0:T(8,128)(2,1)} async-done(((bf16[16,160,128]{2,1,0:T(8,128)(2,1)}), bf16[16,160,128]{2,1,0:T(8,128)(2,1)}, u32[]{:S(2)}, u32[]{:S(2)}) %all-to-all-start.5) | async-done | bytes 655392 | tf_op jit(solution)/shard_map/all_to_all | solution.py:1193
  581.9 6.0 side_by_side.3
  588.8 4.9 all-to-all-start.6
  605.3 5.0 all-to-all-done.6
  620.6 12.5 %conv_back.1 = (bf16[4096,384]{1,0:T(8,128)(2,1)}, bf16[4096,128]{1,0:T(8,128)(2,1)}, f32[8,128]{1,0:T(8,128)}) custom-call(s32[2]{0:T(128)} %lengths.7, s32[4096,1]{1,0:T(8,128)} %copy.124.refs_16_.ids_ref, bf16[2,4,4,160,128]{4,3,2,1,0:T(8,128)(2,1)} %maximum_select_fusion.1.feat_grad, f32[4096,128]{1,0:T(8,128)} %get-tuple-element.126.act_part, ...), custom_call_target="tpu_custom_call" | custom-call | bytes 3690000 | tf_op jit(solution)/shard_map/conv_back/pallas_call | solution.py:1154
  686.0 4.3 all-to-all-start.7
  703.1 6.0 collective-permute-done.47
  739.5 4.7 copy.151
  774.0 7.6 collective-permute-done.50
  785.4 10.3 %copy.154 = f32[3,256,2,1024]{3,2,1,0:T(2,128)} copy(f32[3,256,2,1024]{1,3,0,2:T(8,128)} %maximum_convert_fusion) | data formatting | bytes 12582912
  (441 shorter events, 303.5 us)
Async XLA Ops:
  67.3 79.3 %all-to-all-start = ((bf16[8,6,272,128]{3,2,1,0:T(8,128)(2,1)}), bf16[8,6,272,128]{3,2,1,0:T(8,128)(2,1)S(1)}, u32[]{:S(2)}, u32[]{:S(2)}) async-start(bf16[8,6,272,128]{3,2,1,0:T(8,128)(2,1)} %pad_maximum_fusion), calls=%async_computation | async-start | bytes 6684672 | tf_op jit(solution)/shard_map/all_to_all | solution.py:1193
  71.0 314.5 %all-gather.2.cloned.1.call-start = ((), (), s32[]{:S(2)}) async-start(), calls=%async_computation.9 | async-start | bytes 17301504 | tf_op jit(solution)/shard_map/all_gather | solution.py:1389
  87.8 58.8 %collective-permute-start.9 = (bf16[2,2,2,128,512]{4,3,2,1,0:T(8,128)(2,1)}, bf16[2,2,2,128,512]{4,3,2,1,0:T(8,128)(2,1)}, u32[]{:S(2)}, u32[]{:S(2)}) collective-permute-start(bf16[2,2,2,128,512]{4,3,2,1,0:T(8,128)(2,1)} %maximum_select_fusion.2.refs_0_), channel_id=1, source_target_pairs={{0,2},{1,3},{2,0},{3,1},{4,6},{5,7},{6,4},{7,5},{8,10},{9,11},{10,... | collective-permute-start | bytes 3145736 | tf_op jit(solution)/shard_map/ppermute | solution.py:1202
  89.4 58.8 %collective-permute-start.10 = (bf16[2,2,2,128,512]{4,3,2,1,0:T(8,128)(2,1)}, bf16[2,2,2,128,512]{4,3,2,1,0:T(8,128)(2,1)}, u32[]{:S(2)}, u32[]{:S(2)}) collective-permute-start(bf16[2,2,2,128,512]{4,3,2,1,0:T(8,128)(2,1)} %maximum_select_fusion.2.refs_0_), channel_id=1, source_target_pairs={{0,4},{4,0},{1,5},{5,1},{2,6},{6,2},{3,7},{7,3},{8,12},{12,8},{9,1... | collective-permute-start | bytes 3145736 | tf_op jit(solution)/shard_map/ppermute | solution.py:1202
  92.2 31.7 %collective-permute-start.20 = (bf16[2,2,128,512]{3,2,1,0:T(8,128)(2,1)S(1)}, bf16[2,2,128,512]{3,2,1,0:T(8,128)(2,1)S(1)}, u32[]{:S(2)}, u32[]{:S(2)}) collective-permute-start(bf16[2,2,128,512]{3,2,1,0:T(8,128)(2,1)S(1)} %copy-done.61), channel_id=1, source_target_pairs={{0,2},{1,3},{2,0},{3,1},{4,6},{5,7},{6,4},{7,5},{8,10},{9,11},{10,... | collective-permute-start | bytes 1572872 | tf_op jit(solution)/shard_map/ppermute | solution.py:1202
  95.0 54.7 %collective-permute-start.13 = (bf16[2,2,2,128,512]{4,3,2,1,0:T(8,128)(2,1)}, bf16[2,2,2,128,512]{4,3,2,1,0:T(8,128)(2,1)}, u32[]{:S(2)}, u32[]{:S(2)}) collective-permute-start(bf16[2,2,2,128,512]{4,3,2,1,0:T(8,128)(2,1)} %maximum_select_fusion.3.refs_4_), channel_id=1, source_target_pairs={{0,1},{1,0},{2,3},{3,2},{4,5},{5,4},{6,7},{7,6},{8,9},{9,8},{10,11... | collective-permute-start | bytes 3145736 | tf_op jit(solution)/shard_map/ppermute | solution.py:1202
  104.3 45.4 %collective-permute-start.14 = (bf16[2,2,2,128,512]{4,3,2,1,0:T(8,128)(2,1)}, bf16[2,2,2,128,512]{4,3,2,1,0:T(8,128)(2,1)}, u32[]{:S(2)}, u32[]{:S(2)}) collective-permute-start(bf16[2,2,2,128,512]{4,3,2,1,0:T(8,128)(2,1)} %maximum_select_fusion.3.refs_4_), channel_id=1, source_target_pairs={{0,4},{4,0},{1,5},{5,1},{2,6},{6,2},{3,7},{7,3},{8,12},{12,8},{9,1... | collective-permute-start | bytes 3145736 | tf_op jit(solution)/shard_map/ppermute | solution.py:1202
  123.8 26.3 %collective-permute-start.18 = (bf16[2,2,2,128,512]{4,3,2,1,0:T(8,128)(2,1)}, bf16[2,2,2,128,512]{4,3,2,1,0:T(8,128)(2,1)}, u32[]{:S(2)}, u32[]{:S(2)}) collective-permute-start(bf16[2,2,2,128,512]{4,3,2,1,0:T(8,128)(2,1)} %maximum_select_fusion.4.refs_8_), channel_id=1, source_target_pairs={{0,4},{4,0},{1,5},{5,1},{2,6},{6,2},{3,7},{7,3},{8,12},{12,8},{9,1... | collective-permute-start | bytes 3145736 | tf_op jit(solution)/shard_map/ppermute | solution.py:1202
  149.7 27.6 %collective-permute-start.22 = (bf16[2,2,2,128,512]{4,3,2,1,0:T(8,128)(2,1)}, bf16[2,2,2,128,512]{4,3,2,1,0:T(8,128)(2,1)}, u32[]{:S(2)}, u32[]{:S(2)}) collective-permute-start(bf16[2,2,2,128,512]{4,3,2,1,0:T(8,128)(2,1)} %maximum_select_fusion.5.refs_12_), channel_id=1, source_target_pairs={{0,4},{4,0},{1,5},{5,1},{2,6},{6,2},{3,7},{7,3},{8,12},{12,8},{9,1... | collective-permute-start | bytes 3145736 | tf_op jit(solution)/shard_map/ppermute | solution.py:1202
  149.7 27.6 %collective-permute-start.11 = (bf16[2,2,2,128,512]{4,3,2,1,0:T(8,128)(2,1)}, bf16[2,2,2,128,512]{4,3,2,1,0:T(8,128)(2,1)}, u32[]{:S(2)}, u32[]{:S(2)}) collective-permute-start(bf16[2,2,2,128,512]{4,3,2,1,0:T(8,128)(2,1)} %collective-permute-done.9.refs_1_), channel_id=1, source_target_pairs={{0,4},{4,0},{1,5},{5,1},{2,6},{6,2},{3,7},{7,3},{8,12},{12,8},{9,1... | collective-permute-start | bytes 3145736 | tf_op jit(solution)/shard_map/ppermute | solution.py:1202
  150.2 27.1 %collective-permute-start.15 = (bf16[2,2,2,128,512]{4,3,2,1,0:T(8,128)(2,1)}, bf16[2,2,2,128,512]{4,3,2,1,0:T(8,128)(2,1)}, u32[]{:S(2)}, u32[]{:S(2)}) collective-permute-start(bf16[2,2,2,128,512]{4,3,2,1,0:T(8,128)(2,1)} %collective-permute-done.13.refs_5_), channel_id=1, source_target_pairs={{0,4},{4,0},{1,5},{5,1},{2,6},{6,2},{3,7},{7,3},{8,12},{12,8},{9,1... | collective-permute-start | bytes 3145736 | tf_op jit(solution)/shard_map/ppermute | solution.py:1202
  209.8 48.6 %all-to-all-start.1 = ((f32[16,160,128]{2,1,0:T(8,128)}), f32[16,160,128]{2,1,0:T(8,128)S(1)}, u32[]{:S(2)}, u32[]{:S(2)}) async-start(f32[16,160,128]{2,1,0:T(8,128)} %bitcast.44), calls=%async_computation.1 | async-start | bytes 2621440 | tf_op jit(solution)/shard_map/all_to_all | solution.py:1193
  320.3 65.2 %all-to-all-start.3 = ((bf16[8,3,256,128]{3,2,1,0:T(8,128)(2,1)}), bf16[8,3,256,128]{3,2,1,0:T(8,128)(2,1)S(1)}, u32[]{:S(2)}, u32[]{:S(2)}) async-start(bf16[8,3,256,128]{3,2,1,0:T(8,128)(2,1)} %bitcast.41), calls=%async_computation.3 | async-start | bytes 3145728 | tf_op jit(solution)/shard_map/all_to_all | solution.py:1193
  445.2 104.6 %all-to-all-start.4 = ((bf16[8,256,768]{1,2,0:T(8,128)(2,1)}), bf16[8,256,768]{1,2,0:T(8,128)(2,1)S(1)}, u32[]{:S(2)}, u32[]{:S(2)}) async-start(bf16[8,256,768]{1,2,0:T(8,128)(2,1)} %pad_maximum_fusion.1), calls=%async_computation.4 | async-start | bytes 6291456 | tf_op jit(solution)/shard_map/all_to_all | solution.py:1193
  462.7 87.0 %collective-permute-start.29 = (bf16[2,2,2,128,1024]{4,3,1,0,2:T(8,128)(2,1)}, bf16[2,2,2,128,1024]{4,3,1,0,2:T(8,128)(2,1)}, u32[]{:S(2)}, u32[]{:S(2)}) collective-permute-start(bf16[2,2,2,128,1024]{4,3,1,0,2:T(8,128)(2,1)} %copy_bitcast_fusion), channel_id=1, source_target_pairs={{0,2},{1,3},{2,0},{3,1},{4,6},{5,7},{6,4},{7,5},{8,10},{9,11},{10,... | collective-permute-start | bytes 6291464 | tf_op jit(solution)/shard_map/ppermute | solution.py:1202
  471.9 77.8 %collective-permute-start.28 = (bf16[2,2,2,128,1024]{4,3,1,0,2:T(8,128)(2,1)}, bf16[2,2,2,128,1024]{4,3,1,0,2:T(8,128)(2,1)}, u32[]{:S(2)}, u32[]{:S(2)}) collective-permute-start(bf16[2,2,2,128,1024]{4,3,1,0,2:T(8,128)(2,1)} %copy_bitcast_fusion.1), channel_id=1, source_target_pairs={{0,1},{1,0},{2,3},{3,2},{4,5},{5,4},{6,7},{7,6},{8,9},{9,8},{10,11... | collective-permute-start | bytes 6291464 | tf_op jit(solution)/shard_map/ppermute | solution.py:1202
  556.4 25.5 %collective-permute-start.32 = (bf16[2048,384]{1,0:T(8,128)(2,1)}, bf16[2048,384]{1,0:T(8,128)(2,1)}, u32[]{:S(2)}, u32[]{:S(2)}) collective-permute-start(bf16[2048,384]{1,0:T(8,128)(2,1)} %get-tuple-element.121.refs_0_), channel_id=1, source_target_pairs={{0,4},{4,0},{1,5},{5,1},{2,6},{6,2},{3,7},{7,3},{8,12},{12,8},{9,1... | collective-permute-start | bytes 4718600 | tf_op jit(solution)/shard_map/ppermute | solution.py:1202
  556.5 25.3 %collective-permute-start.33 = (bf16[2048,384]{1,0:T(8,128)(2,1)}, bf16[2048,384]{1,0:T(8,128)(2,1)}, u32[]{:S(2)}, u32[]{:S(2)}) collective-permute-start(bf16[2048,384]{1,0:T(8,128)(2,1)} %get-tuple-element.122.refs_5_.refs_2_), channel_id=1, source_target_pairs={{0,4},{4,0},{1,5},{5,1},{2,6},{6,2},{3,7},{7,3},{8,12},{12,8},{9,1... | collective-permute-start | bytes 4718600 | tf_op jit(solution)/shard_map/ppermute | solution.py:1202
  600.6 38.4 %collective-permute-start.30 = (bf16[2,2,128,1024]{3,2,1,0:T(8,128)(2,1)}, bf16[2,2,128,1024]{3,2,1,0:T(8,128)(2,1)}, u32[]{:S(2)}, u32[]{:S(2)}) collective-permute-start(bf16[2,2,128,1024]{3,2,1,0:T(8,128)(2,1)} %fusion.7), channel_id=1, source_target_pairs={{0,2},{1,3},{2,0},{3,1},{4,6},{5,7},{6,4},{7,5},{8,10},{9,11},{10,... | collective-permute-start | bytes 3145736 | tf_op jit(solution)/shard_map/ppermute | solution.py:1202
  602.6 36.4 %collective-permute-start.35 = (bf16[2,2,128,1024]{3,2,1,0:T(8,128)(2,1)}, bf16[2,2,128,1024]{3,2,1,0:T(8,128)(2,1)}, u32[]{:S(2)}, u32[]{:S(2)}) collective-permute-start(bf16[2,2,128,1024]{3,2,1,0:T(8,128)(2,1)} %fusion.6), channel_id=1, source_target_pairs={{0,1},{1,0},{2,3},{3,2},{4,5},{5,4},{6,7},{7,6},{8,9},{9,8},{10,11... | collective-permute-start | bytes 3145736 | tf_op jit(solution)/shard_map/ppermute | solution.py:1202
  614.1 28.6 %collective-permute-start.37 = (bf16[2048,128]{1,0:T(8,128)(2,1)}, bf16[2048,128]{1,0:T(8,128)(2,1)S(1)}, u32[]{:S(2)}, u32[]{:S(2)}) collective-permute-start(bf16[2048,128]{1,0:T(8,128)(2,1)} %bitcast.77), channel_id=1, source_target_pairs={{0,4},{4,0},{1,5},{5,1},{2,6},{6,2},{3,7},{7,3},{8,12},{12,8},{9,1... | collective-permute-start | bytes 1572872 | tf_op jit(solution)/shard_map/ppermute | solution.py:1202
  660.3 36.8 %collective-permute-start.41 = (bf16[2,2,2,128,512]{4,3,1,0,2:T(8,128)(2,1)}, bf16[2,2,2,128,512]{4,3,1,0,2:T(8,128)(2,1)}, u32[]{:S(2)}, u32[]{:S(2)}) collective-permute-start(bf16[2,2,2,128,512]{4,3,1,0,2:T(8,128)(2,1)} %copy_bitcast_fusion.4), channel_id=1, source_target_pairs={{0,2},{1,3},{2,0},{3,1},{4,6},{5,7},{6,4},{7,5},{8,10},{9,11},{10,... | collective-permute-start | bytes 3145736 | tf_op jit(solution)/shard_map/ppermute | solution.py:1202
  662.7 37.1 %collective-permute-start.40 = (bf16[2,2,2,128,512]{4,3,1,0,2:T(8,128)(2,1)}, bf16[2,2,2,128,512]{4,3,1,0,2:T(8,128)(2,1)}, u32[]{:S(2)}, u32[]{:S(2)}) collective-permute-start(bf16[2,2,2,128,512]{4,3,1,0,2:T(8,128)(2,1)} %copy_bitcast_fusion.5), channel_id=1, source_target_pairs={{0,1},{1,0},{2,3},{3,2},{4,5},{5,4},{6,7},{7,6},{8,9},{9,8},{10,11... | collective-permute-start | bytes 3145736 | tf_op jit(solution)/shard_map/ppermute | solution.py:1202
  664.4 44.6 %collective-permute-start.47 = (bf16[2,2,2,128,512]{4,3,1,0,2:T(8,128)(2,1)}, bf16[2,2,2,128,512]{4,3,1,0,2:T(8,128)(2,1)}, u32[]{:S(2)}, u32[]{:S(2)}) collective-permute-start(bf16[2,2,2,128,512]{4,3,1,0,2:T(8,128)(2,1)} %copy_bitcast_fusion.2), channel_id=1, source_target_pairs={{0,2},{1,3},{2,0},{3,1},{4,6},{5,7},{6,4},{7,5},{8,10},{9,11},{10,... | collective-permute-start | bytes 3145736 | tf_op jit(solution)/shard_map/ppermute | solution.py:1202
  666.1 45.6 %collective-permute-start.46 = (bf16[2,2,2,128,512]{4,3,1,0,2:T(8,128)(2,1)}, bf16[2,2,2,128,512]{4,3,1,0,2:T(8,128)(2,1)}, u32[]{:S(2)}, u32[]{:S(2)}) collective-permute-start(bf16[2,2,2,128,512]{4,3,1,0,2:T(8,128)(2,1)} %copy_bitcast_fusion.3), channel_id=1, source_target_pairs={{0,1},{1,0},{2,3},{3,2},{4,5},{5,4},{6,7},{7,6},{8,9},{9,8},{10,11... | collective-permute-start | bytes 3145736 | tf_op jit(solution)/shard_map/ppermute | solution.py:1202
  676.2 44.1 %collective-permute-start.38 = (bf16[2,128,2048]{2,1,0:T(8,128)(2,1)}, bf16[2,128,2048]{2,1,0:T(8,128)(2,1)}, u32[]{:S(2)}, u32[]{:S(2)}) collective-permute-start(bf16[2,128,2048]{2,1,0:T(8,128)(2,1)} %fusion.25), channel_id=1, source_target_pairs={{0,8},{8,0},{16,24},{24,16},{1,9},{9,1},{17,25},{25,17},{2,10},{10... | collective-permute-start | bytes 3145736 | tf_op jit(solution)/shard_map/ppermute | solution.py:1202
  686.0 67.6 %all-to-all-start.7 = ((bf16[8,256,384]{1,2,0:T(8,128)(2,1)}), bf16[8,256,384]{1,2,0:T(8,128)(2,1)}, u32[]{:S(2)}, u32[]{:S(2)}) async-start(bf16[8,256,384]{1,2,0:T(8,128)(2,1)} %copy.143), calls=%async_computation.7 | async-start | bytes 3145728 | tf_op jit(solution)/shard_map/all_to_all | solution.py:1193
  699.3 46.1 %collective-permute-start.43 = (bf16[2,2,128,512]{3,2,1,0:T(8,128)(2,1)}, bf16[2,2,128,512]{3,2,1,0:T(8,128)(2,1)}, u32[]{:S(2)}, u32[]{:S(2)}) collective-permute-start(bf16[2,2,128,512]{3,2,1,0:T(8,128)(2,1)} %fusion.30), channel_id=1, source_target_pairs={{0,1},{1,0},{2,3},{3,2},{4,5},{5,4},{6,7},{7,6},{8,9},{9,8},{10,11... | collective-permute-start | bytes 1572872 | tf_op jit(solution)/shard_map/ppermute | solution.py:1202
  702.0 42.3 %collective-permute-start.42 = (bf16[2,2,128,512]{3,2,1,0:T(8,128)(2,1)}, bf16[2,2,128,512]{3,2,1,0:T(8,128)(2,1)}, u32[]{:S(2)}, u32[]{:S(2)}) collective-permute-start(bf16[2,2,128,512]{3,2,1,0:T(8,128)(2,1)} %fusion.31), channel_id=1, source_target_pairs={{0,2},{1,3},{2,0},{3,1},{4,6},{5,7},{6,4},{7,5},{8,10},{9,11},{10,... | collective-permute-start | bytes 1572872 | tf_op jit(solution)/shard_map/ppermute | solution.py:1202
  711.2 46.4 %collective-permute-start.49 = (bf16[2,2,128,512]{3,2,1,0:T(8,128)(2,1)}, bf16[2,2,128,512]{3,2,1,0:T(8,128)(2,1)}, u32[]{:S(2)}, u32[]{:S(2)}) collective-permute-start(bf16[2,2,128,512]{3,2,1,0:T(8,128)(2,1)} %fusion.28), channel_id=1, source_target_pairs={{0,1},{1,0},{2,3},{3,2},{4,5},{5,4},{6,7},{7,6},{8,9},{9,8},{10,11... | collective-permute-start | bytes 1572872 | tf_op jit(solution)/shard_map/ppermute | solution.py:1202
  713.7 38.1 %collective-permute-start.48 = (bf16[2,2,128,512]{3,2,1,0:T(8,128)(2,1)}, bf16[2,2,128,512]{3,2,1,0:T(8,128)(2,1)}, u32[]{:S(2)}, u32[]{:S(2)}) collective-permute-start(bf16[2,2,128,512]{3,2,1,0:T(8,128)(2,1)} %fusion.29), channel_id=1, source_target_pairs={{0,2},{1,3},{2,0},{3,1},{4,6},{5,7},{6,4},{7,5},{8,10},{9,11},{10,... | collective-permute-start | bytes 1572872 | tf_op jit(solution)/shard_map/ppermute | solution.py:1202
  722.8 76.7 %collective-permute-start.39 = (bf16[128,2048]{1,0:T(8,128)(2,1)}, bf16[128,2048]{1,0:T(8,128)(2,1)}, u32[]{:S(2)}, u32[]{:S(2)}) collective-permute-start(bf16[128,2048]{1,0:T(8,128)(2,1)} %fusion.32), channel_id=1, source_target_pairs={{0,16},{8,24},{16,0},{24,8},{1,17},{9,25},{17,1},{25,9},{2,18},{10... | collective-permute-start | bytes 1572872 | tf_op jit(solution)/shard_map/ppermute | solution.py:1202
  (109 other events, 1294.6 us)
Sparse Core Ops, SparseCore 0:
  203.9 165.8 all-gather.1
where the time goes:
time: 821 us; the launch traced here: 810 us
  Pallas kernels  214 us (26%)
  waiting for transfers between devices  168 us (20%)
  local copies, waits for them, and re-layouts  102 us (12%)
  other arithmetic  97.9 us (12%)
  starting transfers between devices  91.3 us (11%)
  matrix products  65 us (8%)
  blocking collectives  56.3 us (7%)
  between operations  15.8 us (2%)
    ppermute x52, waiting for transfers between devices, flip(): lax.ppermute(value, axis, [(i, i ^ bit) for i in range(size)])  101 us
    pallas_call x1, Pallas kernels, scan_back(): pl.pallas_call(back_kernel, grid=(chunks,), in_specs=[pl.BlockSpec(memory...  74.8 us
    dot_general x17, matrix products, dot(): lax.dot_general(left, right, (((left_dim,), (right_dim,)), ((), ())), pre...  65 us
    all_to_all x6, waiting for transfers between devices, exchange(): return lax.all_to_all(blocks, axes, 0, 0)  61.1 us
    pallas_call x1, Pallas kernels, scan(): pl.pallas_call(scan_kernel, grid=(total // rows,), in_specs=[pl.BlockSpec...  57 us
    all_to_all x1, blocking collectives, share(): lax.all_to_all(jnp.broadcast_to(values, (size,) + values.shape), axes, 0, 0)  56.3 us
    ppermute x52, starting transfers between devices, flip(): lax.ppermute(value, axis, [(i, i ^ bit) for i in range(size)])  53.7 us
    all_to_all x6, starting transfers between devices, exchange(): return lax.all_to_all(blocks, axes, 0, 0)  29.6 us
  transfers between devices with their start and end apart: 61, of which 22 were waited for; matrix products, arithmetic and copies ran while one was open for 24% of the time, Pallas kernels for 20%

commit v1 on v0

--- a/solution.py
+++ b/solution.py
@@ -20,10 +20,9 @@
 SCAN_ROWS = 512
 
 LANES = 128
-SEGMENTS = 8
-CHUNK = 32
-UNROLL = 8
-BACK = 4
+SUB = 8
+STEPS = 4
+UNROLL = 4
 COLUMNS = 4
 FAR = 1e9
 VMEM_BYTES = 60 * 1024 * 1024
@@ -486,14 +485,6 @@
     return first + lax.broadcasted_iota(jnp.int32, (rows, 1), 0)
 
 
-def lane(values, at):
-    return jnp.broadcast_to(values[:, at : at + 1], (SEGMENTS, LANES))
-
-
-def tile(at):
-    return pl.ds(at * LANES, LANES)
-
-
 def whole(shape):
     return pl.BlockSpec(shape, lambda *_: (0,) * len(shape), pipeline_mode=pl.Buffered(1))
 
@@ -731,6 +722,43 @@
     )(cotangents, ids, blocks, pre, out)
 
 
+def spread_rates(rate_t, out):
+    for group in range(rate_t.shape[0] // SUB):
+        rows = rate_t[group * SUB : (group + 1) * SUB, :]
+        for n in range(N):
+            at = (group * N + n) * SUB
+            out[at : at + SUB, :] = jnp.broadcast_to(rows[:, n : n + 1], (SUB, LANES))
+
+
+def turned_rows(tau, length):
+    return pl.ds(tau, LANES, stride=length)
+
+
+def step_rows(tau, rows=LANES):
+    return pl.ds(pl.multiple_of(tau * rows, rows), rows)
+
+
+def over_segments(spent, ends, rates, backward):
+    at = lax.broadcasted_iota(jnp.int32, (SUB, LANES), 1)
+    ends = list(ends)
+    reach = 1
+    while reach < LANES:
+        shift = LANES - reach if backward else reach
+        inside = at < LANES - reach if backward else at >= reach
+        for n in range(N):
+            earlier = jnp.where(inside, pltpu.roll(ends[n], shift, 1), 0.0)
+            ends[n] = ends[n] + jnp.exp2(spent * rates[n]) * earlier
+        spent = spent + jnp.where(inside, pltpu.roll(spent, shift, 1), 0.0)
+        reach *= 2
+    shift = LANES - 1 if backward else 1
+    inside = at < LANES - 1 if backward else at >= 1
+    return [jnp.where(inside, pltpu.roll(end, shift, 1), 0.0) for end in ends]
+
+
+def pieces_of(values, count):
+    return [values[n * SUB : (n + 1) * SUB] for n in range(count)]
+
+
 def scan_kernel(
     lengths,
     ids_ref,
@@ -738,132 +766,150 @@
     pre,
     step_w,
     step_b,
-    rate,
+    rate_t,
     skip,
     states,
     enter,
     step_pre,
-    mix,
-    scan_out,
     s_turn,
     u_turn,
     mix_turn,
+    scan_out,
+    s_flat,
+    u_flat,
+    mix_flat,
     y_turn,
     held,
+    rates,
 ):
     chunk = pl.program_id(0)
-    total = pre.shape[0]
-    length = total // SEGMENTS
-    steps = states.shape[0] // SEGMENTS
+    total, channels = pre.shape
+    length = total // LANES
+    steps = states.shape[0]
+    groups = channels // SUB
     split = lengths[0]
-    rows_on = UNROLL * SEGMENTS
-
-    def rated(n):
-        return jnp.broadcast_to(rate[n : n + 1, :], (SEGMENTS, LANES))
-
-    def cut(values):
-        return [values[j * SEGMENTS : (j + 1) * SEGMENTS] for j in range(UNROLL)]
+    wide = N * SUB
 
     @pl.when(chunk == 0)
     def _():
-        for seg in range(SEGMENTS):
-            rows = pl.ds(seg * length, length)
-            turned = pl.ds(seg, length, stride=SEGMENTS)
-            ids = ids_ref[rows, :]
-            block_rows = length // feats.shape[2]
-            for j in range(feats.shape[2]):
-                block = pl.ds(seg * length + j * block_rows, block_rows)
+        spread_rates(rate_t, rates)
+        across = feats.shape[2]
+        block_rows = feats.shape[4]
+        for seq in range(2 * feats.shape[1]):
+            for j in range(across):
+                first = (seq * across + j) * block_rows
+                block = pl.ds(first, block_rows)
                 block_ids = ids_ref[block, :]
-                low = feats[seg % 2, seg // 2, j, 0:R, :]
-                step_pre[block, :] = pick(
-                    block_ids, [dot(low, step_w[m], 0, 0) for m in range(MODS)]
-                ) + pick(block_ids, [step_b[m : m + 1, :] for m in range(MODS)])
-                mixed = feats[seg % 2, seg // 2, j, R : R + 2 * N, :].astype(f32)
-                mixed = mixed + feats[seg % 2, seg // 2, j, R + 2 * N :, :].astype(f32)
+                low = feats[seq % 2, seq // 2, j, 0:R, :]
+                here = pick(block_ids, [dot(low, step_w[m], 0, 0) for m in range(MODS)]) + pick(
+                    block_ids, [step_b[m : m + 1, :] for m in range(MODS)]
+                )
+                step_pre[block, :] = here
+                step = softplus(here)
+                places = row_places(first, block_rows)
+                start = (places == 0) | (places == split)
+                s_flat[block, :] = jnp.where(start, FAR, step)
+                u_flat[block, :] = step * silu(pre[block, :])
+                mixed = feats[seq % 2, seq // 2, j, R : R + 2 * N, :].astype(f32)
+                mixed = mixed + feats[seq % 2, seq // 2, j, R + 2 * N :, :].astype(f32)
                 blank = jnp.zeros((LANES - 2 * N, block_rows), f32)
-                mix[block, :] = jnp.transpose(jnp.concatenate([mixed, blank], axis=0))
-            step = softplus(step_pre[rows, :])
-            places = row_places(seg * length, length)
-            start = (places == 0) | (places == split)
-            s_turn[turned, :] = jnp.where(start, FAR, step)
-            u_turn[turned, :] = step * silu(pre[rows, :])
-            mix_turn[turned, :] = mix[rows, :]
-
-        def ahead(i, spent):
-            at = pl.ds(pl.multiple_of(i * rows_on, rows_on), rows_on)
-            s, u, bc = [cut(v[at, :]) for v in (s_turn, u_turn, mix_turn)]
+                mix_flat[block, :] = jnp.transpose(jnp.concatenate([mixed, blank], axis=0))
+
+        def turn(tau, carried):
+            rows = turned_rows(tau, length)
+            s_turn[step_rows(tau), :] = jnp.transpose(s_flat[rows, :])
+            u_turn[step_rows(tau), :] = jnp.transpose(u_flat[rows, :])
+            mixed = jnp.transpose(mix_flat[rows, :])
+            spread = [jnp.broadcast_to(mixed[n : n + 1, :], (SUB, LANES)) for n in range(2 * N)]
+            mix_turn[step_rows(tau, 2 * wide), :] = jnp.concatenate(spread, axis=0)
+            return carried
+
+        lax.fori_loop(0, length, turn, 0)
+
+        def ahead(group, carried):
+            rate = pieces_of(rates[step_rows(group, wide), :], N)
+
+            def some(i, carried):
+                hidden, spent = list(carried[0]), carried[1]
+                for j in range(UNROLL):
+                    tau = i * UNROLL + j
+                    at = pl.ds(pl.multiple_of(tau * channels + group * SUB, SUB), SUB)
+                    s, u = s_turn[at, :], u_turn[at, :]
+                    for n in range(N):
+                        row = pl.ds(pl.multiple_of((tau * 2 * N + n) * SUB, SUB), SUB)
+                        hidden[n] = jnp.exp2(s * rate[n]) * hidden[n] + u * mix_turn[row, :]
+                    spent = spent + s
+                return hidden, spent
+
+            zero = jnp.zeros((SUB, LANES), f32)
+            ends, spent = lax.fori_loop(0, length // UNROLL, some, ([zero] * N, zero))
+            inside = jnp.concatenate(over_segments(spent, ends, rate, False), axis=0)
+            held[step_rows(group, wide), :] = inside
+            enter[step_rows(group, wide), :] = inside
+            return carried
+
+        lax.fori_loop(0, groups, ahead, 0)
+
+    def advance(group, carried):
+        own = step_rows(group, wide)
+        rate = pieces_of(rates[own, :], N)
+        hidden = pieces_of(held[own, :], N)
+        for j in range(steps):
+            tau = chunk * steps + j
+            at = pl.ds(pl.multiple_of(tau * channels + group * SUB, SUB), SUB)
+            s, u = s_turn[at, :], u_turn[at, :]
+            terms = []
             for n in range(N):
-                rate_n, hidden = rated(n), held[:, tile(n)]
-                for j in range(UNROLL):
-                    hidden = jnp.exp2(s[j] * rate_n) * hidden + u[j] * lane(bc[j], n)
-                held[:, tile(n)] = hidden
-            return spent + sum(s)
-
-        zero = jnp.zeros((SEGMENTS, LANES), f32)
-        held[...] = jnp.zeros(held.shape, f32)
-        spent = lax.fori_loop(0, length // UNROLL, ahead, zero)
-        first = lax.broadcasted_iota(jnp.int32, (SEGMENTS, LANES), 0) == 0
-        for n in range(N):
-            through = jnp.exp2(spent * rated(n))
-            end = held[:, tile(n)]
-            inside = zero
-            for _ in range(SEGMENTS - 1):
-                inside = jnp.where(first, 0.0, pltpu.roll(end + through * inside, 1, 0))
-            held[:, tile(n)] = inside
-            enter[:, tile(n)] = inside
-
-    base = chunk * steps
-
-    def steps_on(i, carried):
-        at = pl.ds(pl.multiple_of((base + i * UNROLL) * SEGMENTS, rows_on), rows_on)
-        s, u, bc = [cut(v[at, :]) for v in (s_turn, u_turn, mix_turn)]
-        result = [0.0] * UNROLL
-        for n in range(N):
-            rate_n, hidden = rated(n), held[:, tile(n)]
-            for j in range(UNROLL):
-                hidden = jnp.exp2(s[j] * rate_n) * hidden + u[j] * lane(bc[j], n)
-                out = pl.ds(pl.multiple_of((i * UNROLL + j) * SEGMENTS, SEGMENTS), SEGMENTS)
-                states[out, tile(n)] = hidden
-                result[j] = result[j] + hidden * lane(bc[j], N + n)
-            held[:, tile(n)] = hidden
-        y_turn[at, :] = jnp.concatenate(result, axis=0)
+                row = pl.ds(pl.multiple_of((tau * 2 * N + n) * SUB, SUB), SUB)
+                other = pl.ds(pl.multiple_of((tau * 2 * N + N + n) * SUB, SUB), SUB)
+                hidden[n] = jnp.exp2(s * rate[n]) * hidden[n] + u * mix_turn[row, :]
+                states[j, pl.ds(pl.multiple_of((group * N + n) * SUB, SUB), SUB), :] = hidden[n]
+                terms.append(hidden[n] * mix_turn[other, :])
+            while len(terms) > 1:
+                terms = [a + b for a, b in zip(terms[::2], terms[1::2])]
+            y_turn[at, :] = terms[0]
+        held[own, :] = jnp.concatenate(hidden, axis=0)
         return carried
 
-    lax.fori_loop(0, steps // UNROLL, steps_on, 0)
+    lax.fori_loop(0, groups, advance, 0)
 
     @pl.when(chunk == pl.num_programs(0) - 1)
     def _():
-        for seg in range(SEGMENTS):
-            rows = pl.ds(seg * length, length)
-            turned = pl.ds(seg, length, stride=SEGMENTS)
-            scan_out[rows, :] = y_turn[turned, :] + skip[...] * silu(pre[rows, :])
-
-
-def scan(lengths, ids, feats, pre, step_w, step_b, rate, skip):
+        def turn_back(tau, carried):
+            s_flat[turned_rows(tau, length), :] = jnp.transpose(y_turn[step_rows(tau), :])
+            return carried
+
+        lax.fori_loop(0, length, turn_back, 0)
+        for block in range(total // 512):
+            rows = pl.ds(block * 512, 512)
+            scan_out[rows, :] = s_flat[rows, :] + skip[...] * silu(pre[rows, :])
+
+
+def scan(lengths, ids, feats, pre, step_w, step_b, rate_t, skip):
     total, channels = pre.shape
-    steps = math.gcd(total // SEGMENTS, CHUNK)
-    rows = steps * SEGMENTS
-    turn = pltpu.VMEM((total, channels), f32)
-    ins = (ids, feats, pre, step_w, step_b, rate, skip)
+    length = total // LANES
+    steps = math.gcd(length, STEPS)
+    wide = N * channels
+    flat = pltpu.VMEM((total, channels), f32)
+    ins = (ids, feats, pre, step_w, step_b, rate_t, skip)
+    shapes = [
+        (wide, LANES),
+        (total, channels),
+        (length * channels, LANES),
+        (length * channels, LANES),
+        (length * 2 * N * SUB, LANES),
+        (total, channels),
+    ]
     return pl.pallas_call(
         scan_kernel,
-        grid=(total // rows,),
+        grid=(length // steps,),
         in_specs=[pl.BlockSpec(memory_space=pltpu.SMEM)] + [whole(a.shape) for a in ins],
-        out_specs=[
-            pl.BlockSpec((rows, N * channels), lambda i: (i, 0)),
-            whole((SEGMENTS, N * channels)),
-            whole((total, channels)),
-            whole((total, channels)),
-            whole((total, channels)),
-        ],
-        out_shape=[
-            jax.ShapeDtypeStruct((total, N * channels), f32),
-            jax.ShapeDtypeStruct((SEGMENTS, N * channels), f32),
-            jax.ShapeDtypeStruct((total, channels), f32),
-            jax.ShapeDtypeStruct((total, channels), f32),
-            jax.ShapeDtypeStruct((total, channels), f32),
-        ],
-        scratch_shapes=[turn, turn, turn, turn, pltpu.VMEM((SEGMENTS, N * channels), f32)],
+        out_specs=[pl.BlockSpec((steps, wide, LANES), lambda i: (i, 0, 0))]
+        + [whole(shape) for shape in shapes],
+        out_shape=[jax.ShapeDtypeStruct((length, wide, LANES), f32)]
+        + [jax.ShapeDtypeStruct(shape, f32) for shape in shapes],
+        scratch_shapes=[flat, flat, flat, pltpu.VMEM((length * channels, LANES), f32)]
+        + [pltpu.VMEM((wide, LANES), f32)] * 2,
         compiler_params=pltpu.CompilerParams(vmem_limit_bytes=VMEM_BYTES),
         cost_estimate=cost(1),
         name="scan",
@@ -871,11 +917,12 @@
 
 
 def back_kernel(
-    lengths,
     core,
     ids_ref,
     ids_rows,
-    mix,
+    s_turn,
+    u_turn,
+    mix_turn,
     pre,
     step_pre,
     grad,
@@ -883,188 +930,188 @@
     before,
     enter,
     step_w,
-    rate,
+    rate_t,
     skip,
-    gather_in,
-    gather_out,
     act_part,
     step_grad_low,
     feat_part,
     sums,
     rate_out,
-    s_turn,
-    u_turn,
     g_turn,
-    mix_turn,
     step_turn,
     in_turn,
     mix_grad,
+    step_flat,
+    in_flat,
+    mix_flat,
     in_terms,
     out_terms,
     held,
     rate_sum,
+    rates,
 ):
     turn_at = pl.program_id(0)
     chunks = pl.num_programs(0)
     chunk = chunks - 1 - turn_at
-    total = pre.shape[0]
-    length = total // SEGMENTS
-    steps = states.shape[0] // SEGMENTS
-    split = lengths[0]
-    zero = jnp.zeros((SEGMENTS, LANES), f32)
-
-    def rated(n):
-        return jnp.broadcast_to(rate[n : n + 1, :], (SEGMENTS, LANES))
-
-    def cut(values):
-        count = values.shape[0] // SEGMENTS
-        return [values[j * SEGMENTS : (j + 1) * SEGMENTS] for j in range(count)]
+    total, channels = pre.shape
+    length = total // LANES
+    steps = states.shape[0]
+    groups = channels // SUB
+    wide = N * SUB
 
     @pl.when(turn_at == 0)
     def _():
-        for seg in range(SEGMENTS):
-            rows = pl.ds(seg * length, length)
-            turned = pl.ds(seg, length, stride=SEGMENTS)
-            step = softplus(step_pre[rows, :])
-            places = row_places(seg * length, length)
-            start = (places == 0) | (places == split)
-            s_turn[turned, :] = jnp.where(start, FAR, step)
-            u_turn[turned, :] = step * silu(pre[rows, :])
-            mix_turn[turned, :] = mix[rows, :]
-            g_turn[turned, :] = grad[rows, :]
-
-        def ahead(i, spent):
-            rows_on = UNROLL * SEGMENTS
-            first_row = total - (i + 1) * rows_on
-            at = pl.ds(pl.multiple_of(first_row, rows_on), rows_on)
-            s, g, bc = [cut(v[at, :]) for v in (s_turn, g_turn, mix_turn)]
+        spread_rates(rate_t, rates)
+        rate_sum[...] = jnp.zeros(rate_sum.shape, f32)
+
+        def turn(tau, carried):
+            g_turn[step_rows(tau), :] = jnp.transpose(grad[turned_rows(tau, length), :])
+            return carried
+
+        lax.fori_loop(0, length, turn, 0)
+
+        def ahead(group, carried):
+            rate = pieces_of(rates[step_rows(group, wide), :], N)
+
+            def some(i, carried):
+                pulled, spent = list(carried[0]), carried[1]
+                for j in range(UNROLL):
+                    tau = length - 1 - (i * UNROLL + j)
+                    at = pl.ds(pl.multiple_of(tau * channels + group * SUB, SUB), SUB)
+                    s, g = s_turn[at, :], g_turn[at, :]
+                    for n in range(N):
+                        row = pl.ds(pl.multiple_of((tau * 2 * N + N + n) * SUB, SUB), SUB)
+                        pulled[n] = jnp.exp2(s * rate[n]) * (pulled[n] + g * mix_turn[row, :])
+                    spent = spent + s
+                return pulled, spent
+
+            zero = jnp.zeros((SUB, LANES), f32)
+            ends, spent = lax.fori_loop(0, length // UNROLL, some, ([zero] * N, zero))
+            inside = jnp.concatenate(over_segments(spent, ends, rate, True), axis=0)
+            held[step_rows(group, wide), :] = inside
+            return carried
+
+        lax.fori_loop(0, groups, ahead, 0)
+
+    in_terms[...] = jnp.zeros(in_terms.shape, f32)
+    out_terms[...] = jnp.zeros(out_terms.shape, f32)
+
+    def retreat(group, carried):
+        ats = [
+            pl.ds(pl.multiple_of((chunk * steps + j) * channels + group * SUB, SUB), SUB)
+            for j in range(steps)
+        ]
+        s, u, g = [[v[at, :] for at in ats] for v in (s_turn, u_turn, g_turn)]
+        step_sum, in_sum = [0.0] * steps, [0.0] * steps
+        for n in range(N):
+            own = pl.ds(pl.multiple_of((group * N + n) * SUB, SUB), SUB)
+            rate, pull, rate_acc = rates[own, :], held[own, :], rate_sum[own, :]
+            first = jnp.where(chunk == 0, enter[own, :], before[0, own, :])
+            state = [first] + [states[j, own, :] for j in range(steps)]
+            for j in reversed(range(steps)):
+                tau = chunk * steps + j
+                b_row = pl.ds(pl.multiple_of((tau * 2 * N + n) * SUB, SUB), SUB)
+                c_row = pl.ds(pl.multiple_of((tau * 2 * N + N + n) * SUB, SUB), SUB)
+                term = pl.ds((j * N + n) * SUB, SUB)
+                grad_state = g[j] * mix_turn[c_row, :] + pull
+                pull = jnp.exp2(s[j] * rate) * grad_state
+                mult = pull * state[j]
+                step_sum[j] = step_sum[j] + mult * rate
+                rate_acc = rate_acc + mult * s[j]
+                in_sum[j] = in_sum[j] + grad_state * mix_turn[b_row, :]
+                in_terms[term, :] += grad_state * u[j]
+                out_terms[term, :] += state[j + 1] * g[j]
+            held[own, :] = pull
+            rate_sum[own, :] = rate_acc
+        for j, at in enumerate(ats):
+            step_turn[at, :] = step_sum[j]
+            in_turn[at, :] = in_sum[j]
+        return carried
+
+    lax.fori_loop(0, groups, retreat, 0)
+    for j in range(steps):
+        rows = []
+        for terms in (in_terms, out_terms):
             for n in range(N):
-                rate_n, pulled = rated(n), held[:, tile(n)]
-                for j in reversed(range(UNROLL)):
-                    pulled = jnp.exp2(s[j] * rate_n) * (pulled + g[j] * lane(bc[j], N + n))
-                held[:, tile(n)] = pulled
-            return spent + sum(s)
-
-        held[...] = jnp.zeros(held.shape, f32)
-        spent = lax.fori_loop(0, length // UNROLL, ahead, zero)
-        last = lax.broadcasted_iota(jnp.int32, (SEGMENTS, LANES), 0) == SEGMENTS - 1
-        for n in range(N):
-            through = jnp.exp2(spent * rated(n))
-            end = held[:, tile(n)]
-            inside = zero
-            for _ in range(SEGMENTS - 1):
-                inside = jnp.where(
-                    last, 0.0, pltpu.roll(end + through * inside, SEGMENTS - 1, 0)
-                )
-            held[:, tile(n)] = inside
-            rate_sum[:, tile(n)] = zero
-
-    base = chunk * steps
-
-    def steps_back(low_step, earlier):
-        rows_on = BACK * SEGMENTS
-        at = pl.ds(pl.multiple_of((base + low_step) * SEGMENTS, rows_on), rows_on)
-        here = pl.ds(pl.multiple_of(low_step * SEGMENTS, rows_on), rows_on)
-        s, u, g, bc = [cut(v[at, :]) for v in (s_turn, u_turn, g_turn, mix_turn)]
-        step_sum, in_sum = [0.0] * BACK, [0.0] * BACK
-        for n in range(N):
-            rate_n, pull, rate_acc = rated(n), held[:, tile(n)], rate_sum[:, tile(n)]
-            state = [earlier(n)] + cut(states[here, tile(n)])
-            parts_in, parts_out = [None] * BACK, [None] * BACK
-            for j in reversed(range(BACK)):
-                grad_state = g[j] * lane(bc[j], N + n) + pull
-                pull = jnp.exp2(s[j] * rate_n) * grad_state
-                mult = pull * state[j]
-                step_sum[j] = step_sum[j] + mult * rate_n
-                rate_acc = rate_acc + mult * s[j]
-                in_sum[j] = in_sum[j] + grad_state * lane(bc[j], n)
-                parts_in[j] = grad_state * u[j]
-                parts_out[j] = state[j + 1] * g[j]
-            in_terms[here, tile(n)] = jnp.concatenate(parts_in, axis=0).astype(bf16)
-            out_terms[here, tile(n)] = jnp.concatenate(parts_out, axis=0).astype(bf16)
-            held[:, tile(n)] = pull
-            rate_sum[:, tile(n)] = rate_acc
-        step_turn[at, :] = jnp.concatenate(step_sum, axis=0)
-        in_turn[at, :] = jnp.concatenate(in_sum, axis=0)
-
-    def inside(i, carried):
-        low_step = steps - BACK * (i + 1)
-        prior = pl.ds(pl.multiple_of((low_step - 1) * SEGMENTS, SEGMENTS), SEGMENTS)
-        steps_back(low_step, lambda n: states[prior, tile(n)])
-        return carried
-
-    def entering(n):
-        return jnp.where(chunk == 0, enter[:, tile(n)], before[:, tile(n)])
-
-    lax.fori_loop(0, steps // BACK - 1, inside, 0)
-    steps_back(0, entering)
-    mix_grad[pl.ds(pl.multiple_of(base * SEGMENTS, SEGMENTS), steps * SEGMENTS), :] = dot(
-        in_terms[...], gather_in[...]
-    ) + dot(out_terms[...], gather_out[...])
+                at = (j * N + n) * SUB
+                rows.append(jnp.sum(terms[at : at + SUB, :], axis=0, keepdims=True))
+        mix_grad[step_rows(chunk * steps + j, 2 * N), :] = jnp.concatenate(rows, axis=0)
 
     @pl.when(turn_at == chunks - 1)
     def _():
+        def turn_back(tau, carried):
+            rows = turned_rows(tau, length)
+            step_flat[rows, :] = jnp.transpose(step_turn[step_rows(tau), :])
+            in_flat[rows, :] = jnp.transpose(in_turn[step_rows(tau), :])
+            mixed = mix_grad[step_rows(tau, 2 * N), :]
+            blank = jnp.zeros((LANES - 2 * N, LANES), f32)
+            mix_flat[rows, :] = jnp.transpose(jnp.concatenate([mixed, blank], axis=0))
+            return carried
+
+        lax.fori_loop(0, length, turn_back, 0)
         sums[...] = jnp.zeros(sums.shape, f32)
-        for seg in range(SEGMENTS):
-            rows = pl.ds(seg * length, length)
-            turned = pl.ds(seg, length, stride=SEGMENTS)
+        across, block_rows = feat_part.shape[2], feat_part.shape[4]
+        for seq in range(2 * feat_part.shape[1]):
+            rows = pl.ds(seq * across * block_rows, across * block_rows)
             ids = ids_ref[rows, :]
             act = silu(pre[rows, :])
             step_in = step_pre[rows, :]
-            state_in = in_turn[turned, :]
+            state_in = in_flat[rows, :]
             grad_here = grad[rows, :]
-            step_grad = step_turn[turned, :] * math.log(2.0) + state_in * act
+            step_grad = step_flat[rows, :] * math.log(2.0) + state_in * act
             pre_grad = step_grad * jax.nn.sigmoid(step_in)
             low = pre_grad.astype(bf16)
             step_grad_low[rows, :] = low
             act_part[rows, :] = grad_here * skip[...] + state_in * softplus(step_in)
-            block_rows = feat_part.shape[4]
-            ours = jnp.where(core[0] == seg % 2, 1, 0)
-            for j in range(length // block_rows):
-                block = seg * (length // block_rows) + j
+            ours = jnp.where(core[0] == seq % 2, 1, 0)
+            for j in range(across):
+                block = seq * across + j
                 block_low = low[j * block_rows : (j + 1) * block_rows]
-                feat_part[ours, seg // 2, j, 0:R, :] = pick(
+                feat_part[ours, seq // 2, j, 0:R, :] = pick(
                     ids_rows[block : block + 1, :],
                     [dot(step_w[m], block_low, 1, 1) for m in range(MODS)],
                 )
-                part = pl.ds(j * block_rows * SEGMENTS + seg, block_rows, stride=SEGMENTS)
-                turned_mix = jnp.transpose(mix_grad[part, :])
-                feat_part[ours, seg // 2, j, R : R + 2 * N, :] = turned_mix[: 2 * N]
+                turned = jnp.transpose(mix_flat[pl.ds(block * block_rows, block_rows), :])
+                feat_part[ours, seq // 2, j, R : R + 2 * N, :] = turned[: 2 * N]
             for m in range(MODS):
                 sums[m : m + 1, :] += jnp.sum(
                     jnp.where(ids == m, pre_grad, 0.0), axis=0, keepdims=True
                 )
             sums[MODS : MODS + 1, :] += jnp.sum(grad_here * act, axis=0, keepdims=True)
-        for n in range(N):
-            rate_out[n : n + 1, :] = jnp.sum(rate_sum[:, tile(n)], axis=0, keepdims=True)
+        lane_at = lax.broadcasted_iota(jnp.int32, (SUB, LANES), 1)
+        for group in range(groups):
+            found = jnp.zeros((SUB, LANES), f32)
+            for n in range(N):
+                at = (group * N + n) * SUB
+                total_rate = jnp.sum(rate_sum[at : at + SUB, :], axis=1, keepdims=True)
+                found = jnp.where(lane_at == n, total_rate, found)
+            rate_out[group * SUB : (group + 1) * SUB, :] = found
 
 
 def scan_back(
-    lengths, core, ids, ids_rows, mix, pre, step_pre, grad, states, enter, step_w, rate, skip
+    core, ids, ids_rows, turned, pre, step_pre, grad, states, enter, step_w, rate_t, skip
 ):
     total, channels = pre.shape
-    steps = math.gcd(total // SEGMENTS, CHUNK)
-    rows = steps * SEGMENTS
-    chunks = total // rows
-    turn = pltpu.VMEM((total, channels), f32)
-    state_lane = jnp.arange(N * channels, dtype=jnp.int32)[:, None] // channels
-    column = jnp.arange(LANES, dtype=jnp.int32)[None, :]
-    gather_in = (state_lane == column).astype(bf16)
-    gather_out = (state_lane + N == column).astype(bf16)
-    across = lax.axis_size("mod")
-    feats = (2, lax.axis_size("z"), across, R + 2 * N, ids_rows.shape[1])
-    first = (ids, ids_rows, mix, pre, step_pre, grad)
-    second = (enter, step_w, rate, skip, gather_in, gather_out)
+    length = total // LANES
+    steps = math.gcd(length, STEPS)
+    chunks = length // steps
+    wide = N * channels
+    feats = (2, lax.axis_size("z"), lax.axis_size("mod"), R + 2 * N, ids_rows.shape[1])
+    first = (ids, ids_rows) + turned + (pre, step_pre, grad)
+    second = (enter, step_w, rate_t, skip)
+    turn = pltpu.VMEM((length * channels, LANES), f32)
+    flat = pltpu.VMEM((total, channels), f32)
+    terms = pltpu.VMEM((steps * N * SUB, LANES), f32)
+    states_row = pltpu.VMEM((wide, LANES), f32)
     return pl.pallas_call(
         back_kernel,
         grid=(chunks,),
-        in_specs=[pl.BlockSpec(memory_space=pltpu.SMEM)] * 2
+        in_specs=[pl.BlockSpec(memory_space=pltpu.SMEM)]
         + [whole(a.shape) for a in first]
         + [
-            pl.BlockSpec((rows, N * channels), lambda i: (chunks - 1 - i, 0)),
+            pl.BlockSpec((steps, wide, LANES), lambda i: (chunks - 1 - i, 0, 0)),
             pl.BlockSpec(
-                (SEGMENTS, N * channels),
-                lambda i: (jnp.maximum((chunks - 1 - i) * steps - 1, 0), 0),
+                (1, wide, LANES), lambda i: (jnp.maximum((chunks - 1 - i) * steps - 1, 0), 0, 0)
             ),
         ]
         + [whole(a.shape) for a in second],
@@ -1072,23 +1119,22 @@
             whole((total, channels)),
             whole((total, channels)),
             whole(feats),
-            whole((SEGMENTS, channels)),
-            whole((N, channels)),
+            whole((SUB, channels)),
+            whole((channels, LANES)),
         ],
         out_shape=[
             jax.ShapeDtypeStruct((total, channels), f32),
             jax.ShapeDtypeStruct((total, channels), bf16),
             jax.ShapeDtypeStruct(feats, f32),
-            jax.ShapeDtypeStruct((SEGMENTS, channels), f32),
-            jax.ShapeDtypeStruct((N, channels), f32),
+            jax.ShapeDtypeStruct((SUB, channels), f32),
+            jax.ShapeDtypeStruct((channels, LANES), f32),
         ],
-        scratch_shapes=[turn] * 7
-        + [pltpu.VMEM((rows, N * channels), bf16)] * 2
-        + [pltpu.VMEM((SEGMENTS, N * channels), f32)] * 2,
+        scratch_shapes=[turn, turn, turn, pltpu.VMEM((length * 2 * N, LANES), f32)]
+        + [flat, flat, flat, terms, terms, states_row, states_row, states_row],
         compiler_params=pltpu.CompilerParams(vmem_limit_bytes=VMEM_BYTES),
         cost_estimate=cost(1),
         name="scan_back",
-    )(lengths, core, *first, states, states, *second)
+    )(core, *first, states, states, *second)
 
 
 def conv_back_kernel(
@@ -1373,7 +1419,7 @@
     taps = conv_weight.astype(f32)
     skip = skip_gain.astype(f32)[None, :]
     decay_rate = -jnp.exp(decay_log.astype(f32))
-    rate = decay_rate * math.log2(math.e)
+    rate_t = jnp.pad((decay_rate * math.log2(math.e)).T, ((0, 0), (0, LANES - N)))
 
     *normed, own_inner, own_gate, inner, conv_pre, act_low, feats = project(
         lengths,
@@ -1398,8 +1444,8 @@
     feats = shared_features(feats)
 
     out_blocks = exchange(held_back(send_out, [feats]), SEQ)
-    states, enter, step_pre, mix, scan_out = scan(
-        lengths, ids, feats, conv_pre, step_weight, step_bias.astype(f32), rate, skip
+    states, enter, step_pre, *turned, scan_out = scan(
+        lengths, ids, feats, conv_pre, step_weight, step_bias.astype(f32), rate_t, skip
     )
     out_blocks, scan_out = lax.optimization_barrier((out_blocks, scan_out))
     own_out, grad_scan, gate_wide, gated_wide, gate_rows, gated_rows = gates(
@@ -1437,21 +1483,19 @@
     grad_out = grad_out.reshape(MODS, seqs * channels, slab).astype(f32)
 
     act_part, step_grad_low, feat_grad, sums, rate_sum = scan_back(
-        lengths,
         place,
         ids,
         ids_rows,
-        mix,
+        tuple(turned),
         conv_pre,
         step_pre,
         grad_scan,
         states,
         enter,
         step_weight,
-        rate,
+        rate_t,
         skip,
     )
-
     feat_grad = held_back(feat_grad, [more_low] + branch.arrived())
     gate_rows = held_back(gate_rows, [feat_grad])
     gate_both = both_cores(gate_rows, ids_ours)
@@ -1519,7 +1563,7 @@
         grad_out,
         tap_sums[:KW],
         tap_sums[KW],
-        rate_sum * decay_rate,
+        rate_sum[:, :N].T * decay_rate,
         sums[MODS],
         sums[:MODS],
     )

time: 821 us -> 817 us (level)
  waiting for transfers between devices: 168 us -> 182 us
  Pallas kernels: 214 us -> 202 us
    all_to_all x2, waiting for transfers between devices: 5.14 us -> 21.2 us  [share(): lax.all_to_all(jnp.broadcast_to(values, (size,) + values.shape), axes, 0, 0)]
    pallas_call x1, Pallas kernels: 74.8 us -> 66.2 us  [scan_back(): pl.pallas_call(back_kernel, grid=(chunks,), in_specs=[pl.BlockSpec(memory...]
    squeeze x18 -> x17, local copies, waits for them, and re-layouts: 27.9 us -> 24.8 us  [taken(): return lax.dynamic_index_in_dim(values, at, dim, keepdims=False)]
    unnamed x179 -> x194, local copies, waits for them, and re-layouts: 24.2 us -> 21.8 us
  transfers between devices with their start and end apart: 61 -> 61, of which waited for: 22 -> 23; matrix products, arithmetic and copies ran while one was open for 24% -> 23% of each run, Pallas kernels for 20% -> 19%
where the time goes in v1:
time: 817 us; the launch traced here: 805 us
  Pallas kernels  202 us (25%)
  waiting for transfers between devices  182 us (22%)
  local copies, waits for them, and re-layouts  96 us (12%)
  other arithmetic  94 us (12%)
  starting transfers between devices  91.9 us (11%)
  matrix products  67.4 us (8%)
  blocking collectives  56.3 us (7%)
  between operations  16.1 us (2%)
    ppermute x52, waiting for transfers between devices, flip(): lax.ppermute(value, axis, [(i, i ^ bit) for i in range(size)])  100 us
    dot_general x17, matrix products, dot(): lax.dot_general(left, right, (((left_dim,), (right_dim,)), ((), ())), pre...  67.4 us
    pallas_call x1, Pallas kernels, scan_back(): pl.pallas_call(back_kernel, grid=(chunks,), in_specs=[pl.BlockSpec(memory...  66.2 us
    all_to_all x6, waiting for transfers between devices, exchange(): return lax.all_to_all(blocks, axes, 0, 0)  60.1 us
    all_to_all x1, blocking collectives, share(): lax.all_to_all(jnp.broadcast_to(values, (size,) + values.shape), axes, 0, 0)  56.3 us
    ppermute x52, starting transfers between devices, flip(): lax.ppermute(value, axis, [(i, i ^ bit) for i in range(size)])  54.5 us
    pallas_call x1, Pallas kernels, scan(): pl.pallas_call(scan_kernel, grid=(length // steps,), in_specs=[pl.BlockSp...  53.4 us
    all_to_all x6, starting transfers between devices, exchange(): return lax.all_to_all(blocks, axes, 0, 0)  29.7 us
  transfers between devices with their start and end apart: 61, of which 23 were waited for; matrix products, arithmetic and copies ran while one was open for 23% of the time, Pallas kernels for 19%

profile of v1, /device:TPU:0, one launch (start us, length us, event | category | flops | bytes accessed | tf_op | source)
XLA Modules:
  0.0 805.3 jit_solution(17531695816328345830)
XLA Ops:
  15.3 6.3 collective-permute-done
  25.9 5.1 collective-permute-done.1
  38.5 6.3 collective-permute-done.2
  49.9 4.6 reshape.1098
  76.6 8.9 %collective-permute-done.8 = bf16[2,2,128,512]{3,2,1,0:T(8,128)(2,1)} collective-permute-done((bf16[2,2,128,512]{3,2,1,0:T(8,128)(2,1)}, bf16[2,2,128,512]{3,2,1,0:T(8,128)(2,1)}, u32[]{:S(2)}, u32[]{:S(2)}) %collective-permute-start.8) | collective-permute-done | bytes 524320 | tf_op jit(solution)/shard_map/ppermute | solution.py:1248
  95.1 8.5 %collective-permute-done.16 = bf16[2,2,128,512]{3,2,1,0:T(8,128)(2,1)S(1)} collective-permute-done((bf16[2,2,128,512]{3,2,1,0:T(8,128)(2,1)S(1)}, bf16[2,2,128,512]{3,2,1,0:T(8,128)(2,1)S(1)}, u32[]{:S(2)}, u32[]{:S(2)}) %collective-permute-start.16) | collective-permute-done | bytes 524320 | tf_op jit(solution)/shard_map/ppermute | solution.py:1248
  106.2 18.6 %collective-permute-done.20 = bf16[2,2,128,512]{3,2,1,0:T(8,128)(2,1)S(1)} collective-permute-done((bf16[2,2,128,512]{3,2,1,0:T(8,128)(2,1)S(1)}, bf16[2,2,128,512]{3,2,1,0:T(8,128)(2,1)S(1)}, u32[]{:S(2)}, u32[]{:S(2)}) %collective-permute-start.20) | collective-permute-done | bytes 524320 | tf_op jit(solution)/shard_map/ppermute | solution.py:1248
  126.0 20.6 %all-to-all-done.refs_18_ = bf16[8,6,272,128]{3,2,1,0:T(8,128)(2,1)S(1)} async-done(((bf16[8,6,272,128]{3,2,1,0:T(8,128)(2,1)}), bf16[8,6,272,128]{3,2,1,0:T(8,128)(2,1)S(1)}, u32[]{:S(2)}, u32[]{:S(2)}) %all-to-all-start) | async-done | bytes 3342368 | tf_op jit(solution)/shard_map/all_to_all | solution.py:1239
  150.2 21.4 %collective-permute-done.17.refs_9_ = bf16[2,2,2,128,512]{4,3,2,1,0:T(8,128)(2,1)} collective-permute-done((bf16[2,2,2,128,512]{4,3,2,1,0:T(8,128)(2,1)}, bf16[2,2,2,128,512]{4,3,2,1,0:T(8,128)(2,1)}, u32[]{:S(2)}, u32[]{:S(2)}) %collective-permute-start.17) | collective-permute-done | bytes 1048608 | tf_op jit(solution)/shard_map/ppermute | solution.py:1248
  177.3 26.4 %project.1 = (bf16[4096,512]{1,0:T(8,128)(2,1)}, bf16[4096,512]{1,0:T(8,128)(2,1)}, bf16[4096,512]{1,0:T(8,128)(2,1)}, bf16[4096,512]{1,0:T(8,128)(2,1)}, bf16[2...) custom-call(s32[2]{0:T(128)} %lengths.5, ...), custom_call_target="tpu_custom_call" | custom-call | bytes 3690000 | tf_op jit(solution)/shard_map/project/pallas_call | solution.py:592
  215.8 14.8 %modal_rows.1.pre = f32[4096,128]{1,0:T(8,128)} custom-call(bf16[4096,512]{1,0:T(8,128)(2,1)} %get-tuple-element.94.refs_0_, bf16[4096,512]{1,0:T(8,128)(2,1)} %get-tuple-element.95.refs_1_, bf16[4096,512]{1,0:T(8,128)(2,1)} %get-tuple-element.96.refs_2_, bf16[4096,512]{1,0:T(8,128)(2,1)} %get-tuple-element.97.refs_3_, s32[4096,1]{1,0:T(8,128)} %copy.134.refs_4_, ...), custom_call_target="tpu_custom_call" | custom-call | bytes 3690000 | tf_op jit(solution)/shard_map/modal_rows/pallas_call | solution.py:635
  230.5 27.8 %all-to-all-done.1 = f32[16,160,128]{2,1,0:T(8,128)S(1)} async-done(((f32[16,160,128]{2,1,0:T(8,128)}), f32[16,160,128]{2,1,0:T(8,128)S(1)}, u32[]{:S(2)}, u32[]{:S(2)}) %all-to-all-start.1) | async-done | bytes 1310752 | tf_op jit(solution)/shard_map/all_to_all | solution.py:1239
  258.6 56.3 %all_to_all.46 = bf16[16,192,128]{2,1,0:T(8,128)(2,1)S(1)} all-to-all(bf16[16,192,128]{2,1,0:T(8,128)(2,1)S(1)} %broadcast_in_dim.129), channel_id=1, replica_groups=mesh['z'=4,'core'=2,'mod'=4] {'z','mod'}, dimensions={0} | all-to-all | bytes 1572864 | tf_op jit(solution)/shard_map/all_to_all | solution.py:1235
  320.1 6.4 all-to-all-start.3
  328.6 53.4 %scan.1 = (f32[32,2048,128]{2,1,0:T(8,128)}, f32[2048,128]{1,0:T(8,128)}, f32[4096,128]{1,0:T(8,128)}, f32[4096,128]{1,0:T(8,128)}, f32[4096,128]{1,0:T(8,128)},...) custom-call(s32[2]{0:T(128)} %lengths.5, s32[4096,1]{1,0:T(8,128)} %copy.132.refs_16_.ids_ref, ...), custom_call_target="tpu_custom_call" | custom-call | bytes 3690000 | tf_op jit(solution)/shard_map/scan/pallas_call | solution.py:903
  383.1 18.3 %gates.1 = (bf16[2048,384]{1,0:T(8,128)(2,1)}, f32[4096,128]{1,0:T(8,128)}, bf16[4096,384]{1,0:T(8,128)(2,1)}, bf16[4096,384]{1,0:T(8,128)(2,1)}, bf16[4096,128]{1,0:T(8,128)(2,1)}, /*index=5*/bf16[4096,128]{1,0:T(8,128)(2,1)}) custom-call(bf16[4096,2048]{1,0:T(8,128)(2,1)} %all-gather.2.cloned.1.call-done.cot, s32[4096,1]{1,0:T(8,128)} %copy.132.refs_16_.ids_ref, ...), custom_call_target="tpu_custom_call" | custom-call | bytes 3690000 | tf_op jit(solution)/shard_map/gates/pallas_call | solution.py:700
  401.4 5.7 fusion.62
  424.3 13.4 %convolution_convert_fusion.6 = bf16[2048,384]{1,0:T(8,128)(2,1)} fusion(bf16[4096,2048]{1,0:T(8,128)(2,1)} %all-gather.2.cloned.1.call-done.cot, bf16[4096,384]{1,0:T(8,128)(2,1)S(1)} %copy-done.82), kind=kOutput, calls=%fused_computation.17 | convolution fusion | flops 6443237376 | bytes 21495808 | tf_op jit(solution)/shard_map/dot_general | solution.py:479
  441.3 5.1 all-to-all-start.4
  468.7 66.2 %scan_back.1 = (f32[4096,128]{1,0:T(8,128)}, bf16[4096,128]{1,0:T(8,128)(2,1)}, f32[2,4,4,160,128]{4,3,2,1,0:T(8,128)}, f32[8,128]{1,0:T(8,128)}, f32[128,128]{1,0:T(8,128)}) custom-call(s32[3]{0:T(128)} %pad_add_fusion.place.core, s32[4096,1]{1,0:T(8,128)} %copy.132.refs_16_.ids_ref, s32[32,128]{1,0:T(8,128)} %reshape.1102.refs_17_.ids_rows, ...), custom_call_target="tpu_custom_call" | custom-call | bytes 3690000 | tf_op jit(solution)/shard_map/scan_back/pallas_call | solution.py:1106
  542.1 6.2 all-to-all-start.5
  554.2 11.8 %all-to-all-done.5 = bf16[16,160,128]{2,1,0:T(8,128)(2,1)} async-done(((bf16[16,160,128]{2,1,0:T(8,128)(2,1)}), bf16[16,160,128]{2,1,0:T(8,128)(2,1)}, u32[]{:S(2)}, u32[]{:S(2)}) %all-to-all-start.5) | async-done | bytes 655392 | tf_op jit(solution)/shard_map/all_to_all | solution.py:1239
  567.2 6.0 side_by_side.3
  574.1 4.5 all-to-all-start.6
  587.1 8.1 %all-to-all-done.6 = bf16[16,160,128]{2,1,0:T(8,128)(2,1)} async-done(((bf16[16,160,128]{2,1,0:T(8,128)(2,1)}), bf16[16,160,128]{2,1,0:T(8,128)(2,1)}, u32[]{:S(2)}, u32[]{:S(2)}) %all-to-all-start.6) | async-done | bytes 655392 | tf_op jit(solution)/shard_map/all_to_all | solution.py:1235
  605.2 12.5 %conv_back.1 = (bf16[4096,384]{1,0:T(8,128)(2,1)}, bf16[4096,128]{1,0:T(8,128)(2,1)}, f32[8,128]{1,0:T(8,128)}) custom-call(s32[2]{0:T(128)} %lengths.5, s32[4096,1]{1,0:T(8,128)} %copy.132.refs_16_.ids_ref, bf16[2,4,4,160,128]{4,3,2,1,0:T(8,128)(2,1)} %maximum_select_fusion.1.feat_grad, f32[4096,128]{1,0:T(8,128)} %get-tuple-element.130.act_part, ...), custom_call_target="tpu_custom_call" | custom-call | bytes 3690000 | tf_op jit(solution)/shard_map/conv_back/pallas_call | solution.py:1200
  671.6 4.3 all-to-all-start.7
  736.4 4.3 fusion
  740.7 4.7 copy.160
  750.3 13.1 %all-to-all-done.8 = f32[32,1,2048]{2,1,0:T(1,128)S(1)} async-done(((f32[32,1,2048]{2,1,0:T(1,128)}), f32[32,1,2048]{2,1,0:T(1,128)S(1)}, u32[]{:S(2)}, u32[]{:S(2)}) %all-to-all-start.8) | async-done | bytes 262176 | tf_op jit(solution)/shard_map/all_to_all | solution.py:1235
  772.8 10.3 %copy.163 = f32[3,256,2,1024]{3,2,1,0:T(2,128)} copy(f32[3,256,2,1024]{1,3,0,2:T(8,128)} %maximum_convert_fusion) | data formatting | bytes 12582912
  783.1 4.3 collective-permute-done.51
  (455 shorter events, 305.3 us)
Async XLA Ops:
  67.3 79.3 %all-to-all-start = ((bf16[8,6,272,128]{3,2,1,0:T(8,128)(2,1)}), bf16[8,6,272,128]{3,2,1,0:T(8,128)(2,1)S(1)}, u32[]{:S(2)}, u32[]{:S(2)}) async-start(bf16[8,6,272,128]{3,2,1,0:T(8,128)(2,1)} %pad_maximum_fusion), calls=%async_computation | async-start | bytes 6684672 | tf_op jit(solution)/shard_map/all_to_all | solution.py:1239
  70.9 311.1 %all-gather.2.cloned.1.call-start = ((), (), s32[]{:S(2)}) async-start(), calls=%async_computation.9 | async-start | bytes 17301504 | tf_op jit(solution)/shard_map/all_gather | solution.py:1435
  87.8 58.8 %collective-permute-start.10 = (bf16[2,2,2,128,512]{4,3,2,1,0:T(8,128)(2,1)}, bf16[2,2,2,128,512]{4,3,2,1,0:T(8,128)(2,1)}, u32[]{:S(2)}, u32[]{:S(2)}) collective-permute-start(bf16[2,2,2,128,512]{4,3,2,1,0:T(8,128)(2,1)} %maximum_select_fusion.2.refs_0_), channel_id=1, source_target_pairs={{0,4},{4,0},{1,5},{5,1},{2,6},{6,2},{3,7},{7,3},{8,12},{12,8},{9,1... | collective-permute-start | bytes 3145736 | tf_op jit(solution)/shard_map/ppermute | solution.py:1248
  87.8 60.3 %collective-permute-start.9 = (bf16[2,2,2,128,512]{4,3,2,1,0:T(8,128)(2,1)}, bf16[2,2,2,128,512]{4,3,2,1,0:T(8,128)(2,1)}, u32[]{:S(2)}, u32[]{:S(2)}) collective-permute-start(bf16[2,2,2,128,512]{4,3,2,1,0:T(8,128)(2,1)} %maximum_select_fusion.2.refs_0_), channel_id=1, source_target_pairs={{0,2},{1,3},{2,0},{3,1},{4,6},{5,7},{6,4},{7,5},{8,10},{9,11},{10,... | collective-permute-start | bytes 3145736 | tf_op jit(solution)/shard_map/ppermute | solution.py:1248
  92.1 32.7 %collective-permute-start.20 = (bf16[2,2,128,512]{3,2,1,0:T(8,128)(2,1)S(1)}, bf16[2,2,128,512]{3,2,1,0:T(8,128)(2,1)S(1)}, u32[]{:S(2)}, u32[]{:S(2)}) collective-permute-start(bf16[2,2,128,512]{3,2,1,0:T(8,128)(2,1)S(1)} %copy-done.70), channel_id=1, source_target_pairs={{0,2},{1,3},{2,0},{3,1},{4,6},{5,7},{6,4},{7,5},{8,10},{9,11},{10,... | collective-permute-start | bytes 1572872 | tf_op jit(solution)/shard_map/ppermute | solution.py:1248
  95.0 54.7 %collective-permute-start.14 = (bf16[2,2,2,128,512]{4,3,2,1,0:T(8,128)(2,1)}, bf16[2,2,2,128,512]{4,3,2,1,0:T(8,128)(2,1)}, u32[]{:S(2)}, u32[]{:S(2)}) collective-permute-start(bf16[2,2,2,128,512]{4,3,2,1,0:T(8,128)(2,1)} %maximum_select_fusion.3.refs_4_), channel_id=1, source_target_pairs={{0,4},{4,0},{1,5},{5,1},{2,6},{6,2},{3,7},{7,3},{8,12},{12,8},{9,1... | collective-permute-start | bytes 3145736 | tf_op jit(solution)/shard_map/ppermute | solution.py:1248
  103.6 46.1 %collective-permute-start.13 = (bf16[2,2,2,128,512]{4,3,2,1,0:T(8,128)(2,1)}, bf16[2,2,2,128,512]{4,3,2,1,0:T(8,128)(2,1)}, u32[]{:S(2)}, u32[]{:S(2)}) collective-permute-start(bf16[2,2,2,128,512]{4,3,2,1,0:T(8,128)(2,1)} %maximum_select_fusion.3.refs_4_), channel_id=1, source_target_pairs={{0,1},{1,0},{2,3},{3,2},{4,5},{5,4},{6,7},{7,6},{8,9},{9,8},{10,11... | collective-permute-start | bytes 3145736 | tf_op jit(solution)/shard_map/ppermute | solution.py:1248
  149.6 27.6 %collective-permute-start.22 = (bf16[2,2,2,128,512]{4,3,2,1,0:T(8,128)(2,1)}, bf16[2,2,2,128,512]{4,3,2,1,0:T(8,128)(2,1)}, u32[]{:S(2)}, u32[]{:S(2)}) collective-permute-start(bf16[2,2,2,128,512]{4,3,2,1,0:T(8,128)(2,1)} %maximum_select_fusion.5.refs_12_), channel_id=1, source_target_pairs={{0,4},{4,0},{1,5},{5,1},{2,6},{6,2},{3,7},{7,3},{8,12},{12,8},{9,1... | collective-permute-start | bytes 3145736 | tf_op jit(solution)/shard_map/ppermute | solution.py:1248
  149.6 27.6 %collective-permute-start.11 = (bf16[2,2,2,128,512]{4,3,2,1,0:T(8,128)(2,1)}, bf16[2,2,2,128,512]{4,3,2,1,0:T(8,128)(2,1)}, u32[]{:S(2)}, u32[]{:S(2)}) collective-permute-start(bf16[2,2,2,128,512]{4,3,2,1,0:T(8,128)(2,1)} %collective-permute-done.9.refs_1_), channel_id=1, source_target_pairs={{0,4},{4,0},{1,5},{5,1},{2,6},{6,2},{3,7},{7,3},{8,12},{12,8},{9,1... | collective-permute-start | bytes 3145736 | tf_op jit(solution)/shard_map/ppermute | solution.py:1248
  150.1 27.1 %collective-permute-start.15 = (bf16[2,2,2,128,512]{4,3,2,1,0:T(8,128)(2,1)}, bf16[2,2,2,128,512]{4,3,2,1,0:T(8,128)(2,1)}, u32[]{:S(2)}, u32[]{:S(2)}) collective-permute-start(bf16[2,2,2,128,512]{4,3,2,1,0:T(8,128)(2,1)} %collective-permute-done.13.refs_5_), channel_id=1, source_target_pairs={{0,4},{4,0},{1,5},{5,1},{2,6},{6,2},{3,7},{7,3},{8,12},{12,8},{9,1... | collective-permute-start | bytes 3145736 | tf_op jit(solution)/shard_map/ppermute | solution.py:1248
  209.7 48.6 %all-to-all-start.1 = ((f32[16,160,128]{2,1,0:T(8,128)}), f32[16,160,128]{2,1,0:T(8,128)S(1)}, u32[]{:S(2)}, u32[]{:S(2)}) async-start(f32[16,160,128]{2,1,0:T(8,128)} %bitcast.44), calls=%async_computation.1 | async-start | bytes 2621440 | tf_op jit(solution)/shard_map/all_to_all | solution.py:1239
  320.1 61.8 %all-to-all-start.3 = ((bf16[8,3,256,128]{3,2,1,0:T(8,128)(2,1)}), bf16[8,3,256,128]{3,2,1,0:T(8,128)(2,1)S(1)}, u32[]{:S(2)}, u32[]{:S(2)}) async-start(bf16[8,3,256,128]{3,2,1,0:T(8,128)(2,1)} %bitcast.41), calls=%async_computation.3 | async-start | bytes 3145728 | tf_op jit(solution)/shard_map/all_to_all | solution.py:1239
  441.3 93.6 %all-to-all-start.4 = ((bf16[8,256,768]{1,2,0:T(8,128)(2,1)}), bf16[8,256,768]{1,2,0:T(8,128)(2,1)S(1)}, u32[]{:S(2)}, u32[]{:S(2)}) async-start(bf16[8,256,768]{1,2,0:T(8,128)(2,1)} %pad_maximum_fusion.1), calls=%async_computation.4 | async-start | bytes 6291456 | tf_op jit(solution)/shard_map/all_to_all | solution.py:1239
  458.8 76.1 %collective-permute-start.28 = (bf16[2,2,2,128,1024]{4,3,1,0,2:T(8,128)(2,1)}, bf16[2,2,2,128,1024]{4,3,1,0,2:T(8,128)(2,1)}, u32[]{:S(2)}, u32[]{:S(2)}) collective-permute-start(bf16[2,2,2,128,1024]{4,3,1,0,2:T(8,128)(2,1)} %copy_bitcast_fusion.1), channel_id=1, source_target_pairs={{0,1},{1,0},{2,3},{3,2},{4,5},{5,4},{6,7},{7,6},{8,9},{9,8},{10,11... | collective-permute-start | bytes 6291464 | tf_op jit(solution)/shard_map/ppermute | solution.py:1248
  468.0 66.9 %collective-permute-start.29 = (bf16[2,2,2,128,1024]{4,3,1,0,2:T(8,128)(2,1)}, bf16[2,2,2,128,1024]{4,3,1,0,2:T(8,128)(2,1)}, u32[]{:S(2)}, u32[]{:S(2)}) collective-permute-start(bf16[2,2,2,128,1024]{4,3,1,0,2:T(8,128)(2,1)} %copy_bitcast_fusion), channel_id=1, source_target_pairs={{0,2},{1,3},{2,0},{3,1},{4,6},{5,7},{6,4},{7,5},{8,10},{9,11},{10,... | collective-permute-start | bytes 6291464 | tf_op jit(solution)/shard_map/ppermute | solution.py:1248
  541.6 25.6 %collective-permute-start.33 = (bf16[2048,384]{1,0:T(8,128)(2,1)}, bf16[2048,384]{1,0:T(8,128)(2,1)}, u32[]{:S(2)}, u32[]{:S(2)}) collective-permute-start(bf16[2048,384]{1,0:T(8,128)(2,1)} %get-tuple-element.126.refs_5_.refs_2_), channel_id=1, source_target_pairs={{0,4},{4,0},{1,5},{5,1},{2,6},{6,2},{3,7},{7,3},{8,12},{12,8},{9,1... | collective-permute-start | bytes 4718600 | tf_op jit(solution)/shard_map/ppermute | solution.py:1248
  580.2 37.5 %collective-permute-start.35 = (bf16[2,2,128,1024]{3,2,1,0:T(8,128)(2,1)}, bf16[2,2,128,1024]{3,2,1,0:T(8,128)(2,1)}, u32[]{:S(2)}, u32[]{:S(2)}) collective-permute-start(bf16[2,2,128,1024]{3,2,1,0:T(8,128)(2,1)} %fusion.6), channel_id=1, source_target_pairs={{0,1},{1,0},{2,3},{3,2},{4,5},{5,4},{6,7},{7,6},{8,9},{9,8},{10,11... | collective-permute-start | bytes 3145736 | tf_op jit(solution)/shard_map/ppermute | solution.py:1248
  582.6 37.5 %collective-permute-start.30 = (bf16[2,2,128,1024]{3,2,1,0:T(8,128)(2,1)}, bf16[2,2,128,1024]{3,2,1,0:T(8,128)(2,1)}, u32[]{:S(2)}, u32[]{:S(2)}) collective-permute-start(bf16[2,2,128,1024]{3,2,1,0:T(8,128)(2,1)} %fusion.7), channel_id=1, source_target_pairs={{0,2},{1,3},{2,0},{3,1},{4,6},{5,7},{6,4},{7,5},{8,10},{9,11},{10,... | collective-permute-start | bytes 3145736 | tf_op jit(solution)/shard_map/ppermute | solution.py:1248
  645.8 37.0 %collective-permute-start.47 = (bf16[2,2,2,128,512]{4,3,1,0,2:T(8,128)(2,1)}, bf16[2,2,2,128,512]{4,3,1,0,2:T(8,128)(2,1)}, u32[]{:S(2)}, u32[]{:S(2)}) collective-permute-start(bf16[2,2,2,128,512]{4,3,1,0,2:T(8,128)(2,1)} %copy_bitcast_fusion.2), channel_id=1, source_target_pairs={{0,2},{1,3},{2,0},{3,1},{4,6},{5,7},{6,4},{7,5},{8,10},{9,11},{10,... | collective-permute-start | bytes 3145736 | tf_op jit(solution)/shard_map/ppermute | solution.py:1248
  648.2 37.3 %collective-permute-start.46 = (bf16[2,2,2,128,512]{4,3,1,0,2:T(8,128)(2,1)}, bf16[2,2,2,128,512]{4,3,1,0,2:T(8,128)(2,1)}, u32[]{:S(2)}, u32[]{:S(2)}) collective-permute-start(bf16[2,2,2,128,512]{4,3,1,0,2:T(8,128)(2,1)} %copy_bitcast_fusion.3), channel_id=1, source_target_pairs={{0,1},{1,0},{2,3},{3,2},{4,5},{5,4},{6,7},{7,6},{8,9},{9,8},{10,11... | collective-permute-start | bytes 3145736 | tf_op jit(solution)/shard_map/ppermute | solution.py:1248
  658.0 39.0 %collective-permute-start.40 = (bf16[2,2,2,128,512]{4,3,1,0,2:T(8,128)(2,1)}, bf16[2,2,2,128,512]{4,3,1,0,2:T(8,128)(2,1)}, u32[]{:S(2)}, u32[]{:S(2)}) collective-permute-start(bf16[2,2,2,128,512]{4,3,1,0,2:T(8,128)(2,1)} %copy_bitcast_fusion.5), channel_id=1, source_target_pairs={{0,1},{1,0},{2,3},{3,2},{4,5},{5,4},{6,7},{7,6},{8,9},{9,8},{10,11... | collective-permute-start | bytes 3145736 | tf_op jit(solution)/shard_map/ppermute | solution.py:1248
  659.6 41.0 %collective-permute-start.41 = (bf16[2,2,2,128,512]{4,3,1,0,2:T(8,128)(2,1)}, bf16[2,2,2,128,512]{4,3,1,0,2:T(8,128)(2,1)}, u32[]{:S(2)}, u32[]{:S(2)}) collective-permute-start(bf16[2,2,2,128,512]{4,3,1,0,2:T(8,128)(2,1)} %copy_bitcast_fusion.4), channel_id=1, source_target_pairs={{0,2},{1,3},{2,0},{3,1},{4,6},{5,7},{6,4},{7,5},{8,10},{9,11},{10,... | collective-permute-start | bytes 3145736 | tf_op jit(solution)/shard_map/ppermute | solution.py:1248
  661.8 28.5 %collective-permute-start.38 = (bf16[2,128,2048]{2,1,0:T(8,128)(2,1)}, bf16[2,128,2048]{2,1,0:T(8,128)(2,1)}, u32[]{:S(2)}, u32[]{:S(2)}) collective-permute-start(bf16[2,128,2048]{2,1,0:T(8,128)(2,1)} %fusion.25), channel_id=1, source_target_pairs={{0,8},{8,0},{16,24},{24,16},{1,9},{9,1},{17,25},{25,17},{2,10},{10... | collective-permute-start | bytes 3145736 | tf_op jit(solution)/shard_map/ppermute | solution.py:1248
  671.6 60.8 %all-to-all-start.7 = ((bf16[8,256,384]{1,2,0:T(8,128)(2,1)}), bf16[8,256,384]{1,2,0:T(8,128)(2,1)}, u32[]{:S(2)}, u32[]{:S(2)}) async-start(bf16[8,256,384]{1,2,0:T(8,128)(2,1)} %copy.152), calls=%async_computation.7 | async-start | bytes 3145728 | tf_op jit(solution)/shard_map/all_to_all | solution.py:1239
  684.9 38.7 %collective-permute-start.49 = (bf16[2,2,128,512]{3,2,1,0:T(8,128)(2,1)}, bf16[2,2,128,512]{3,2,1,0:T(8,128)(2,1)}, u32[]{:S(2)}, u32[]{:S(2)}) collective-permute-start(bf16[2,2,128,512]{3,2,1,0:T(8,128)(2,1)} %fusion.28), channel_id=1, source_target_pairs={{0,1},{1,0},{2,3},{3,2},{4,5},{5,4},{6,7},{7,6},{8,9},{9,8},{10,11... | collective-permute-start | bytes 1572872 | tf_op jit(solution)/shard_map/ppermute | solution.py:1248
  687.6 34.7 %collective-permute-start.48 = (bf16[2,2,128,512]{3,2,1,0:T(8,128)(2,1)}, bf16[2,2,128,512]{3,2,1,0:T(8,128)(2,1)}, u32[]{:S(2)}, u32[]{:S(2)}) collective-permute-start(bf16[2,2,128,512]{3,2,1,0:T(8,128)(2,1)} %fusion.29), channel_id=1, source_target_pairs={{0,2},{1,3},{2,0},{3,1},{4,6},{5,7},{6,4},{7,5},{8,10},{9,11},{10,... | collective-permute-start | bytes 1572872 | tf_op jit(solution)/shard_map/ppermute | solution.py:1248
  692.7 102.0 %collective-permute-start.39 = (bf16[128,2048]{1,0:T(8,128)(2,1)}, bf16[128,2048]{1,0:T(8,128)(2,1)}, u32[]{:S(2)}, u32[]{:S(2)}) collective-permute-start(bf16[128,2048]{1,0:T(8,128)(2,1)} %fusion.32), channel_id=1, source_target_pairs={{0,16},{8,24},{16,0},{24,8},{1,17},{9,25},{17,1},{25,9},{2,18},{10... | collective-permute-start | bytes 1572872 | tf_op jit(solution)/shard_map/ppermute | solution.py:1248
  699.0 30.0 %collective-permute-start.42 = (bf16[2,2,128,512]{3,2,1,0:T(8,128)(2,1)}, bf16[2,2,128,512]{3,2,1,0:T(8,128)(2,1)}, u32[]{:S(2)}, u32[]{:S(2)}) collective-permute-start(bf16[2,2,128,512]{3,2,1,0:T(8,128)(2,1)} %fusion.31), channel_id=1, source_target_pairs={{0,2},{1,3},{2,0},{3,1},{4,6},{5,7},{6,4},{7,5},{8,10},{9,11},{10,... | collective-permute-start | bytes 1572872 | tf_op jit(solution)/shard_map/ppermute | solution.py:1248
  702.7 27.3 %collective-permute-start.43 = (bf16[2,2,128,512]{3,2,1,0:T(8,128)(2,1)}, bf16[2,2,128,512]{3,2,1,0:T(8,128)(2,1)}, u32[]{:S(2)}, u32[]{:S(2)}) collective-permute-start(bf16[2,2,128,512]{3,2,1,0:T(8,128)(2,1)} %fusion.30), channel_id=1, source_target_pairs={{0,1},{1,0},{2,3},{3,2},{4,5},{5,4},{6,7},{7,6},{8,9},{9,8},{10,11... | collective-permute-start | bytes 1572872 | tf_op jit(solution)/shard_map/ppermute | solution.py:1248
  726.0 38.2 %collective-permute-start.50 = (bf16[2,128,1024]{2,1,0:T(8,128)(2,1)}, bf16[2,128,1024]{2,1,0:T(8,128)(2,1)}, u32[]{:S(2)}, u32[]{:S(2)}) collective-permute-start(bf16[2,128,1024]{2,1,0:T(8,128)(2,1)} %fusion.35), channel_id=1, source_target_pairs={{0,8},{8,0},{16,24},{24,16},{1,9},{9,1},{17,25},{25,17},{2,10},{10... | collective-permute-start | bytes 1572872 | tf_op jit(solution)/shard_map/ppermute | solution.py:1248
  732.4 31.8 %collective-permute-start.44 = (bf16[2,128,1024]{2,1,0:T(8,128)(2,1)}, bf16[2,128,1024]{2,1,0:T(8,128)(2,1)}, u32[]{:S(2)}, u32[]{:S(2)}) collective-permute-start(bf16[2,128,1024]{2,1,0:T(8,128)(2,1)} %fusion.34), channel_id=1, source_target_pairs={{0,8},{8,0},{16,24},{24,16},{1,9},{9,1},{17,25},{25,17},{2,10},{10... | collective-permute-start | bytes 1572872 | tf_op jit(solution)/shard_map/ppermute | solution.py:1248
  733.2 30.2 %all-to-all-start.8 = ((f32[32,1,2048]{2,1,0:T(1,128)}), f32[32,1,2048]{2,1,0:T(1,128)S(1)}, u32[]{:S(2)}, u32[]{:S(2)}) async-start(f32[32,1,2048]{2,1,0:T(1,128)} %broadcast_in_dim.135), calls=%async_computation.8 | async-start | bytes 524288 | tf_op jit(solution)/shard_map/all_to_all | solution.py:1235
  (116 other events, 1428.4 us)
Sparse Core Ops, SparseCore 0:
  203.8 165.9 all-gather.1

commit v2 on v1

--- a/solution.py
+++ b/solution.py
@@ -500,6 +500,12 @@
     return pick(ids, [wide[:, m * channels : (m + 1) * channels] for m in range(MODS)])
 
 
+def modal_rows_of(weight, values, ids_row):
+    stacked = dot(weight, values, 1, 1)
+    height = stacked.shape[0] // MODS
+    return pick(ids_row, [stacked[m * height : (m + 1) * height] for m in range(MODS)])
+
+
 def put_masked(ref, rows, ids, values):
     channels = values.shape[1]
     for m in range(MODS):
@@ -510,11 +516,11 @@
 
 def arrange(blocks, first, out):
     slab = out.shape[0] // blocks.shape[0]
-    channels = blocks.shape[3]
+    channels = blocks.shape[2]
     for at in range(blocks.shape[0]):
         for m in range(MODS):
             out[at * slab : (at + 1) * slab, m * channels : (m + 1) * channels] = blocks[
-                at, first + m, 0:slab, :
+                at, (first + m) * slab : (first + m + 1) * slab, :
             ]
 
 
@@ -574,9 +580,8 @@
     ours = jnp.where(place[0] == step % 2, 1, 0)
     for j in range(across):
         block = low[j * block_rows : (j + 1) * block_rows]
-        feats[ours, step // 2, j] = pick(
-            ids_rows[pl.ds(step * across + j, 1), :],
-            [dot(param_t[m], block, 1, 1) for m in range(MODS)],
+        feats[ours, step // 2, j] = modal_rows_of(
+            param_t[...], block, ids_rows[pl.ds(step * across + j, 1), :]
         )
 
 
@@ -587,7 +592,7 @@
     rows = total // (2 * chips)
     width = pieces[0].shape[4]
     by_rows = lambda i: (i, 0)
-    feats = (2, chips, across, param_t.shape[1], rows // across)
+    feats = (2, chips, across, param_t.shape[0] // MODS, rows // across)
     smem = pl.BlockSpec(memory_space=pltpu.SMEM)
     return pl.pallas_call(
         project_kernel,
@@ -730,6 +735,11 @@
             out[at : at + SUB, :] = jnp.broadcast_to(rows[:, n : n + 1], (SUB, LANES))
 
 
+def spread_mix(mixed, out, tau):
+    spread = [jnp.broadcast_to(mixed[n : n + 1, :], (SUB, LANES)) for n in range(2 * N)]
+    out[step_rows(tau, 2 * N * SUB), :] = jnp.concatenate(spread, axis=0)
+
+
 def turned_rows(tau, length):
     return pl.ds(tau, LANES, stride=length)
 
@@ -747,12 +757,21 @@
         inside = at < LANES - reach if backward else at >= reach
         for n in range(N):
             earlier = jnp.where(inside, pltpu.roll(ends[n], shift, 1), 0.0)
-            ends[n] = ends[n] + jnp.exp2(spent * rates[n]) * earlier
+            ends[n] = ends[n] + jnp.exp(spent * rates[n]) * earlier
         spent = spent + jnp.where(inside, pltpu.roll(spent, shift, 1), 0.0)
         reach *= 2
     shift = LANES - 1 if backward else 1
     inside = at < LANES - 1 if backward else at >= 1
     return [jnp.where(inside, pltpu.roll(end, shift, 1), 0.0) for end in ends]
+
+
+def row_of(at):
+    return slice(at * SUB, (at + 1) * SUB)
+
+
+def group_view(ref, first, count, group):
+    start = pl.multiple_of(first * (count * LANES) + group * SUB, SUB)
+    return ref.at[pl.ds(start, (count - 1) * LANES + SUB)]
 
 
 def pieces_of(values, count):
@@ -773,7 +792,7 @@
     step_pre,
     s_turn,
     u_turn,
-    mix_turn,
+    mix_rows,
     scan_out,
     s_flat,
     u_flat,
@@ -781,6 +800,7 @@
     y_turn,
     held,
     rates,
+    mix_turn,
 ):
     chunk = pl.program_id(0)
     total, channels = pre.shape
@@ -801,8 +821,9 @@
                 block = pl.ds(first, block_rows)
                 block_ids = ids_ref[block, :]
                 low = feats[seq % 2, seq // 2, j, 0:R, :]
-                here = pick(block_ids, [dot(low, step_w[m], 0, 0) for m in range(MODS)]) + pick(
-                    block_ids, [step_b[m : m + 1, :] for m in range(MODS)]
+                stacked = dot(low, step_w[...], 0, 0) + step_b[...]
+                here = pick(
+                    block_ids, [stacked[:, m * channels : (m + 1) * channels] for m in range(MODS)]
                 )
                 step_pre[block, :] = here
                 step = softplus(here)
@@ -819,9 +840,9 @@
             rows = turned_rows(tau, length)
             s_turn[step_rows(tau), :] = jnp.transpose(s_flat[rows, :])
             u_turn[step_rows(tau), :] = jnp.transpose(u_flat[rows, :])
-            mixed = jnp.transpose(mix_flat[rows, :])
-            spread = [jnp.broadcast_to(mixed[n : n + 1, :], (SUB, LANES)) for n in range(2 * N)]
-            mix_turn[step_rows(tau, 2 * wide), :] = jnp.concatenate(spread, axis=0)
+            mixed = jnp.transpose(mix_flat[rows, :])[: 2 * N]
+            mix_rows[step_rows(tau, 2 * N), :] = mixed
+            spread_mix(mixed, mix_turn, tau)
             return carried
 
         lax.fori_loop(0, length, turn, 0)
@@ -831,13 +852,13 @@
 
             def some(i, carried):
                 hidden, spent = list(carried[0]), carried[1]
+                s_here, u_here = [group_view(v, i, UNROLL, group) for v in (s_turn, u_turn)]
+                mix_here = mix_turn.at[step_rows(i, UNROLL * 2 * wide)]
                 for j in range(UNROLL):
-                    tau = i * UNROLL + j
-                    at = pl.ds(pl.multiple_of(tau * channels + group * SUB, SUB), SUB)
-                    s, u = s_turn[at, :], u_turn[at, :]
+                    s, u = s_here[row_of(j * groups), :], u_here[row_of(j * groups), :]
                     for n in range(N):
-                        row = pl.ds(pl.multiple_of((tau * 2 * N + n) * SUB, SUB), SUB)
-                        hidden[n] = jnp.exp2(s * rate[n]) * hidden[n] + u * mix_turn[row, :]
+                        b = mix_here[row_of(j * 2 * N + n), :]
+                        hidden[n] = jnp.exp(s * rate[n]) * hidden[n] + u * b
                     spent = spent + s
                 return hidden, spent
 
@@ -854,20 +875,22 @@
         own = step_rows(group, wide)
         rate = pieces_of(rates[own, :], N)
         hidden = pieces_of(held[own, :], N)
+        s_here, u_here, y_here = [
+            group_view(v, chunk, steps, group) for v in (s_turn, u_turn, y_turn)
+        ]
+        mix_here = mix_turn.at[step_rows(chunk, steps * 2 * wide)]
         for j in range(steps):
-            tau = chunk * steps + j
-            at = pl.ds(pl.multiple_of(tau * channels + group * SUB, SUB), SUB)
-            s, u = s_turn[at, :], u_turn[at, :]
+            s, u = s_here[row_of(j * groups), :], u_here[row_of(j * groups), :]
+            out = states.at[j, own]
             terms = []
             for n in range(N):
-                row = pl.ds(pl.multiple_of((tau * 2 * N + n) * SUB, SUB), SUB)
-                other = pl.ds(pl.multiple_of((tau * 2 * N + N + n) * SUB, SUB), SUB)
-                hidden[n] = jnp.exp2(s * rate[n]) * hidden[n] + u * mix_turn[row, :]
-                states[j, pl.ds(pl.multiple_of((group * N + n) * SUB, SUB), SUB), :] = hidden[n]
-                terms.append(hidden[n] * mix_turn[other, :])
+                b = mix_here[row_of(j * 2 * N + n), :]
+                hidden[n] = jnp.exp(s * rate[n]) * hidden[n] + u * b
+                out[row_of(n), :] = hidden[n]
+                terms.append(hidden[n] * mix_here[row_of(j * 2 * N + N + n), :])
             while len(terms) > 1:
                 terms = [a + b for a, b in zip(terms[::2], terms[1::2])]
-            y_turn[at, :] = terms[0]
+            y_here[row_of(j * groups), :] = terms[0]
         held[own, :] = jnp.concatenate(hidden, axis=0)
         return carried
 
@@ -897,7 +920,7 @@
         (total, channels),
         (length * channels, LANES),
         (length * channels, LANES),
-        (length * 2 * N * SUB, LANES),
+        (length * 2 * N, LANES),
         (total, channels),
     ]
     return pl.pallas_call(
@@ -909,7 +932,8 @@
         out_shape=[jax.ShapeDtypeStruct((length, wide, LANES), f32)]
         + [jax.ShapeDtypeStruct(shape, f32) for shape in shapes],
         scratch_shapes=[flat, flat, flat, pltpu.VMEM((length * channels, LANES), f32)]
-        + [pltpu.VMEM((wide, LANES), f32)] * 2,
+        + [pltpu.VMEM((wide, LANES), f32)] * 2
+        + [pltpu.VMEM((length * 2 * N * SUB, LANES), f32)],
         compiler_params=pltpu.CompilerParams(vmem_limit_bytes=VMEM_BYTES),
         cost_estimate=cost(1),
         name="scan",
@@ -922,7 +946,7 @@
     ids_rows,
     s_turn,
     u_turn,
-    mix_turn,
+    mix_rows,
     pre,
     step_pre,
     grad,
@@ -949,6 +973,7 @@
     held,
     rate_sum,
     rates,
+    mix_turn,
 ):
     turn_at = pl.program_id(0)
     chunks = pl.num_programs(0)
@@ -966,6 +991,7 @@
 
         def turn(tau, carried):
             g_turn[step_rows(tau), :] = jnp.transpose(grad[turned_rows(tau, length), :])
+            spread_mix(mix_rows[step_rows(tau, 2 * N), :], mix_turn, tau)
             return carried
 
         lax.fori_loop(0, length, turn, 0)
@@ -975,13 +1001,14 @@
 
             def some(i, carried):
                 pulled, spent = list(carried[0]), carried[1]
-                for j in range(UNROLL):
-                    tau = length - 1 - (i * UNROLL + j)
-                    at = pl.ds(pl.multiple_of(tau * channels + group * SUB, SUB), SUB)
-                    s, g = s_turn[at, :], g_turn[at, :]
+                block = length // UNROLL - 1 - i
+                s_here, g_here = [group_view(v, block, UNROLL, group) for v in (s_turn, g_turn)]
+                mix_here = mix_turn.at[step_rows(block, UNROLL * 2 * wide)]
+                for j in reversed(range(UNROLL)):
+                    s, g = s_here[row_of(j * groups), :], g_here[row_of(j * groups), :]
                     for n in range(N):
-                        row = pl.ds(pl.multiple_of((tau * 2 * N + N + n) * SUB, SUB), SUB)
-                        pulled[n] = jnp.exp2(s * rate[n]) * (pulled[n] + g * mix_turn[row, :])
+                        c = mix_here[row_of(j * 2 * N + N + n), :]
+                        pulled[n] = jnp.exp(s * rate[n]) * (pulled[n] + g * c)
                     spent = spent + s
                 return pulled, spent
 
@@ -997,35 +1024,37 @@
     out_terms[...] = jnp.zeros(out_terms.shape, f32)
 
     def retreat(group, carried):
-        ats = [
-            pl.ds(pl.multiple_of((chunk * steps + j) * channels + group * SUB, SUB), SUB)
-            for j in range(steps)
+        own = step_rows(group, wide)
+        views = [
+            group_view(v, chunk, steps, group)
+            for v in (s_turn, u_turn, g_turn, step_turn, in_turn)
         ]
-        s, u, g = [[v[at, :] for at in ats] for v in (s_turn, u_turn, g_turn)]
+        s, u, g = [[view[row_of(j * groups), :] for j in range(steps)] for view in views[:3]]
+        mix_here = mix_turn.at[step_rows(chunk, steps * 2 * wide)]
+        states_here = [states.at[j, own] for j in range(steps)]
+        enter_here, before_here = enter.at[own], before.at[0, own]
+        rate_here, held_here, sum_here = rates.at[own], held.at[own], rate_sum.at[own]
         step_sum, in_sum = [0.0] * steps, [0.0] * steps
         for n in range(N):
-            own = pl.ds(pl.multiple_of((group * N + n) * SUB, SUB), SUB)
-            rate, pull, rate_acc = rates[own, :], held[own, :], rate_sum[own, :]
-            first = jnp.where(chunk == 0, enter[own, :], before[0, own, :])
-            state = [first] + [states[j, own, :] for j in range(steps)]
+            at = row_of(n)
+            rate, pull, rate_acc = rate_here[at, :], held_here[at, :], sum_here[at, :]
+            first = jnp.where(chunk == 0, enter_here[at, :], before_here[at, :])
+            state = [first] + [view[at, :] for view in states_here]
             for j in reversed(range(steps)):
-                tau = chunk * steps + j
-                b_row = pl.ds(pl.multiple_of((tau * 2 * N + n) * SUB, SUB), SUB)
-                c_row = pl.ds(pl.multiple_of((tau * 2 * N + N + n) * SUB, SUB), SUB)
-                term = pl.ds((j * N + n) * SUB, SUB)
-                grad_state = g[j] * mix_turn[c_row, :] + pull
-                pull = jnp.exp2(s[j] * rate) * grad_state
+                term = row_of(j * N + n)
+                grad_state = g[j] * mix_here[row_of(j * 2 * N + N + n), :] + pull
+                pull = jnp.exp(s[j] * rate) * grad_state
                 mult = pull * state[j]
                 step_sum[j] = step_sum[j] + mult * rate
                 rate_acc = rate_acc + mult * s[j]
-                in_sum[j] = in_sum[j] + grad_state * mix_turn[b_row, :]
+                in_sum[j] = in_sum[j] + grad_state * mix_here[row_of(j * 2 * N + n), :]
                 in_terms[term, :] += grad_state * u[j]
                 out_terms[term, :] += state[j + 1] * g[j]
-            held[own, :] = pull
-            rate_sum[own, :] = rate_acc
-        for j, at in enumerate(ats):
-            step_turn[at, :] = step_sum[j]
-            in_turn[at, :] = in_sum[j]
+            held_here[at, :] = pull
+            sum_here[at, :] = rate_acc
+        for j in range(steps):
+            views[3][row_of(j * groups), :] = step_sum[j]
+            views[4][row_of(j * groups), :] = in_sum[j]
         return carried
 
     lax.fori_loop(0, groups, retreat, 0)
@@ -1058,7 +1087,7 @@
             step_in = step_pre[rows, :]
             state_in = in_flat[rows, :]
             grad_here = grad[rows, :]
-            step_grad = step_flat[rows, :] * math.log(2.0) + state_in * act
+            step_grad = step_flat[rows, :] + state_in * act
             pre_grad = step_grad * jax.nn.sigmoid(step_in)
             low = pre_grad.astype(bf16)
             step_grad_low[rows, :] = low
@@ -1067,9 +1096,8 @@
             for j in range(across):
                 block = seq * across + j
                 block_low = low[j * block_rows : (j + 1) * block_rows]
-                feat_part[ours, seq // 2, j, 0:R, :] = pick(
-                    ids_rows[block : block + 1, :],
-                    [dot(step_w[m], block_low, 1, 1) for m in range(MODS)],
+                feat_part[ours, seq // 2, j, 0:R, :] = modal_rows_of(
+                    step_w[...], block_low, ids_rows[block : block + 1, :]
                 )
                 turned = jnp.transpose(mix_flat[pl.ds(block * block_rows, block_rows), :])
                 feat_part[ours, seq // 2, j, R : R + 2 * N, :] = turned[: 2 * N]
@@ -1130,7 +1158,8 @@
             jax.ShapeDtypeStruct((channels, LANES), f32),
         ],
         scratch_shapes=[turn, turn, turn, pltpu.VMEM((length * 2 * N, LANES), f32)]
-        + [flat, flat, flat, terms, terms, states_row, states_row, states_row],
+        + [flat, flat, flat, terms, terms, states_row, states_row, states_row]
+        + [pltpu.VMEM((length * 2 * N * SUB, LANES), f32)],
         compiler_params=pltpu.CompilerParams(vmem_limit_bytes=VMEM_BYTES),
         cost_estimate=cost(1),
         name="scan_back",
@@ -1146,7 +1175,7 @@
     pre,
     inner,
     taps,
-    param_t,
+    param_w,
     inner_wide,
     inner_low,
     sums,
@@ -1164,8 +1193,9 @@
             block_rows = feat_grad.shape[4]
             block = pl.ds(pl.multiple_of(i * rows + j * block_rows, block_rows), block_rows)
             low = feat_grad[i % 2, i // 2, j]
+            stacked = dot(low, param_w[...], 0, 0)
             ext[block, :] = pick(
-                ids_ref[block, :], [dot(low, param_t[m], 0, 0) for m in range(MODS)]
+                ids_ref[block, :], [stacked[:, m * channels : (m + 1) * channels] for m in range(MODS)]
             )
         act_grad = act_part[at, :] + ext[at, :]
         here = pre[at, :]
@@ -1193,9 +1223,9 @@
         inner_low[at, :] = grad.astype(bf16)
 
 
-def conv_back(seqs, lengths, ids, feat_grad, act_part, pre, inner, taps, param_t):
+def conv_back(seqs, lengths, ids, feat_grad, act_part, pre, inner, taps, param_w):
     total, channels = pre.shape
-    ins = (ids, feat_grad, act_part, pre, inner, taps, param_t)
+    ins = (ids, feat_grad, act_part, pre, inner, taps, param_w)
     vmem = pl.BlockSpec(memory_space=pltpu.VMEM)
     return pl.pallas_call(
         functools.partial(conv_back_kernel, seqs),
@@ -1394,13 +1424,11 @@
     gain_vals = norm_gain.astype(f32)
 
     send_in = input_weight.reshape(MODS, slab, 2, seqs, channels)
-    send_in = send_in.transpose(3, 2, 0, 1, 4).reshape(seqs, 2 * MODS, slab, channels)
+    send_in = send_in.transpose(3, 2, 0, 1, 4).reshape(seqs, 2 * MODS * slab, channels)
     id_rows = 16
     send_ids = jnp.pad(modality.astype(bf16), (0, id_rows * channels - modality.shape[0]))
-    send_ids = jnp.broadcast_to(
-        send_ids.reshape(id_rows, channels), (seqs, 2 * MODS, id_rows, channels)
-    )
-    send_in = jnp.concatenate([send_in, send_ids], axis=2)
+    send_ids = jnp.broadcast_to(send_ids.reshape(id_rows, channels), (seqs, id_rows, channels))
+    send_in = jnp.concatenate([send_in, send_ids], axis=1)
     made = []
 
     def send(line):
@@ -1409,17 +1437,21 @@
 
     pieces, arrived = gathered_columns((normal_rows * gain_vals[None, :]).astype(bf16), send)
     inner_blocks = made[0]
-    ids = inner_blocks[:, 0, slab:].reshape(seqs, -1)[:, : modality.shape[0]].astype(jnp.int32)
+    ids = inner_blocks[:, 2 * MODS * slab :].reshape(seqs, -1)[:, : modality.shape[0]].astype(jnp.int32)
     ids_rows = ids.reshape(-1, tokens.shape[0])
     ids = ids.reshape(-1, 1)
     send_out = output_weight.reshape(MODS, seqs, channels, slab).transpose(1, 0, 3, 2)
-    param_t = param_weight.transpose(0, 2, 1)
+    send_out = send_out.reshape(seqs, MODS * slab, channels)
+    param_rows = param_weight.transpose(0, 2, 1).reshape(MODS * features, channels)
+    param_columns = param_weight.transpose(2, 0, 1).reshape(features, MODS * channels)
+    step_rows_w = step_weight.reshape(MODS * R, channels)
+    step_columns = step_weight.transpose(1, 0, 2).reshape(R, MODS * channels)
     core = place_bit(CORE)
     place = jnp.stack([place_bit(at) for at in (CORE, Y, X)]).astype(jnp.int32)
     taps = conv_weight.astype(f32)
     skip = skip_gain.astype(f32)[None, :]
     decay_rate = -jnp.exp(decay_log.astype(f32))
-    rate_t = jnp.pad((decay_rate * math.log2(math.e)).T, ((0, 0), (0, LANES - N)))
+    rate_t = jnp.pad(decay_rate.T, ((0, 0), (0, LANES - N)))
 
     *normed, own_inner, own_gate, inner, conv_pre, act_low, feats = project(
         lengths,
@@ -1430,14 +1462,15 @@
         inner_blocks,
         taps,
         conv_bias.astype(f32)[None, :],
-        param_t,
+        param_rows,
     )
     cotangents = lax.all_gather(
         held_back(cotangent, [inner]), SEQ + ("mod",), axis=0, tiled=True
     )
     feats, sent = summed_features(feats)
     gate_pre = modal_rows(normed, held_back(ids, [sent]), own_gate)
-    feats = held_back(feats, [gate_pre])
+    pair_in = side_by_side(own_inner, flip(*CORE)(own_inner), own_gate, flip(*CORE)(own_gate))
+    feats = held_back(feats, [gate_pre, pair_in])
     mix_high = feats[R:].astype(bf16)
     mix_rest = (feats[R:] - mix_high.astype(f32)).astype(bf16)
     feats = jnp.concatenate([feats[:R].astype(bf16), mix_high, mix_rest], axis=0)
@@ -1445,7 +1478,14 @@
 
     out_blocks = exchange(held_back(send_out, [feats]), SEQ)
     states, enter, step_pre, *turned, scan_out = scan(
-        lengths, ids, feats, conv_pre, step_weight, step_bias.astype(f32), rate_t, skip
+        lengths,
+        ids,
+        feats,
+        conv_pre,
+        step_columns,
+        step_bias.astype(f32).reshape(1, MODS * channels),
+        rate_t,
+        skip,
     )
     out_blocks, scan_out = lax.optimization_barrier((out_blocks, scan_out))
     own_out, grad_scan, gate_wide, gated_wide, gate_rows, gated_rows = gates(
@@ -1465,22 +1505,11 @@
         return low.reshape(seqs, slab, MODS * channels)
 
     ids_ours = core_rows(ids, core)
-    gated_both = both_cores(gated_rows, ids_ours)
-    other_out = flip(*CORE)(own_out)
-    gate_low, gate_gain = token_sums(gate_wide, own_gate)
-    gated_both, other_out, gated_wide = lax.optimization_barrier(
-        (gated_both, other_out, gated_wide)
-    )
-    out_low = dot(cotangents, gated_wide, 0, 0).astype(bf16)
-    gated_both = jnp.concatenate(gated_both, axis=1)
-    branch = SummedRows(row_parts(gated_both, side_by_side(own_out, other_out), 2))
+    gated_both = jnp.concatenate(both_cores(gated_rows, ids_ours), axis=1)
+    pair_out = side_by_side(own_out, flip(*CORE)(own_out))
+    branch = SummedRows(row_parts(gated_both, pair_out, 2))
     branch_sent = branch.stage(("x", "y"))
-    more_low = jnp.concatenate([by_holder(gate_low), by_holder(out_low)], axis=2)
-    grad_scan = held_back(grad_scan, branch_sent + [more_low])
-    more_low = exchange(more_low, SEQ).reshape(seqs, slab, 2, MODS, channels)
-    grad_gate = more_low[:, :, 0].transpose(2, 1, 0, 3)
-    grad_out = more_low[:, :, 1].transpose(2, 0, 3, 1)
-    grad_out = grad_out.reshape(MODS, seqs * channels, slab).astype(f32)
+    grad_scan = held_back(grad_scan, branch_sent)
 
     act_part, step_grad_low, feat_grad, sums, rate_sum = scan_back(
         place,
@@ -1492,18 +1521,21 @@
         grad_scan,
         states,
         enter,
-        step_weight,
+        step_rows_w,
         rate_t,
         skip,
     )
-    feat_grad = held_back(feat_grad, [more_low] + branch.arrived())
-    gate_rows = held_back(gate_rows, [feat_grad])
+    feat_grad = held_back(feat_grad, branch.arrived())
+    gate_rows, gate_wide, gated_wide = held_back((gate_rows, gate_wide, gated_wide), [feat_grad])
     gate_both = both_cores(gate_rows, ids_ours)
     feat_grad, sent = summed_features(feat_grad, bf16)
-    own_inner, own_gate = held_back((own_inner, own_gate), [sent])
-    pair_in = side_by_side(own_inner, flip(*CORE)(own_inner), own_gate, flip(*CORE)(own_gate))
-    feat_grad = held_back(feat_grad.astype(bf16), branch.stage(("y", "x")) + [pair_in])
-    feat_grad = shared_features(feat_grad)
+    feat_grad = held_back(feat_grad.astype(bf16), branch.stage(("y", "x")))
+    gate_wide, gated_wide = held_back((gate_wide, gated_wide), [sent])
+    gate_low, gate_gain = token_sums(gate_wide, own_gate)
+    out_low = dot(cotangents, gated_wide, 0, 0).astype(bf16)
+    more_low = jnp.concatenate([by_holder(gate_low), by_holder(out_low)], axis=2)
+    feat_grad = shared_features(feat_grad, [more_low])
+    more_low = exchange(held_back(more_low, [feat_grad]), SEQ)
     branch.hold([feat_grad])
     branch.merge()
 
@@ -1516,7 +1548,7 @@
         conv_pre,
         inner,
         taps,
-        param_t,
+        param_columns,
     )
     both_wide = jnp.concatenate(both_cores(inner_rows, ids_ours) + gate_both, axis=1)
     products = row_parts(both_wide, pair_in, COLUMNS)
@@ -1525,7 +1557,12 @@
     branch.hold(sent)
     branch.stage(("zl", "zl"))
     inner_low, inner_gain = token_sums(held_back(inner_wide, sent), own_inner)
-    inner_low = exchange(by_holder(inner_low), SEQ).reshape(seqs, slab, MODS, channels)
+    inner_low, more_low = lax.optimization_barrier((by_holder(inner_low), more_low))
+    inner_low = exchange(inner_low, SEQ).reshape(seqs, slab, MODS, channels)
+    more_low = more_low.reshape(seqs, slab, 2, MODS, channels)
+    grad_gate = more_low[:, :, 0].transpose(2, 1, 0, 3)
+    grad_out = more_low[:, :, 1].transpose(2, 0, 3, 1)
+    grad_out = grad_out.reshape(MODS, seqs * channels, slab).astype(f32)
     branch.stage(("zh", "zh"))
     sent = normed_sums.stage(("y", "x"))
     output = (token_vals + branch.result()).astype(bf16)

time: 817 us -> 807 us (0.988)
  local copies, waits for them, and re-layouts: 96 us -> 86.7 us
    ppermute x52, waiting for transfers between devices: 100 us -> 116 us  [flip(): lax.ppermute(value, axis, [(i, i ^ bit) for i in range(size)])]
    all_to_all x2, waiting for transfers between devices: 21.2 us -> 9.58 us  [share(): lax.all_to_all(jnp.broadcast_to(values, (size,) + values.shape), axes, 0, 0)]
    all_to_all x6, waiting for transfers between devices: 60.1 us -> 48.6 us  [exchange(): return lax.all_to_all(blocks, axes, 0, 0)]
    squeeze x17, local copies, waits for them, and re-layouts: 24.8 us -> 15.5 us  [taken(): return lax.dynamic_index_in_dim(values, at, dim, keepdims=False)]
    unnamed x194 -> x202, local copies, waits for them, and re-layouts: 21.8 us -> 20.9 us
  transfers between devices with their start and end apart: 61 -> 61, of which waited for: 23 -> 23; matrix products, arithmetic and copies ran while one was open for 23% -> 28% of each run, Pallas kernels for 19% -> 19%
where the time goes in v2:
time: 807 us; the launch traced here: 795 us
  Pallas kernels  202 us (25%)
  waiting for transfers between devices  174 us (22%)
  starting transfers between devices  95 us (12%)
  other arithmetic  94.5 us (12%)
  local copies, waits for them, and re-layouts  86.7 us (11%)
  matrix products  70.7 us (9%)
  blocking collectives  56.1 us (7%)
  between operations  15.8 us (2%)
    ppermute x52, waiting for transfers between devices, flip(): lax.ppermute(value, axis, [(i, i ^ bit) for i in range(size)])  116 us
    dot_general x17, matrix products, dot(): lax.dot_general(left, right, (((left_dim,), (right_dim,)), ((), ())), pre...  70.7 us
    pallas_call x1, Pallas kernels, scan_back(): pl.pallas_call(back_kernel, grid=(chunks,), in_specs=[pl.BlockSpec(memory...  67.4 us
    all_to_all x1, blocking collectives, share(): lax.all_to_all(jnp.broadcast_to(values, (size,) + values.shape), axes, 0, 0)  56.1 us
    ppermute x52, starting transfers between devices, flip(): lax.ppermute(value, axis, [(i, i ^ bit) for i in range(size)])  54.1 us
    pallas_call x1, Pallas kernels, scan(): pl.pallas_call(scan_kernel, grid=(length // steps,), in_specs=[pl.BlockSp...  53.7 us
    all_to_all x6, waiting for transfers between devices, exchange(): return lax.all_to_all(blocks, axes, 0, 0)  48.6 us
    all_to_all x6, starting transfers between devices, exchange(): return lax.all_to_all(blocks, axes, 0, 0)  30.3 us
  transfers between devices with their start and end apart: 61, of which 23 were waited for; matrix products, arithmetic and copies ran while one was open for 28% of the time, Pallas kernels for 19%

profile of v2, /device:TPU:0, one launch (start us, length us, event | category | flops | bytes accessed | tf_op | source)
XLA Modules:
  0.0 794.9 jit_solution(5438169737333561086)
XLA Ops:
  15.3 6.3 collective-permute-done
  25.8 5.1 collective-permute-done.1
  38.5 6.3 collective-permute-done.2
  49.9 4.6 reshape.1121
  76.6 8.9 %collective-permute-done.8 = bf16[2,2,128,512]{3,2,1,0:T(8,128)(2,1)} collective-permute-done((bf16[2,2,128,512]{3,2,1,0:T(8,128)(2,1)}, bf16[2,2,128,512]{3,2,1,0:T(8,128)(2,1)}, u32[]{:S(2)}, u32[]{:S(2)}) %collective-permute-start.8) | collective-permute-done | bytes 524320 | tf_op jit(solution)/shard_map/ppermute | solution.py:1278
  95.0 8.5 %collective-permute-done.16 = bf16[2,2,128,512]{3,2,1,0:T(8,128)(2,1)S(1)} collective-permute-done((bf16[2,2,128,512]{3,2,1,0:T(8,128)(2,1)S(1)}, bf16[2,2,128,512]{3,2,1,0:T(8,128)(2,1)S(1)}, u32[]{:S(2)}, u32[]{:S(2)}) %collective-permute-start.16) | collective-permute-done | bytes 524320 | tf_op jit(solution)/shard_map/ppermute | solution.py:1278
  106.2 18.6 %collective-permute-done.20 = bf16[2,2,128,512]{3,2,1,0:T(8,128)(2,1)S(1)} collective-permute-done((bf16[2,2,128,512]{3,2,1,0:T(8,128)(2,1)S(1)}, bf16[2,2,128,512]{3,2,1,0:T(8,128)(2,1)S(1)}, u32[]{:S(2)}, u32[]{:S(2)}) %collective-permute-start.20) | collective-permute-done | bytes 524320 | tf_op jit(solution)/shard_map/ppermute | solution.py:1278
  126.0 17.0 %all-to-all-done.refs_18_ = bf16[8,1552,128]{2,1,0:T(8,128)(2,1)S(1)} async-done(((bf16[8,1552,128]{2,1,0:T(8,128)(2,1)}), bf16[8,1552,128]{2,1,0:T(8,128)(2,1)S(1)}, u32[]{:S(2)}, u32[]{:S(2)}) %all-to-all-start) | async-done | bytes 3178528 | tf_op jit(solution)/shard_map/all_to_all | solution.py:1269
  146.7 21.4 %collective-permute-done.17.refs_9_ = bf16[2,2,2,128,512]{4,3,2,1,0:T(8,128)(2,1)} collective-permute-done((bf16[2,2,2,128,512]{4,3,2,1,0:T(8,128)(2,1)}, bf16[2,2,2,128,512]{4,3,2,1,0:T(8,128)(2,1)}, u32[]{:S(2)}, u32[]{:S(2)}) %collective-permute-start.17) | collective-permute-done | bytes 1048608 | tf_op jit(solution)/shard_map/ppermute | solution.py:1278
  173.7 26.1 %project.1 = (bf16[4096,512]{1,0:T(8,128)(2,1)}, bf16[4096,512]{1,0:T(8,128)(2,1)}, bf16[4096,512]{1,0:T(8,128)(2,1)}, bf16[4096,512]{1,0:T(8,128)(2,1)}, bf16[2...) custom-call(s32[2]{0:T(128)} %lengths.5, ...), custom_call_target="tpu_custom_call" | custom-call | bytes 3690000 | tf_op jit(solution)/shard_map/project/pallas_call | solution.py:597
  212.5 14.8 %modal_rows.1.pre = f32[4096,128]{1,0:T(8,128)} custom-call(bf16[4096,512]{1,0:T(8,128)(2,1)} %get-tuple-element.96.refs_0_, bf16[4096,512]{1,0:T(8,128)(2,1)} %get-tuple-element.97.refs_1_, bf16[4096,512]{1,0:T(8,128)(2,1)} %get-tuple-element.98.refs_2_, bf16[4096,512]{1,0:T(8,128)(2,1)} %get-tuple-element.99.refs_3_, s32[4096,1]{1,0:T(8,128)} %copy.146.refs_4_, ...), custom_call_target="tpu_custom_call" | custom-call | bytes 3690000 | tf_op jit(solution)/shard_map/modal_rows/pallas_call | solution.py:640
  227.3 5.9 side_by_side.2
  233.2 21.3 %all-to-all-done.1 = f32[16,160,128]{2,1,0:T(8,128)S(1)} async-done(((f32[16,160,128]{2,1,0:T(8,128)}), f32[16,160,128]{2,1,0:T(8,128)S(1)}, u32[]{:S(2)}, u32[]{:S(2)}) %all-to-all-start.1) | async-done | bytes 1310752 | tf_op jit(solution)/shard_map/all_to_all | solution.py:1269
  254.7 56.1 %all_to_all.46 = bf16[16,192,128]{2,1,0:T(8,128)(2,1)S(1)} all-to-all(bf16[16,192,128]{2,1,0:T(8,128)(2,1)S(1)} %broadcast_in_dim.129), channel_id=1, replica_groups=mesh['z'=4,'core'=2,'mod'=4] {'z','mod'}, dimensions={0} | all-to-all | bytes 1572864 | tf_op jit(solution)/shard_map/all_to_all | solution.py:1265
  316.0 6.5 all-to-all-start.3
  325.5 53.7 %scan.1 = (f32[32,2048,128]{2,1,0:T(8,128)}, f32[2048,128]{1,0:T(8,128)}, f32[4096,128]{1,0:T(8,128)}, f32[4096,128]{1,0:T(8,128)}, f32[4096,128]{1,0:T(8,128)},...) custom-call(s32[2]{0:T(128)} %lengths.5, s32[4096,1]{1,0:T(8,128)} %copy.144.refs_16_.ids_ref, ...), custom_call_target="tpu_custom_call" | custom-call | bytes 3690000 | tf_op jit(solution)/shard_map/scan/pallas_call | solution.py:926
  380.5 18.1 %gates.1 = (bf16[2048,384]{1,0:T(8,128)(2,1)}, f32[4096,128]{1,0:T(8,128)}, bf16[4096,384]{1,0:T(8,128)(2,1)}, bf16[4096,384]{1,0:T(8,128)(2,1)}, bf16[4096,128]{1,0:T(8,128)(2,1)}, /*index=5*/bf16[4096,128]{1,0:T(8,128)(2,1)}) custom-call(bf16[4096,2048]{1,0:T(8,128)(2,1)} %all-gather.2.cloned.1.call-done.cot, s32[4096,1]{1,0:T(8,128)} %copy.144.refs_16_.ids_ref, ...), custom_call_target="tpu_custom_call" | custom-call | bytes 3690000 | tf_op jit(solution)/shard_map/gates/pallas_call | solution.py:705
  411.0 6.0 convolution_convert_fusion
  426.7 67.4 %scan_back.1 = (f32[4096,128]{1,0:T(8,128)}, bf16[4096,128]{1,0:T(8,128)(2,1)}, f32[2,4,4,160,128]{4,3,2,1,0:T(8,128)}, f32[8,128]{1,0:T(8,128)}, f32[128,128]{1,0:T(8,128)}) custom-call(s32[3]{0:T(128)} %pad_add_fusion.place.core, s32[4096,1]{1,0:T(8,128)} %copy.144.refs_16_.ids_ref, s32[32,128]{1,0:T(8,128)} %reshape.1126.refs_17_.ids_rows, ...), custom_call_target="tpu_custom_call" | custom-call | bytes 3690000 | tf_op jit(solution)/shard_map/scan_back/pallas_call | solution.py:1134
  510.3 6.9 all-to-all-start.4
  517.2 5.6 fusion.62
  526.0 13.4 %convolution_convert_fusion.6 = bf16[2048,384]{1,0:T(8,128)(2,1)} fusion(bf16[4096,2048]{1,0:T(8,128)(2,1)} %all-gather.2.cloned.1.call-done.cot, bf16[4096,384]{1,0:T(8,128)(2,1)S(1)} %copy-done.83), kind=kOutput, calls=%fused_computation.17 | convolution fusion | flops 6443237376 | bytes 21495808 | tf_op jit(solution)/shard_map/dot_general | solution.py:479
  542.2 6.6 all-to-all-start.5
  548.8 4.7 fusion.60
  574.3 11.9 %conv_back.1 = (bf16[4096,384]{1,0:T(8,128)(2,1)}, bf16[4096,128]{1,0:T(8,128)(2,1)}, f32[8,128]{1,0:T(8,128)}) custom-call(s32[2]{0:T(128)} %lengths.5, s32[4096,1]{1,0:T(8,128)} %copy.144.refs_16_.ids_ref, bf16[2,4,4,160,128]{4,3,2,1,0:T(8,128)(2,1)} %maximum_select_fusion.1.feat_grad, f32[4096,128]{1,0:T(8,128)} %get-tuple-element.132.act_part, ...), custom_call_target="tpu_custom_call" | custom-call | bytes 3690000 | tf_op jit(solution)/shard_map/conv_back/pallas_call | solution.py:1230
  588.6 4.7 all-to-all-start.6
  648.5 21.0 %collective-permute-done.38 = bf16[2,128,2048]{2,1,0:T(8,128)(2,1)S(1)} collective-permute-done((bf16[2,128,2048]{2,1,0:T(8,128)(2,1)S(1)}, bf16[2,128,2048]{2,1,0:T(8,128)(2,1)S(1)}, u32[]{:S(2)}, u32[]{:S(2)}) %collective-permute-start.38) | collective-permute-done | bytes 1048608 | tf_op jit(solution)/shard_map/ppermute | solution.py:1278
  677.5 4.9 broadcast_select_fusion.5
  705.7 4.6 copy.175
  721.0 9.6 %all-to-all-done.7 = bf16[8,256,384]{1,2,0:T(8,128)(2,1)} async-done(((bf16[8,256,384]{1,2,0:T(8,128)(2,1)}), bf16[8,256,384]{1,2,0:T(8,128)(2,1)}, u32[]{:S(2)}, u32[]{:S(2)}) %all-to-all-start.7) | async-done | bytes 1572896 | tf_op jit(solution)/shard_map/all_to_all | solution.py:1269
  744.3 8.1 %all-to-all-done.8 = f32[32,1,2048]{2,1,0:T(1,128)S(1)} async-done(((f32[32,1,2048]{2,1,0:T(1,128)}), f32[32,1,2048]{2,1,0:T(1,128)S(1)}, u32[]{:S(2)}, u32[]{:S(2)}) %all-to-all-start.8) | async-done | bytes 262176 | tf_op jit(solution)/shard_map/all_to_all | solution.py:1265
  763.9 10.3 %copy.178 = f32[3,256,2,1024]{3,2,1,0:T(2,128)} copy(f32[3,256,2,1024]{1,3,0,2:T(8,128)} %maximum_convert_fusion) | data formatting | bytes 12582912
  (465 shorter events, 294.5 us)
Async XLA Ops:
  67.2 75.8 %all-to-all-start = ((bf16[8,1552,128]{2,1,0:T(8,128)(2,1)}), bf16[8,1552,128]{2,1,0:T(8,128)(2,1)S(1)}, u32[]{:S(2)}, u32[]{:S(2)}) async-start(bf16[8,1552,128]{2,1,0:T(8,128)(2,1)} %pad_maximum_fusion), calls=%async_computation | async-start | bytes 6356992 | tf_op jit(solution)/shard_map/all_to_all | solution.py:1269
  70.9 308.4 %all-gather.2.cloned.1.call-start = ((), (), s32[]{:S(2)}) async-start(), calls=%async_computation.9 | async-start | bytes 17301504 | tf_op jit(solution)/shard_map/all_gather | solution.py:1467
  87.8 55.3 %collective-permute-start.10 = (bf16[2,2,2,128,512]{4,3,2,1,0:T(8,128)(2,1)}, bf16[2,2,2,128,512]{4,3,2,1,0:T(8,128)(2,1)}, u32[]{:S(2)}, u32[]{:S(2)}) collective-permute-start(bf16[2,2,2,128,512]{4,3,2,1,0:T(8,128)(2,1)} %maximum_select_fusion.2.refs_0_), channel_id=1, source_target_pairs={{0,4},{4,0},{1,5},{5,1},{2,6},{6,2},{3,7},{7,3},{8,12},{12,8},{9,1... | collective-permute-start | bytes 3145736 | tf_op jit(solution)/shard_map/ppermute | solution.py:1278
  87.8 56.8 %collective-permute-start.9 = (bf16[2,2,2,128,512]{4,3,2,1,0:T(8,128)(2,1)}, bf16[2,2,2,128,512]{4,3,2,1,0:T(8,128)(2,1)}, u32[]{:S(2)}, u32[]{:S(2)}) collective-permute-start(bf16[2,2,2,128,512]{4,3,2,1,0:T(8,128)(2,1)} %maximum_select_fusion.2.refs_0_), channel_id=1, source_target_pairs={{0,2},{1,3},{2,0},{3,1},{4,6},{5,7},{6,4},{7,5},{8,10},{9,11},{10,... | collective-permute-start | bytes 3145736 | tf_op jit(solution)/shard_map/ppermute | solution.py:1278
  92.1 32.7 %collective-permute-start.20 = (bf16[2,2,128,512]{3,2,1,0:T(8,128)(2,1)S(1)}, bf16[2,2,128,512]{3,2,1,0:T(8,128)(2,1)S(1)}, u32[]{:S(2)}, u32[]{:S(2)}) collective-permute-start(bf16[2,2,128,512]{3,2,1,0:T(8,128)(2,1)S(1)} %copy-done.67), channel_id=1, source_target_pairs={{0,2},{1,3},{2,0},{3,1},{4,6},{5,7},{6,4},{7,5},{8,10},{9,11},{10,... | collective-permute-start | bytes 1572872 | tf_op jit(solution)/shard_map/ppermute | solution.py:1278
  94.9 51.2 %collective-permute-start.14 = (bf16[2,2,2,128,512]{4,3,2,1,0:T(8,128)(2,1)}, bf16[2,2,2,128,512]{4,3,2,1,0:T(8,128)(2,1)}, u32[]{:S(2)}, u32[]{:S(2)}) collective-permute-start(bf16[2,2,2,128,512]{4,3,2,1,0:T(8,128)(2,1)} %maximum_select_fusion.3.refs_4_), channel_id=1, source_target_pairs={{0,4},{4,0},{1,5},{5,1},{2,6},{6,2},{3,7},{7,3},{8,12},{12,8},{9,1... | collective-permute-start | bytes 3145736 | tf_op jit(solution)/shard_map/ppermute | solution.py:1278
  103.5 42.6 %collective-permute-start.13 = (bf16[2,2,2,128,512]{4,3,2,1,0:T(8,128)(2,1)}, bf16[2,2,2,128,512]{4,3,2,1,0:T(8,128)(2,1)}, u32[]{:S(2)}, u32[]{:S(2)}) collective-permute-start(bf16[2,2,2,128,512]{4,3,2,1,0:T(8,128)(2,1)} %maximum_select_fusion.3.refs_4_), channel_id=1, source_target_pairs={{0,1},{1,0},{2,3},{3,2},{4,5},{5,4},{6,7},{7,6},{8,9},{9,8},{10,11... | collective-permute-start | bytes 3145736 | tf_op jit(solution)/shard_map/ppermute | solution.py:1278
  143.1 25.0 %collective-permute-start.17 = (bf16[2,2,2,128,512]{4,3,2,1,0:T(8,128)(2,1)}, bf16[2,2,2,128,512]{4,3,2,1,0:T(8,128)(2,1)}, u32[]{:S(2)}, u32[]{:S(2)}) collective-permute-start(bf16[2,2,2,128,512]{4,3,2,1,0:T(8,128)(2,1)} %maximum_select_fusion.4.refs_8_), channel_id=1, source_target_pairs={{0,2},{1,3},{2,0},{3,1},{4,6},{5,7},{6,4},{7,5},{8,10},{9,11},{10,... | collective-permute-start | bytes 3145736 | tf_op jit(solution)/shard_map/ppermute | solution.py:1278
  146.1 27.6 %collective-permute-start.22 = (bf16[2,2,2,128,512]{4,3,2,1,0:T(8,128)(2,1)}, bf16[2,2,2,128,512]{4,3,2,1,0:T(8,128)(2,1)}, u32[]{:S(2)}, u32[]{:S(2)}) collective-permute-start(bf16[2,2,2,128,512]{4,3,2,1,0:T(8,128)(2,1)} %maximum_select_fusion.5.refs_12_), channel_id=1, source_target_pairs={{0,4},{4,0},{1,5},{5,1},{2,6},{6,2},{3,7},{7,3},{8,12},{12,8},{9,1... | collective-permute-start | bytes 3145736 | tf_op jit(solution)/shard_map/ppermute | solution.py:1278
  146.1 27.6 %collective-permute-start.11 = (bf16[2,2,2,128,512]{4,3,2,1,0:T(8,128)(2,1)}, bf16[2,2,2,128,512]{4,3,2,1,0:T(8,128)(2,1)}, u32[]{:S(2)}, u32[]{:S(2)}) collective-permute-start(bf16[2,2,2,128,512]{4,3,2,1,0:T(8,128)(2,1)} %collective-permute-done.9.refs_1_), channel_id=1, source_target_pairs={{0,4},{4,0},{1,5},{5,1},{2,6},{6,2},{3,7},{7,3},{8,12},{12,8},{9,1... | collective-permute-start | bytes 3145736 | tf_op jit(solution)/shard_map/ppermute | solution.py:1278
  146.6 27.1 %collective-permute-start.15 = (bf16[2,2,2,128,512]{4,3,2,1,0:T(8,128)(2,1)}, bf16[2,2,2,128,512]{4,3,2,1,0:T(8,128)(2,1)}, u32[]{:S(2)}, u32[]{:S(2)}) collective-permute-start(bf16[2,2,2,128,512]{4,3,2,1,0:T(8,128)(2,1)} %collective-permute-done.13.refs_5_), channel_id=1, source_target_pairs={{0,4},{4,0},{1,5},{5,1},{2,6},{6,2},{3,7},{7,3},{8,12},{12,8},{9,1... | collective-permute-start | bytes 3145736 | tf_op jit(solution)/shard_map/ppermute | solution.py:1278
  205.9 48.6 %all-to-all-start.1 = ((f32[16,160,128]{2,1,0:T(8,128)}), f32[16,160,128]{2,1,0:T(8,128)S(1)}, u32[]{:S(2)}, u32[]{:S(2)}) async-start(f32[16,160,128]{2,1,0:T(8,128)} %bitcast.344), calls=%async_computation.1 | async-start | bytes 2621440 | tf_op jit(solution)/shard_map/all_to_all | solution.py:1269
  316.0 63.2 %all-to-all-start.3 = ((bf16[8,768,128]{2,1,0:T(8,128)(2,1)}), bf16[8,768,128]{2,1,0:T(8,128)(2,1)S(1)}, u32[]{:S(2)}, u32[]{:S(2)}) async-start(bf16[8,768,128]{2,1,0:T(8,128)(2,1)} %bitcast.43), calls=%async_computation.3 | async-start | bytes 3145728 | tf_op jit(solution)/shard_map/all_to_all | solution.py:1269
  422.7 71.4 %collective-permute-start.30 = (bf16[2,2,2,128,1024]{4,3,1,0,2:T(8,128)(2,1)}, bf16[2,2,2,128,1024]{4,3,1,0,2:T(8,128)(2,1)}, u32[]{:S(2)}, u32[]{:S(2)}) collective-permute-start(bf16[2,2,2,128,1024]{4,3,1,0,2:T(8,128)(2,1)} %copy_bitcast_fusion.1), channel_id=1, source_target_pairs={{0,1},{1,0},{2,3},{3,2},{4,5},{5,4},{6,7},{7,6},{8,9},{9,8},{10,11... | collective-permute-start | bytes 6291464 | tf_op jit(solution)/shard_map/ppermute | solution.py:1278
  425.8 68.3 %collective-permute-start.31 = (bf16[2,2,2,128,1024]{4,3,1,0,2:T(8,128)(2,1)}, bf16[2,2,2,128,1024]{4,3,1,0,2:T(8,128)(2,1)}, u32[]{:S(2)}, u32[]{:S(2)}) collective-permute-start(bf16[2,2,2,128,1024]{4,3,1,0,2:T(8,128)(2,1)} %copy_bitcast_fusion), channel_id=1, source_target_pairs={{0,2},{1,3},{2,0},{3,1},{4,6},{5,7},{6,4},{7,5},{8,10},{9,11},{10,... | collective-permute-start | bytes 6291464 | tf_op jit(solution)/shard_map/ppermute | solution.py:1278
  503.2 85.4 %collective-permute-start.32 = (bf16[2,2,128,1024]{3,2,1,0:T(8,128)(2,1)}, bf16[2,2,128,1024]{3,2,1,0:T(8,128)(2,1)}, u32[]{:S(2)}, u32[]{:S(2)}) collective-permute-start(bf16[2,2,128,1024]{3,2,1,0:T(8,128)(2,1)} %fusion.7), channel_id=1, source_target_pairs={{0,2},{1,3},{2,0},{3,1},{4,6},{5,7},{6,4},{7,5},{8,10},{9,11},{10,... | collective-permute-start | bytes 3145736 | tf_op jit(solution)/shard_map/ppermute | solution.py:1278
  507.4 66.9 %collective-permute-start.35 = (bf16[2,2,128,1024]{3,2,1,0:T(8,128)(2,1)}, bf16[2,2,128,1024]{3,2,1,0:T(8,128)(2,1)}, u32[]{:S(2)}, u32[]{:S(2)}) collective-permute-start(bf16[2,2,128,1024]{3,2,1,0:T(8,128)(2,1)} %fusion.6), channel_id=1, source_target_pairs={{0,1},{1,0},{2,3},{3,2},{4,5},{5,4},{6,7},{7,6},{8,9},{9,8},{10,11... | collective-permute-start | bytes 3145736 | tf_op jit(solution)/shard_map/ppermute | solution.py:1278
  510.3 29.8 %all-to-all-start.4 = ((bf16[16,160,128]{2,1,0:T(8,128)(2,1)}), bf16[16,160,128]{2,1,0:T(8,128)(2,1)}, u32[]{:S(2)}, u32[]{:S(2)}) async-start(bf16[16,160,128]{2,1,0:T(8,128)(2,1)} %bitcast.354), calls=%async_computation.4 | async-start | bytes 1310720 | tf_op jit(solution)/shard_map/all_to_all | solution.py:1269
  588.6 93.7 %all-to-all-start.6 = ((bf16[8,256,768]{1,2,0:T(8,128)(2,1)}), bf16[8,256,768]{1,2,0:T(8,128)(2,1)}, u32[]{:S(2)}, u32[]{:S(2)}) async-start(bf16[8,256,768]{1,2,0:T(8,128)(2,1)} %pad_maximum_fusion.1), calls=%async_computation.6 | async-start | bytes 6291456 | tf_op jit(solution)/shard_map/all_to_all | solution.py:1269
  618.0 26.0 %collective-permute-start.47 = (bf16[2,2,2,128,512]{4,3,1,0,2:T(8,128)(2,1)S(1)}, bf16[2,2,2,128,512]{4,3,1,0,2:T(8,128)(2,1)S(1)}, u32[]{:S(2)}, u32[]{:S(2)}) collective-permute-start(bf16[2,2,2,128,512]{4,3,1,0,2:T(8,128)(2,1)S(1)} %copy_bitcast_fusion.2), channel_id=1, source_target_pairs={{0,2},{1,3},{2,0},{3,1},{4,6},{5,7},{6,4},{7,5},{8,10},{9,11},{10,... | collective-permute-start | bytes 3145736 | tf_op jit(solution)/shard_map/ppermute | solution.py:1278
  619.5 26.5 %collective-permute-start.46 = (bf16[2,2,2,128,512]{4,3,1,0,2:T(8,128)(2,1)S(1)}, bf16[2,2,2,128,512]{4,3,1,0,2:T(8,128)(2,1)S(1)}, u32[]{:S(2)}, u32[]{:S(2)}) collective-permute-start(bf16[2,2,2,128,512]{4,3,1,0,2:T(8,128)(2,1)S(1)} %copy_bitcast_fusion.3), channel_id=1, source_target_pairs={{0,1},{1,0},{2,3},{3,2},{4,5},{5,4},{6,7},{7,6},{8,9},{9,8},{10,11... | collective-permute-start | bytes 3145736 | tf_op jit(solution)/shard_map/ppermute | solution.py:1278
  620.7 52.4 %collective-permute-start.40 = (bf16[2,2,2,128,512]{4,3,1,0,2:T(8,128)(2,1)S(1)}, bf16[2,2,2,128,512]{4,3,1,0,2:T(8,128)(2,1)S(1)}, u32[]{:S(2)}, u32[]{:S(2)}) collective-permute-start(bf16[2,2,2,128,512]{4,3,1,0,2:T(8,128)(2,1)S(1)} %copy_bitcast_fusion.5), channel_id=1, source_target_pairs={{0,1},{1,0},{2,3},{3,2},{4,5},{5,4},{6,7},{7,6},{8,9},{9,8},{10,11... | collective-permute-start | bytes 3145736 | tf_op jit(solution)/shard_map/ppermute | solution.py:1278
  621.8 53.6 %collective-permute-start.41 = (bf16[2,2,2,128,512]{4,3,1,0,2:T(8,128)(2,1)S(1)}, bf16[2,2,2,128,512]{4,3,1,0,2:T(8,128)(2,1)S(1)}, u32[]{:S(2)}, u32[]{:S(2)}) collective-permute-start(bf16[2,2,2,128,512]{4,3,1,0,2:T(8,128)(2,1)S(1)} %copy_bitcast_fusion.4), channel_id=1, source_target_pairs={{0,2},{1,3},{2,0},{3,1},{4,6},{5,7},{6,4},{7,5},{8,10},{9,11},{10,... | collective-permute-start | bytes 3145736 | tf_op jit(solution)/shard_map/ppermute | solution.py:1278
  623.1 46.4 %collective-permute-start.38 = (bf16[2,128,2048]{2,1,0:T(8,128)(2,1)S(1)}, bf16[2,128,2048]{2,1,0:T(8,128)(2,1)S(1)}, u32[]{:S(2)}, u32[]{:S(2)}) collective-permute-start(bf16[2,128,2048]{2,1,0:T(8,128)(2,1)S(1)} %fusion.25), channel_id=1, source_target_pairs={{0,8},{8,0},{16,24},{24,16},{1,9},{9,1},{17,25},{25,17},{2,10},{10... | collective-permute-start | bytes 3145736 | tf_op jit(solution)/shard_map/ppermute | solution.py:1278
  645.1 66.4 %collective-permute-start.49 = (bf16[2,2,128,512]{3,2,1,0:T(8,128)(2,1)}, bf16[2,2,128,512]{3,2,1,0:T(8,128)(2,1)}, u32[]{:S(2)}, u32[]{:S(2)}) collective-permute-start(bf16[2,2,128,512]{3,2,1,0:T(8,128)(2,1)} %fusion.28), channel_id=1, source_target_pairs={{0,1},{1,0},{2,3},{3,2},{4,5},{5,4},{6,7},{7,6},{8,9},{9,8},{10,11... | collective-permute-start | bytes 1572872 | tf_op jit(solution)/shard_map/ppermute | solution.py:1278
  647.1 63.3 %collective-permute-start.48 = (bf16[2,2,128,512]{3,2,1,0:T(8,128)(2,1)}, bf16[2,2,128,512]{3,2,1,0:T(8,128)(2,1)}, u32[]{:S(2)}, u32[]{:S(2)}) collective-permute-start(bf16[2,2,128,512]{3,2,1,0:T(8,128)(2,1)} %fusion.29), channel_id=1, source_target_pairs={{0,2},{1,3},{2,0},{3,1},{4,6},{5,7},{6,4},{7,5},{8,10},{9,11},{10,... | collective-permute-start | bytes 1572872 | tf_op jit(solution)/shard_map/ppermute | solution.py:1278
  670.7 114.0 %collective-permute-start.39 = (bf16[128,2048]{1,0:T(8,128)(2,1)}, bf16[128,2048]{1,0:T(8,128)(2,1)}, u32[]{:S(2)}, u32[]{:S(2)}) collective-permute-start(bf16[128,2048]{1,0:T(8,128)(2,1)} %fusion.32), channel_id=1, source_target_pairs={{0,16},{8,24},{16,0},{24,8},{1,17},{9,25},{17,1},{25,9},{2,18},{10... | collective-permute-start | bytes 1572872 | tf_op jit(solution)/shard_map/ppermute | solution.py:1278
  674.1 43.3 %collective-permute-start.42 = (bf16[2,2,128,512]{3,2,1,0:T(8,128)(2,1)}, bf16[2,2,128,512]{3,2,1,0:T(8,128)(2,1)}, u32[]{:S(2)}, u32[]{:S(2)}) collective-permute-start(bf16[2,2,128,512]{3,2,1,0:T(8,128)(2,1)} %fusion.31), channel_id=1, source_target_pairs={{0,2},{1,3},{2,0},{3,1},{4,6},{5,7},{6,4},{7,5},{8,10},{9,11},{10,... | collective-permute-start | bytes 1572872 | tf_op jit(solution)/shard_map/ppermute | solution.py:1278
  676.5 42.0 %collective-permute-start.43 = (bf16[2,2,128,512]{3,2,1,0:T(8,128)(2,1)}, bf16[2,2,128,512]{3,2,1,0:T(8,128)(2,1)}, u32[]{:S(2)}, u32[]{:S(2)}) collective-permute-start(bf16[2,2,128,512]{3,2,1,0:T(8,128)(2,1)} %fusion.30), channel_id=1, source_target_pairs={{0,1},{1,0},{2,3},{3,2},{4,5},{5,4},{6,7},{7,6},{8,9},{9,8},{10,11... | collective-permute-start | bytes 1572872 | tf_op jit(solution)/shard_map/ppermute | solution.py:1278
  685.0 45.6 %all-to-all-start.7 = ((bf16[8,256,384]{1,2,0:T(8,128)(2,1)}), bf16[8,256,384]{1,2,0:T(8,128)(2,1)}, u32[]{:S(2)}, u32[]{:S(2)}) async-start(bf16[8,256,384]{1,2,0:T(8,128)(2,1)} %copy.167), calls=%async_computation.7 | async-start | bytes 3145728 | tf_op jit(solution)/shard_map/all_to_all | solution.py:1269
  715.4 37.7 %collective-permute-start.50 = (bf16[2,128,1024]{2,1,0:T(8,128)(2,1)}, bf16[2,128,1024]{2,1,0:T(8,128)(2,1)}, u32[]{:S(2)}, u32[]{:S(2)}) collective-permute-start(bf16[2,128,1024]{2,1,0:T(8,128)(2,1)} %fusion.35), channel_id=1, source_target_pairs={{0,8},{8,0},{16,24},{24,16},{1,9},{9,1},{17,25},{25,17},{2,10},{10... | collective-permute-start | bytes 1572872 | tf_op jit(solution)/shard_map/ppermute | solution.py:1278
  720.9 32.2 %collective-permute-start.44 = (bf16[2,128,1024]{2,1,0:T(8,128)(2,1)}, bf16[2,128,1024]{2,1,0:T(8,128)(2,1)}, u32[]{:S(2)}, u32[]{:S(2)}) collective-permute-start(bf16[2,128,1024]{2,1,0:T(8,128)(2,1)} %fusion.34), channel_id=1, source_target_pairs={{0,8},{8,0},{16,24},{24,16},{1,9},{9,1},{17,25},{25,17},{2,10},{10... | collective-permute-start | bytes 1572872 | tf_op jit(solution)/shard_map/ppermute | solution.py:1278
  (118 other events, 1467.4 us)
Sparse Core Ops, SparseCore 0:
  200.0 165.6 all-gather.1

commit v3 on v2

--- a/solution.py
+++ b/solution.py
@@ -1557,25 +1557,27 @@
     branch.hold(sent)
     branch.stage(("zl", "zl"))
     inner_low, inner_gain = token_sums(held_back(inner_wide, sent), own_inner)
-    inner_low, more_low = lax.optimization_barrier((by_holder(inner_low), more_low))
+    gain_sum, more_low = lax.optimization_barrier((inner_gain + gate_gain, more_low))
+    gain_sum = jnp.sum(share(gain_sum, SEQ + ("mod",)), axis=0)
+    inner_low, gain_sum = lax.optimization_barrier((by_holder(inner_low), gain_sum))
+    grad_gain = gain_sum / gain_vals
     inner_low = exchange(inner_low, SEQ).reshape(seqs, slab, MODS, channels)
     more_low = more_low.reshape(seqs, slab, 2, MODS, channels)
     grad_gate = more_low[:, :, 0].transpose(2, 1, 0, 3)
     grad_out = more_low[:, :, 1].transpose(2, 0, 3, 1)
     grad_out = grad_out.reshape(MODS, seqs * channels, slab).astype(f32)
+    step_grad_low, feat_late = held_back((step_grad_low, feat_grad), sent)
+    sent = normed_sums.stage(("y", "x"))
+    branch.hold(sent)
     branch.stage(("zh", "zh"))
-    sent = normed_sums.stage(("y", "x"))
     output = (token_vals + branch.result()).astype(bf16)
-    gain_sum, inner_low = lax.optimization_barrier((inner_gain + gate_gain, inner_low))
-    grad_gain = jnp.sum(share(gain_sum, SEQ + ("mod",)), axis=0) / gain_vals
     grad_in = jnp.stack([inner_low.transpose(2, 1, 0, 3), grad_gate], axis=2)
     grad_in = grad_in.reshape(MODS, slab, 2, seqs * channels).astype(f32)
     normed_sums.merge()
     normed_sums.stage(("zl", "zl"))
-    normed_sums.hold([grad_in, grad_gain])
+    normed_sums.hold([grad_in])
     normed_sums.stage(("zh", "zh"))
     normed_grad = normed_sums.result()
-    step_grad_low, feat_late = held_back((step_grad_low, feat_grad), sent)
     step_t = feats[:, :, :, :R].transpose(3, 1, 0, 2, 4).reshape(R, -1)
     grad_step = dot(step_t, masked(step_grad_low, ids))
     grad_step = grad_step.reshape(R, MODS, channels).transpose(1, 0, 2)

time: 807 us -> 812 us (level)
  waiting for transfers between devices: 174 us -> 165 us
    squeeze x17, local copies, waits for them, and re-layouts: 15.5 us -> 25.2 us  [taken(): return lax.dynamic_index_in_dim(values, at, dim, keepdims=False)]
    unnamed x202 -> x218, local copies, waits for them, and re-layouts: 20.9 us -> 19.3 us
  transfers between devices with their start and end apart: 61 -> 61, of which waited for: 23 -> 25; matrix products, arithmetic and copies ran while one was open for 28% -> 29% of each run, Pallas kernels for 19% -> 19%
where the time goes in v3:
time: 812 us; the launch traced here: 800 us
  Pallas kernels  202 us (25%)
  waiting for transfers between devices  165 us (20%)
  starting transfers between devices  96 us (12%)
  other arithmetic  94.3 us (12%)
  local copies, waits for them, and re-layouts  94 us (12%)
  matrix products  76.2 us (9%)
  blocking collectives  56.1 us (7%)
  between operations  16.1 us (2%)
    ppermute x52, waiting for transfers between devices, flip(): lax.ppermute(value, axis, [(i, i ^ bit) for i in range(size)])  116 us
    dot_general x17, matrix products, dot(): lax.dot_general(left, right, (((left_dim,), (right_dim,)), ((), ())), pre...  76.2 us
    pallas_call x1, Pallas kernels, scan_back(): pl.pallas_call(back_kernel, grid=(chunks,), in_specs=[pl.BlockSpec(memory...  67.4 us
    all_to_all x1, blocking collectives, share(): lax.all_to_all(jnp.broadcast_to(values, (size,) + values.shape), axes, 0, 0)  56.1 us
    ppermute x52, starting transfers between devices, flip(): lax.ppermute(value, axis, [(i, i ^ bit) for i in range(size)])  55.3 us
    pallas_call x1, Pallas kernels, scan(): pl.pallas_call(scan_kernel, grid=(length // steps,), in_specs=[pl.BlockSp...  53.7 us
    all_to_all x6, waiting for transfers between devices, exchange(): return lax.all_to_all(blocks, axes, 0, 0)  45.9 us
    all_to_all x6, starting transfers between devices, exchange(): return lax.all_to_all(blocks, axes, 0, 0)  30.4 us
  transfers between devices with their start and end apart: 61, of which 25 were waited for; matrix products, arithmetic and copies ran while one was open for 29% of the time, Pallas kernels for 19%

profile of v3, /device:TPU:0, one launch (start us, length us, event | category | flops | bytes accessed | tf_op | source)
XLA Modules:
  0.0 799.9 jit_solution(15654251902055049006)
XLA Ops:
  15.3 6.3 collective-permute-done
  25.8 5.1 collective-permute-done.1
  38.5 6.3 collective-permute-done.2
  49.9 4.6 reshape.1121
  76.6 8.9 %collective-permute-done.8 = bf16[2,2,128,512]{3,2,1,0:T(8,128)(2,1)} collective-permute-done((bf16[2,2,128,512]{3,2,1,0:T(8,128)(2,1)}, bf16[2,2,128,512]{3,2,1,0:T(8,128)(2,1)}, u32[]{:S(2)}, u32[]{:S(2)}) %collective-permute-start.8) | collective-permute-done | bytes 524320 | tf_op jit(solution)/shard_map/ppermute | solution.py:1278
  95.1 8.5 %collective-permute-done.16 = bf16[2,2,128,512]{3,2,1,0:T(8,128)(2,1)S(1)} collective-permute-done((bf16[2,2,128,512]{3,2,1,0:T(8,128)(2,1)S(1)}, bf16[2,2,128,512]{3,2,1,0:T(8,128)(2,1)S(1)}, u32[]{:S(2)}, u32[]{:S(2)}) %collective-permute-start.16) | collective-permute-done | bytes 524320 | tf_op jit(solution)/shard_map/ppermute | solution.py:1278
  106.3 18.6 %collective-permute-done.20 = bf16[2,2,128,512]{3,2,1,0:T(8,128)(2,1)S(1)} collective-permute-done((bf16[2,2,128,512]{3,2,1,0:T(8,128)(2,1)S(1)}, bf16[2,2,128,512]{3,2,1,0:T(8,128)(2,1)S(1)}, u32[]{:S(2)}, u32[]{:S(2)}) %collective-permute-start.20) | collective-permute-done | bytes 524320 | tf_op jit(solution)/shard_map/ppermute | solution.py:1278
  126.1 17.0 %all-to-all-done.refs_18_ = bf16[8,1552,128]{2,1,0:T(8,128)(2,1)S(1)} async-done(((bf16[8,1552,128]{2,1,0:T(8,128)(2,1)}), bf16[8,1552,128]{2,1,0:T(8,128)(2,1)S(1)}, u32[]{:S(2)}, u32[]{:S(2)}) %all-to-all-start) | async-done | bytes 3178528 | tf_op jit(solution)/shard_map/all_to_all | solution.py:1269
  146.7 21.4 %collective-permute-done.17.refs_9_ = bf16[2,2,2,128,512]{4,3,2,1,0:T(8,128)(2,1)} collective-permute-done((bf16[2,2,2,128,512]{4,3,2,1,0:T(8,128)(2,1)}, bf16[2,2,2,128,512]{4,3,2,1,0:T(8,128)(2,1)}, u32[]{:S(2)}, u32[]{:S(2)}) %collective-permute-start.17) | collective-permute-done | bytes 1048608 | tf_op jit(solution)/shard_map/ppermute | solution.py:1278
  173.9 26.1 %project.1 = (bf16[4096,512]{1,0:T(8,128)(2,1)}, bf16[4096,512]{1,0:T(8,128)(2,1)}, bf16[4096,512]{1,0:T(8,128)(2,1)}, bf16[4096,512]{1,0:T(8,128)(2,1)}, bf16[2...) custom-call(s32[2]{0:T(128)} %lengths.5, ...), custom_call_target="tpu_custom_call" | custom-call | bytes 3690000 | tf_op jit(solution)/shard_map/project/pallas_call | solution.py:597
  212.6 14.8 %modal_rows.1.pre = f32[4096,128]{1,0:T(8,128)} custom-call(bf16[4096,512]{1,0:T(8,128)(2,1)} %get-tuple-element.97.refs_0_, bf16[4096,512]{1,0:T(8,128)(2,1)} %get-tuple-element.98.refs_1_, bf16[4096,512]{1,0:T(8,128)(2,1)} %get-tuple-element.99.refs_2_, bf16[4096,512]{1,0:T(8,128)(2,1)} %get-tuple-element.100.refs_3_, s32[4096,1]{1,0:T(8,128)} %copy.146.refs_4_, ...), custom_call_target="tpu_custom_call" | custom-call | bytes 3690000 | tf_op jit(solution)/shard_map/modal_rows/pallas_call | solution.py:640
  227.4 5.9 side_by_side.2
  233.3 21.3 %all-to-all-done.1 = f32[16,160,128]{2,1,0:T(8,128)S(1)} async-done(((f32[16,160,128]{2,1,0:T(8,128)}), f32[16,160,128]{2,1,0:T(8,128)S(1)}, u32[]{:S(2)}, u32[]{:S(2)}) %all-to-all-start.1) | async-done | bytes 1310752 | tf_op jit(solution)/shard_map/all_to_all | solution.py:1269
  254.8 56.1 %all_to_all.46 = bf16[16,192,128]{2,1,0:T(8,128)(2,1)S(1)} all-to-all(bf16[16,192,128]{2,1,0:T(8,128)(2,1)S(1)} %broadcast_in_dim.129), channel_id=1, replica_groups=mesh['z'=4,'core'=2,'mod'=4] {'z','mod'}, dimensions={0} | all-to-all | bytes 1572864 | tf_op jit(solution)/shard_map/all_to_all | solution.py:1265
  316.2 6.8 all-to-all-start.3
  326.0 53.7 %scan.1 = (f32[32,2048,128]{2,1,0:T(8,128)}, f32[2048,128]{1,0:T(8,128)}, f32[4096,128]{1,0:T(8,128)}, f32[4096,128]{1,0:T(8,128)}, f32[4096,128]{1,0:T(8,128)},...) custom-call(s32[2]{0:T(128)} %lengths.5, s32[4096,1]{1,0:T(8,128)} %copy.144.refs_16_.ids_ref, ...), custom_call_target="tpu_custom_call" | custom-call | bytes 3690000 | tf_op jit(solution)/shard_map/scan/pallas_call | solution.py:926
  381.0 18.1 %gates.1 = (bf16[2048,384]{1,0:T(8,128)(2,1)}, f32[4096,128]{1,0:T(8,128)}, bf16[4096,384]{1,0:T(8,128)(2,1)}, bf16[4096,384]{1,0:T(8,128)(2,1)}, bf16[4096,128]{1,0:T(8,128)(2,1)}, /*index=5*/bf16[4096,128]{1,0:T(8,128)(2,1)}) custom-call(bf16[4096,2048]{1,0:T(8,128)(2,1)} %all-gather.2.cloned.1.call-done.cot, s32[4096,1]{1,0:T(8,128)} %copy.144.refs_16_.ids_ref, ...), custom_call_target="tpu_custom_call" | custom-call | bytes 3690000 | tf_op jit(solution)/shard_map/gates/pallas_call | solution.py:705
  411.6 6.0 convolution_convert_fusion
  427.2 67.4 %scan_back.1 = (f32[4096,128]{1,0:T(8,128)}, bf16[4096,128]{1,0:T(8,128)(2,1)}, f32[2,4,4,160,128]{4,3,2,1,0:T(8,128)}, f32[8,128]{1,0:T(8,128)}, f32[128,128]{1,0:T(8,128)}) custom-call(s32[3]{0:T(128)} %pad_add_fusion.place.core, s32[4096,1]{1,0:T(8,128)} %copy.144.refs_16_.ids_ref, s32[32,128]{1,0:T(8,128)} %reshape.1126.refs_17_.ids_rows, ...), custom_call_target="tpu_custom_call" | custom-call | bytes 3690000 | tf_op jit(solution)/shard_map/scan_back/pallas_call | solution.py:1134
  510.8 6.7 all-to-all-start.4
  517.5 5.6 fusion.62
  526.3 13.4 %convolution_convert_fusion.6 = bf16[2048,384]{1,0:T(8,128)(2,1)} fusion(bf16[4096,2048]{1,0:T(8,128)(2,1)} %all-gather.2.cloned.1.call-done.cot, bf16[4096,384]{1,0:T(8,128)(2,1)S(1)} %copy-done.91), kind=kOutput, calls=%fused_computation.17 | convolution fusion | flops 6443237376 | bytes 21495808 | tf_op jit(solution)/shard_map/dot_general | solution.py:479
  542.7 6.7 all-to-all-start.5
  549.4 4.7 fusion.60
  574.8 11.9 %conv_back.1 = (bf16[4096,384]{1,0:T(8,128)(2,1)}, bf16[4096,128]{1,0:T(8,128)(2,1)}, f32[8,128]{1,0:T(8,128)}) custom-call(s32[2]{0:T(128)} %lengths.5, s32[4096,1]{1,0:T(8,128)} %copy.144.refs_16_.ids_ref, bf16[2,4,4,160,128]{4,3,2,1,0:T(8,128)(2,1)} %maximum_select_fusion.1.feat_grad, f32[4096,128]{1,0:T(8,128)} %get-tuple-element.133.act_part, ...), custom_call_target="tpu_custom_call" | custom-call | bytes 3690000 | tf_op jit(solution)/shard_map/conv_back/pallas_call | solution.py:1230
  589.2 4.6 all-to-all-start.6
  647.6 5.0 multiply_reduce_fusion.7
  691.0 4.6 copy.175
  722.2 5.8 collective-permute-done.44
  743.6 9.4 %collective-permute-done.50 = bf16[2,128,1024]{2,1,0:T(8,128)(2,1)} collective-permute-done((bf16[2,128,1024]{2,1,0:T(8,128)(2,1)}, bf16[2,128,1024]{2,1,0:T(8,128)(2,1)}, u32[]{:S(2)}, u32[]{:S(2)}) %collective-permute-start.50) | collective-permute-done | bytes 524320 | tf_op jit(solution)/shard_map/ppermute | solution.py:1278
  753.1 9.1 %collective-permute-done.46 = bf16[2,128,1024]{2,1,0:T(8,128)(2,1)} collective-permute-done((bf16[2,128,1024]{2,1,0:T(8,128)(2,1)}, bf16[2,128,1024]{2,1,0:T(8,128)(2,1)}, u32[]{:S(2)}, u32[]{:S(2)}) %collective-permute-start.46) | collective-permute-done | bytes 524320 | tf_op jit(solution)/shard_map/ppermute | solution.py:1278
  768.8 10.3 %copy.178 = f32[3,256,2,1024]{3,2,1,0:T(2,128)} copy(f32[3,256,2,1024]{1,3,0,2:T(8,128)} %maximum_convert_fusion) | data formatting | bytes 12582912
  (481 shorter events, 313.3 us)
Async XLA Ops:
  67.3 75.8 %all-to-all-start = ((bf16[8,1552,128]{2,1,0:T(8,128)(2,1)}), bf16[8,1552,128]{2,1,0:T(8,128)(2,1)S(1)}, u32[]{:S(2)}, u32[]{:S(2)}) async-start(bf16[8,1552,128]{2,1,0:T(8,128)(2,1)} %pad_maximum_fusion), calls=%async_computation | async-start | bytes 6356992 | tf_op jit(solution)/shard_map/all_to_all | solution.py:1269
  70.9 308.8 %all-gather.2.cloned.1.call-start = ((), (), s32[]{:S(2)}) async-start(), calls=%async_computation.9 | async-start | bytes 17301504 | tf_op jit(solution)/shard_map/all_gather | solution.py:1467
  87.8 55.3 %collective-permute-start.10 = (bf16[2,2,2,128,512]{4,3,2,1,0:T(8,128)(2,1)}, bf16[2,2,2,128,512]{4,3,2,1,0:T(8,128)(2,1)}, u32[]{:S(2)}, u32[]{:S(2)}) collective-permute-start(bf16[2,2,2,128,512]{4,3,2,1,0:T(8,128)(2,1)} %maximum_select_fusion.2.refs_0_), channel_id=1, source_target_pairs={{0,4},{4,0},{1,5},{5,1},{2,6},{6,2},{3,7},{7,3},{8,12},{12,8},{9,1... | collective-permute-start | bytes 3145736 | tf_op jit(solution)/shard_map/ppermute | solution.py:1278
  87.8 56.8 %collective-permute-start.9 = (bf16[2,2,2,128,512]{4,3,2,1,0:T(8,128)(2,1)}, bf16[2,2,2,128,512]{4,3,2,1,0:T(8,128)(2,1)}, u32[]{:S(2)}, u32[]{:S(2)}) collective-permute-start(bf16[2,2,2,128,512]{4,3,2,1,0:T(8,128)(2,1)} %maximum_select_fusion.2.refs_0_), channel_id=1, source_target_pairs={{0,2},{1,3},{2,0},{3,1},{4,6},{5,7},{6,4},{7,5},{8,10},{9,11},{10,... | collective-permute-start | bytes 3145736 | tf_op jit(solution)/shard_map/ppermute | solution.py:1278
  92.1 32.7 %collective-permute-start.20 = (bf16[2,2,128,512]{3,2,1,0:T(8,128)(2,1)S(1)}, bf16[2,2,128,512]{3,2,1,0:T(8,128)(2,1)S(1)}, u32[]{:S(2)}, u32[]{:S(2)}) collective-permute-start(bf16[2,2,128,512]{3,2,1,0:T(8,128)(2,1)S(1)} %copy-done.71), channel_id=1, source_target_pairs={{0,2},{1,3},{2,0},{3,1},{4,6},{5,7},{6,4},{7,5},{8,10},{9,11},{10,... | collective-permute-start | bytes 1572872 | tf_op jit(solution)/shard_map/ppermute | solution.py:1278
  95.0 51.1 %collective-permute-start.14 = (bf16[2,2,2,128,512]{4,3,2,1,0:T(8,128)(2,1)}, bf16[2,2,2,128,512]{4,3,2,1,0:T(8,128)(2,1)}, u32[]{:S(2)}, u32[]{:S(2)}) collective-permute-start(bf16[2,2,2,128,512]{4,3,2,1,0:T(8,128)(2,1)} %maximum_select_fusion.3.refs_4_), channel_id=1, source_target_pairs={{0,4},{4,0},{1,5},{5,1},{2,6},{6,2},{3,7},{7,3},{8,12},{12,8},{9,1... | collective-permute-start | bytes 3145736 | tf_op jit(solution)/shard_map/ppermute | solution.py:1278
  103.6 42.6 %collective-permute-start.13 = (bf16[2,2,2,128,512]{4,3,2,1,0:T(8,128)(2,1)}, bf16[2,2,2,128,512]{4,3,2,1,0:T(8,128)(2,1)}, u32[]{:S(2)}, u32[]{:S(2)}) collective-permute-start(bf16[2,2,2,128,512]{4,3,2,1,0:T(8,128)(2,1)} %maximum_select_fusion.3.refs_4_), channel_id=1, source_target_pairs={{0,1},{1,0},{2,3},{3,2},{4,5},{5,4},{6,7},{7,6},{8,9},{9,8},{10,11... | collective-permute-start | bytes 3145736 | tf_op jit(solution)/shard_map/ppermute | solution.py:1278
  143.1 25.0 %collective-permute-start.17 = (bf16[2,2,2,128,512]{4,3,2,1,0:T(8,128)(2,1)}, bf16[2,2,2,128,512]{4,3,2,1,0:T(8,128)(2,1)}, u32[]{:S(2)}, u32[]{:S(2)}) collective-permute-start(bf16[2,2,2,128,512]{4,3,2,1,0:T(8,128)(2,1)} %maximum_select_fusion.4.refs_8_), channel_id=1, source_target_pairs={{0,2},{1,3},{2,0},{3,1},{4,6},{5,7},{6,4},{7,5},{8,10},{9,11},{10,... | collective-permute-start | bytes 3145736 | tf_op jit(solution)/shard_map/ppermute | solution.py:1278
  144.6 24.7 %collective-permute-start.21 = (bf16[2,2,2,128,512]{4,3,2,1,0:T(8,128)(2,1)}, bf16[2,2,2,128,512]{4,3,2,1,0:T(8,128)(2,1)}, u32[]{:S(2)}, u32[]{:S(2)}) collective-permute-start(bf16[2,2,2,128,512]{4,3,2,1,0:T(8,128)(2,1)} %maximum_select_fusion.5.refs_12_), channel_id=1, source_target_pairs={{0,1},{1,0},{2,3},{3,2},{4,5},{5,4},{6,7},{7,6},{8,9},{9,8},{10,11... | collective-permute-start | bytes 3145736 | tf_op jit(solution)/shard_map/ppermute | solution.py:1278
  146.1 27.7 %collective-permute-start.22 = (bf16[2,2,2,128,512]{4,3,2,1,0:T(8,128)(2,1)}, bf16[2,2,2,128,512]{4,3,2,1,0:T(8,128)(2,1)}, u32[]{:S(2)}, u32[]{:S(2)}) collective-permute-start(bf16[2,2,2,128,512]{4,3,2,1,0:T(8,128)(2,1)} %maximum_select_fusion.5.refs_12_), channel_id=1, source_target_pairs={{0,4},{4,0},{1,5},{5,1},{2,6},{6,2},{3,7},{7,3},{8,12},{12,8},{9,1... | collective-permute-start | bytes 3145736 | tf_op jit(solution)/shard_map/ppermute | solution.py:1278
  146.1 27.7 %collective-permute-start.11 = (bf16[2,2,2,128,512]{4,3,2,1,0:T(8,128)(2,1)}, bf16[2,2,2,128,512]{4,3,2,1,0:T(8,128)(2,1)}, u32[]{:S(2)}, u32[]{:S(2)}) collective-permute-start(bf16[2,2,2,128,512]{4,3,2,1,0:T(8,128)(2,1)} %collective-permute-done.9.refs_1_), channel_id=1, source_target_pairs={{0,4},{4,0},{1,5},{5,1},{2,6},{6,2},{3,7},{7,3},{8,12},{12,8},{9,1... | collective-permute-start | bytes 3145736 | tf_op jit(solution)/shard_map/ppermute | solution.py:1278
  146.7 27.2 %collective-permute-start.15 = (bf16[2,2,2,128,512]{4,3,2,1,0:T(8,128)(2,1)}, bf16[2,2,2,128,512]{4,3,2,1,0:T(8,128)(2,1)}, u32[]{:S(2)}, u32[]{:S(2)}) collective-permute-start(bf16[2,2,2,128,512]{4,3,2,1,0:T(8,128)(2,1)} %collective-permute-done.13.refs_5_), channel_id=1, source_target_pairs={{0,4},{4,0},{1,5},{5,1},{2,6},{6,2},{3,7},{7,3},{8,12},{12,8},{9,1... | collective-permute-start | bytes 3145736 | tf_op jit(solution)/shard_map/ppermute | solution.py:1278
  206.0 48.6 %all-to-all-start.1 = ((f32[16,160,128]{2,1,0:T(8,128)}), f32[16,160,128]{2,1,0:T(8,128)S(1)}, u32[]{:S(2)}, u32[]{:S(2)}) async-start(f32[16,160,128]{2,1,0:T(8,128)} %bitcast.345), calls=%async_computation.1 | async-start | bytes 2621440 | tf_op jit(solution)/shard_map/all_to_all | solution.py:1269
  316.2 63.5 %all-to-all-start.3 = ((bf16[8,768,128]{2,1,0:T(8,128)(2,1)}), bf16[8,768,128]{2,1,0:T(8,128)(2,1)S(1)}, u32[]{:S(2)}, u32[]{:S(2)}) async-start(bf16[8,768,128]{2,1,0:T(8,128)(2,1)} %bitcast.43), calls=%async_computation.3 | async-start | bytes 3145728 | tf_op jit(solution)/shard_map/all_to_all | solution.py:1269
  423.2 71.3 %collective-permute-start.30 = (bf16[2,2,2,128,1024]{4,3,1,0,2:T(8,128)(2,1)}, bf16[2,2,2,128,1024]{4,3,1,0,2:T(8,128)(2,1)}, u32[]{:S(2)}, u32[]{:S(2)}) collective-permute-start(bf16[2,2,2,128,1024]{4,3,1,0,2:T(8,128)(2,1)} %copy_bitcast_fusion.1), channel_id=1, source_target_pairs={{0,1},{1,0},{2,3},{3,2},{4,5},{5,4},{6,7},{7,6},{8,9},{9,8},{10,11... | collective-permute-start | bytes 6291464 | tf_op jit(solution)/shard_map/ppermute | solution.py:1278
  426.4 68.2 %collective-permute-start.31 = (bf16[2,2,2,128,1024]{4,3,1,0,2:T(8,128)(2,1)}, bf16[2,2,2,128,1024]{4,3,1,0,2:T(8,128)(2,1)}, u32[]{:S(2)}, u32[]{:S(2)}) collective-permute-start(bf16[2,2,2,128,1024]{4,3,1,0,2:T(8,128)(2,1)} %copy_bitcast_fusion), channel_id=1, source_target_pairs={{0,2},{1,3},{2,0},{3,1},{4,6},{5,7},{6,4},{7,5},{8,10},{9,11},{10,... | collective-permute-start | bytes 6291464 | tf_op jit(solution)/shard_map/ppermute | solution.py:1278
  503.7 85.5 %collective-permute-start.32 = (bf16[2,2,128,1024]{3,2,1,0:T(8,128)(2,1)}, bf16[2,2,128,1024]{3,2,1,0:T(8,128)(2,1)}, u32[]{:S(2)}, u32[]{:S(2)}) collective-permute-start(bf16[2,2,128,1024]{3,2,1,0:T(8,128)(2,1)} %fusion.7), channel_id=1, source_target_pairs={{0,2},{1,3},{2,0},{3,1},{4,6},{5,7},{6,4},{7,5},{8,10},{9,11},{10,... | collective-permute-start | bytes 3145736 | tf_op jit(solution)/shard_map/ppermute | solution.py:1278
  508.0 66.9 %collective-permute-start.35 = (bf16[2,2,128,1024]{3,2,1,0:T(8,128)(2,1)}, bf16[2,2,128,1024]{3,2,1,0:T(8,128)(2,1)}, u32[]{:S(2)}, u32[]{:S(2)}) collective-permute-start(bf16[2,2,128,1024]{3,2,1,0:T(8,128)(2,1)} %fusion.6), channel_id=1, source_target_pairs={{0,1},{1,0},{2,3},{3,2},{4,5},{5,4},{6,7},{7,6},{8,9},{9,8},{10,11... | collective-permute-start | bytes 3145736 | tf_op jit(solution)/shard_map/ppermute | solution.py:1278
  510.8 29.8 %all-to-all-start.4 = ((bf16[16,160,128]{2,1,0:T(8,128)(2,1)}), bf16[16,160,128]{2,1,0:T(8,128)(2,1)}, u32[]{:S(2)}, u32[]{:S(2)}) async-start(bf16[16,160,128]{2,1,0:T(8,128)(2,1)} %bitcast.355), calls=%async_computation.4 | async-start | bytes 1310720 | tf_op jit(solution)/shard_map/all_to_all | solution.py:1269
  542.7 23.6 %all-to-all-start.5 = ((bf16[16,160,128]{2,1,0:T(8,128)(2,1)}), bf16[16,160,128]{2,1,0:T(8,128)(2,1)}, u32[]{:S(2)}, u32[]{:S(2)}) async-start(bf16[16,160,128]{2,1,0:T(8,128)(2,1)} %broadcast_in_dim.134), calls=%async_computation.5 | async-start | bytes 1310720 | tf_op jit(solution)/shard_map/all_to_all | solution.py:1265
  589.2 76.3 %all-to-all-start.6 = ((bf16[8,256,768]{1,2,0:T(8,128)(2,1)}), bf16[8,256,768]{1,2,0:T(8,128)(2,1)}, u32[]{:S(2)}, u32[]{:S(2)}) async-start(bf16[8,256,768]{1,2,0:T(8,128)(2,1)} %pad_maximum_fusion.1), calls=%async_computation.6 | async-start | bytes 6291456 | tf_op jit(solution)/shard_map/all_to_all | solution.py:1269
  620.7 78.9 %collective-permute-start.42 = (bf16[2,2,2,128,512]{4,3,1,0,2:T(8,128)(2,1)}, bf16[2,2,2,128,512]{4,3,1,0,2:T(8,128)(2,1)}, u32[]{:S(2)}, u32[]{:S(2)}) collective-permute-start(bf16[2,2,2,128,512]{4,3,1,0,2:T(8,128)(2,1)} %copy_bitcast_fusion.2), channel_id=1, source_target_pairs={{0,2},{1,3},{2,0},{3,1},{4,6},{5,7},{6,4},{7,5},{8,10},{9,11},{10,... | collective-permute-start | bytes 3145736 | tf_op jit(solution)/shard_map/ppermute | solution.py:1278
  623.2 77.9 %collective-permute-start.41 = (bf16[2,2,2,128,512]{4,3,1,0,2:T(8,128)(2,1)}, bf16[2,2,2,128,512]{4,3,1,0,2:T(8,128)(2,1)}, u32[]{:S(2)}, u32[]{:S(2)}) collective-permute-start(bf16[2,2,2,128,512]{4,3,1,0,2:T(8,128)(2,1)} %copy_bitcast_fusion.3), channel_id=1, source_target_pairs={{0,1},{1,0},{2,3},{3,2},{4,5},{5,4},{6,7},{7,6},{8,9},{9,8},{10,11... | collective-permute-start | bytes 3145736 | tf_op jit(solution)/shard_map/ppermute | solution.py:1278
  626.7 77.1 %collective-permute-start.39 = (bf16[2,2,2,128,512]{4,3,1,0,2:T(8,128)(2,1)}, bf16[2,2,2,128,512]{4,3,1,0,2:T(8,128)(2,1)}, u32[]{:S(2)}, u32[]{:S(2)}) collective-permute-start(bf16[2,2,2,128,512]{4,3,1,0,2:T(8,128)(2,1)} %copy_bitcast_fusion.5), channel_id=1, source_target_pairs={{0,1},{1,0},{2,3},{3,2},{4,5},{5,4},{6,7},{7,6},{8,9},{9,8},{10,11... | collective-permute-start | bytes 3145736 | tf_op jit(solution)/shard_map/ppermute | solution.py:1278
  627.3 78.6 %collective-permute-start.40 = (bf16[2,2,2,128,512]{4,3,1,0,2:T(8,128)(2,1)}, bf16[2,2,2,128,512]{4,3,1,0,2:T(8,128)(2,1)}, u32[]{:S(2)}, u32[]{:S(2)}) collective-permute-start(bf16[2,2,2,128,512]{4,3,1,0,2:T(8,128)(2,1)} %copy_bitcast_fusion.4), channel_id=1, source_target_pairs={{0,2},{1,3},{2,0},{3,1},{4,6},{5,7},{6,4},{7,5},{8,10},{9,11},{10,... | collective-permute-start | bytes 3145736 | tf_op jit(solution)/shard_map/ppermute | solution.py:1278
  636.4 73.0 %collective-permute-start.38 = (bf16[2,128,2048]{2,1,0:T(8,128)(2,1)}, bf16[2,128,2048]{2,1,0:T(8,128)(2,1)}, u32[]{:S(2)}, u32[]{:S(2)}) collective-permute-start(bf16[2,128,2048]{2,1,0:T(8,128)(2,1)} %fusion.25), channel_id=1, source_target_pairs={{0,8},{8,0},{16,24},{24,16},{1,9},{9,1},{17,25},{25,17},{2,10},{10... | collective-permute-start | bytes 3145736 | tf_op jit(solution)/shard_map/ppermute | solution.py:1278
  684.5 54.2 %all-to-all-start.8 = ((bf16[8,256,384]{1,2,0:T(8,128)(2,1)}), bf16[8,256,384]{1,2,0:T(8,128)(2,1)}, u32[]{:S(2)}, u32[]{:S(2)}) async-start(bf16[8,256,384]{1,2,0:T(8,128)(2,1)} %copy.170), calls=%async_computation.8 | async-start | bytes 3145728 | tf_op jit(solution)/shard_map/all_to_all | solution.py:1269
  705.2 22.8 %collective-permute-start.44 = (bf16[2,2,128,512]{3,2,1,0:T(8,128)(2,1)S(1)}, bf16[2,2,128,512]{3,2,1,0:T(8,128)(2,1)S(1)}, u32[]{:S(2)}, u32[]{:S(2)}) collective-permute-start(bf16[2,2,128,512]{3,2,1,0:T(8,128)(2,1)S(1)} %fusion.33), channel_id=1, source_target_pairs={{0,2},{1,3},{2,0},{3,1},{4,6},{5,7},{6,4},{7,5},{8,10},{9,11},{10,... | collective-permute-start | bytes 1572872 | tf_op jit(solution)/shard_map/ppermute | solution.py:1278
  711.7 77.6 %collective-permute-start.43 = (bf16[128,2048]{1,0:T(8,128)(2,1)}, bf16[128,2048]{1,0:T(8,128)(2,1)}, u32[]{:S(2)}, u32[]{:S(2)}) collective-permute-start(bf16[128,2048]{1,0:T(8,128)(2,1)} %fusion.28), channel_id=1, source_target_pairs={{0,16},{8,24},{16,0},{24,8},{1,17},{9,25},{17,1},{25,9},{2,18},{10... | collective-permute-start | bytes 1572872 | tf_op jit(solution)/shard_map/ppermute | solution.py:1278
  720.7 32.3 %collective-permute-start.50 = (bf16[2,128,1024]{2,1,0:T(8,128)(2,1)}, bf16[2,128,1024]{2,1,0:T(8,128)(2,1)}, u32[]{:S(2)}, u32[]{:S(2)}) collective-permute-start(bf16[2,128,1024]{2,1,0:T(8,128)(2,1)} %fusion.35), channel_id=1, source_target_pairs={{0,8},{8,0},{16,24},{24,16},{1,9},{9,1},{17,25},{25,17},{2,10},{10... | collective-permute-start | bytes 1572872 | tf_op jit(solution)/shard_map/ppermute | solution.py:1278
  729.4 32.8 %collective-permute-start.46 = (bf16[2,128,1024]{2,1,0:T(8,128)(2,1)}, bf16[2,128,1024]{2,1,0:T(8,128)(2,1)}, u32[]{:S(2)}, u32[]{:S(2)}) collective-permute-start(bf16[2,128,1024]{2,1,0:T(8,128)(2,1)} %fusion.34), channel_id=1, source_target_pairs={{0,8},{8,0},{16,24},{24,16},{1,9},{9,1},{17,25},{25,17},{2,10},{10... | collective-permute-start | bytes 1572872 | tf_op jit(solution)/shard_map/ppermute | solution.py:1278
  765.2 22.4 %collective-permute-start.47 = (bf16[128,1024]{1,0:T(8,128)(2,1)S(1)}, bf16[128,1024]{1,0:T(8,128)(2,1)}, u32[]{:S(2)}, u32[]{:S(2)}) collective-permute-start(bf16[128,1024]{1,0:T(8,128)(2,1)S(1)} %fusion.46), channel_id=1, source_target_pairs={{0,16},{8,24},{16,0},{24,8},{1,17},{9,25},{17,1},{25,9},{2,18},{10... | collective-permute-start | bytes 786440 | tf_op jit(solution)/shard_map/ppermute | solution.py:1278
  (126 other events, 1542.0 us)
Sparse Core Ops, SparseCore 0:
  200.1 165.2 all-gather.1

commit v4 on v2

--- a/solution.py
+++ b/solution.py
@@ -1558,24 +1558,28 @@
     branch.stage(("zl", "zl"))
     inner_low, inner_gain = token_sums(held_back(inner_wide, sent), own_inner)
     inner_low, more_low = lax.optimization_barrier((by_holder(inner_low), more_low))
-    inner_low = exchange(inner_low, SEQ).reshape(seqs, slab, MODS, channels)
+    inner_low = exchange(inner_low, SEQ)
+    step_grad_low = held_back(step_grad_low, sent)
+    sent = normed_sums.stage(("y", "x"))
+    branch.hold(sent)
+    branch.stage(("zh", "zh"))
+    output = (token_vals + branch.result()).astype(bf16)
+    gain_sum = held_back(inner_gain + gate_gain, sent)
+    gain_sum, inner_low = lax.optimization_barrier((gain_sum, inner_low))
+    grad_gain = jnp.sum(share(gain_sum, SEQ + ("mod",)), axis=0) / gain_vals
+    inner_low = inner_low.reshape(seqs, slab, MODS, channels)
     more_low = more_low.reshape(seqs, slab, 2, MODS, channels)
     grad_gate = more_low[:, :, 0].transpose(2, 1, 0, 3)
-    grad_out = more_low[:, :, 1].transpose(2, 0, 3, 1)
-    grad_out = grad_out.reshape(MODS, seqs * channels, slab).astype(f32)
-    branch.stage(("zh", "zh"))
-    sent = normed_sums.stage(("y", "x"))
-    output = (token_vals + branch.result()).astype(bf16)
-    gain_sum, inner_low = lax.optimization_barrier((inner_gain + gate_gain, inner_low))
-    grad_gain = jnp.sum(share(gain_sum, SEQ + ("mod",)), axis=0) / gain_vals
     grad_in = jnp.stack([inner_low.transpose(2, 1, 0, 3), grad_gate], axis=2)
     grad_in = grad_in.reshape(MODS, slab, 2, seqs * channels).astype(f32)
     normed_sums.merge()
-    normed_sums.stage(("zl", "zl"))
+    sent = normed_sums.stage(("zl", "zl"))
+    feat_late, out_low = held_back((feat_grad, more_low[:, :, 1]), sent)
+    grad_out = out_low.transpose(2, 0, 3, 1)
+    grad_out = grad_out.reshape(MODS, seqs * channels, slab).astype(f32)
     normed_sums.hold([grad_in, grad_gain])
     normed_sums.stage(("zh", "zh"))
     normed_grad = normed_sums.result()
-    step_grad_low, feat_late = held_back((step_grad_low, feat_grad), sent)
     step_t = feats[:, :, :, :R].transpose(3, 1, 0, 2, 4).reshape(R, -1)
     grad_step = dot(step_t, masked(step_grad_low, ids))
     grad_step = grad_step.reshape(R, MODS, channels).transpose(1, 0, 2)

time: 807 us -> 807 us (level)
  waiting for transfers between devices: 174 us -> 159 us
  local copies, waits for them, and re-layouts: 86.7 us -> 97.9 us
    ppermute x52, waiting for transfers between devices: 116 us -> 94.6 us  [flip(): lax.ppermute(value, axis, [(i, i ^ bit) for i in range(size)])]
    all_to_all x6, waiting for transfers between devices: 48.6 us -> 56.7 us  [exchange(): return lax.all_to_all(blocks, axes, 0, 0)]
    unnamed x202 -> x210, local copies, waits for them, and re-layouts: 20.9 us -> 21.1 us
  transfers between devices with their start and end apart: 61 -> 61, of which waited for: 23 -> 22; matrix products, arithmetic and copies ran while one was open for 28% -> 30% of each run, Pallas kernels for 19% -> 19%
where the time goes in v4:
time: 807 us; the launch traced here: 795 us
  Pallas kernels  202 us (25%)
  waiting for transfers between devices  159 us (20%)
  local copies, waits for them, and re-layouts  97.9 us (12%)
  starting transfers between devices  94.5 us (12%)
  other arithmetic  93 us (12%)
  matrix products  76.3 us (9%)
  blocking collectives  56.1 us (7%)
  between operations  16.2 us (2%)
    ppermute x52, waiting for transfers between devices, flip(): lax.ppermute(value, axis, [(i, i ^ bit) for i in range(size)])  94.6 us
    dot_general x17, matrix products, dot(): lax.dot_general(left, right, (((left_dim,), (right_dim,)), ((), ())), pre...  76.3 us
    pallas_call x1, Pallas kernels, scan_back(): pl.pallas_call(back_kernel, grid=(chunks,), in_specs=[pl.BlockSpec(memory...  67.4 us
    all_to_all x6, waiting for transfers between devices, exchange(): return lax.all_to_all(blocks, axes, 0, 0)  56.7 us
    all_to_all x1, blocking collectives, share(): lax.all_to_all(jnp.broadcast_to(values, (size,) + values.shape), axes, 0, 0)  56.1 us
    ppermute x52, starting transfers between devices, flip(): lax.ppermute(value, axis, [(i, i ^ bit) for i in range(size)])  53.9 us
    pallas_call x1, Pallas kernels, scan(): pl.pallas_call(scan_kernel, grid=(length // steps,), in_specs=[pl.BlockSp...  53.7 us
    all_to_all x6, starting transfers between devices, exchange(): return lax.all_to_all(blocks, axes, 0, 0)  31.3 us
  transfers between devices with their start and end apart: 61, of which 22 were waited for; matrix products, arithmetic and copies ran while one was open for 30% of the time, Pallas kernels for 19%

profile of v4, /device:TPU:0, one launch (start us, length us, event | category | flops | bytes accessed | tf_op | source)
XLA Modules:
  0.0 795.4 jit_solution(9799208340603916201)
XLA Ops:
  15.3 6.3 collective-permute-done
  25.8 5.1 collective-permute-done.1
  38.5 6.3 collective-permute-done.2
  76.6 8.9 %collective-permute-done.8 = bf16[2,2,128,512]{3,2,1,0:T(8,128)(2,1)} collective-permute-done((bf16[2,2,128,512]{3,2,1,0:T(8,128)(2,1)}, bf16[2,2,128,512]{3,2,1,0:T(8,128)(2,1)}, u32[]{:S(2)}, u32[]{:S(2)}) %collective-permute-start.8) | collective-permute-done | bytes 524320 | tf_op jit(solution)/shard_map/ppermute | solution.py:1278
  95.1 8.5 %collective-permute-done.16 = bf16[2,2,128,512]{3,2,1,0:T(8,128)(2,1)S(1)} collective-permute-done((bf16[2,2,128,512]{3,2,1,0:T(8,128)(2,1)S(1)}, bf16[2,2,128,512]{3,2,1,0:T(8,128)(2,1)S(1)}, u32[]{:S(2)}, u32[]{:S(2)}) %collective-permute-start.16) | collective-permute-done | bytes 524320 | tf_op jit(solution)/shard_map/ppermute | solution.py:1278
  106.3 18.6 %collective-permute-done.20 = bf16[2,2,128,512]{3,2,1,0:T(8,128)(2,1)S(1)} collective-permute-done((bf16[2,2,128,512]{3,2,1,0:T(8,128)(2,1)S(1)}, bf16[2,2,128,512]{3,2,1,0:T(8,128)(2,1)S(1)}, u32[]{:S(2)}, u32[]{:S(2)}) %collective-permute-start.20) | collective-permute-done | bytes 524320 | tf_op jit(solution)/shard_map/ppermute | solution.py:1278
  126.1 17.0 %all-to-all-done.refs_18_ = bf16[8,1552,128]{2,1,0:T(8,128)(2,1)S(1)} async-done(((bf16[8,1552,128]{2,1,0:T(8,128)(2,1)}), bf16[8,1552,128]{2,1,0:T(8,128)(2,1)S(1)}, u32[]{:S(2)}, u32[]{:S(2)}) %all-to-all-start) | async-done | bytes 3178528 | tf_op jit(solution)/shard_map/all_to_all | solution.py:1269
  146.7 21.4 %collective-permute-done.17.refs_9_ = bf16[2,2,2,128,512]{4,3,2,1,0:T(8,128)(2,1)} collective-permute-done((bf16[2,2,2,128,512]{4,3,2,1,0:T(8,128)(2,1)}, bf16[2,2,2,128,512]{4,3,2,1,0:T(8,128)(2,1)}, u32[]{:S(2)}, u32[]{:S(2)}) %collective-permute-start.17) | collective-permute-done | bytes 1048608 | tf_op jit(solution)/shard_map/ppermute | solution.py:1278
  173.8 26.1 %project.1 = (bf16[4096,512]{1,0:T(8,128)(2,1)}, bf16[4096,512]{1,0:T(8,128)(2,1)}, bf16[4096,512]{1,0:T(8,128)(2,1)}, bf16[4096,512]{1,0:T(8,128)(2,1)}, bf16[2...) custom-call(s32[2]{0:T(128)} %lengths.5, ...), custom_call_target="tpu_custom_call" | custom-call | bytes 3690000 | tf_op jit(solution)/shard_map/project/pallas_call | solution.py:597
  212.6 14.8 %modal_rows.1.pre = f32[4096,128]{1,0:T(8,128)} custom-call(bf16[4096,512]{1,0:T(8,128)(2,1)} %get-tuple-element.99.refs_0_, bf16[4096,512]{1,0:T(8,128)(2,1)} %get-tuple-element.100.refs_1_, bf16[4096,512]{1,0:T(8,128)(2,1)} %get-tuple-element.101.refs_2_, bf16[4096,512]{1,0:T(8,128)(2,1)} %get-tuple-element.102.refs_3_, s32[4096,1]{1,0:T(8,128)} %copy.146.refs_4_, ...), custom_call_target="tpu_custom_call" | custom-call | bytes 3690000 | tf_op jit(solution)/shard_map/modal_rows/pallas_call | solution.py:640
  227.3 5.9 side_by_side.2
  233.2 21.3 %all-to-all-done.1 = f32[16,160,128]{2,1,0:T(8,128)S(1)} async-done(((f32[16,160,128]{2,1,0:T(8,128)}), f32[16,160,128]{2,1,0:T(8,128)S(1)}, u32[]{:S(2)}, u32[]{:S(2)}) %all-to-all-start.1) | async-done | bytes 1310752 | tf_op jit(solution)/shard_map/all_to_all | solution.py:1269
  254.8 56.1 %all_to_all.46 = bf16[16,192,128]{2,1,0:T(8,128)(2,1)S(1)} all-to-all(bf16[16,192,128]{2,1,0:T(8,128)(2,1)S(1)} %broadcast_in_dim.129), channel_id=1, replica_groups=mesh['z'=4,'core'=2,'mod'=4] {'z','mod'}, dimensions={0} | all-to-all | bytes 1572864 | tf_op jit(solution)/shard_map/all_to_all | solution.py:1265
  316.1 6.9 all-to-all-start.3
  325.9 53.7 %scan.1 = (f32[32,2048,128]{2,1,0:T(8,128)}, f32[2048,128]{1,0:T(8,128)}, f32[4096,128]{1,0:T(8,128)}, f32[4096,128]{1,0:T(8,128)}, f32[4096,128]{1,0:T(8,128)},...) custom-call(s32[2]{0:T(128)} %lengths.5, s32[4096,1]{1,0:T(8,128)} %copy.144.refs_16_.ids_ref, ...), custom_call_target="tpu_custom_call" | custom-call | bytes 3690000 | tf_op jit(solution)/shard_map/scan/pallas_call | solution.py:926
  380.9 18.1 %gates.1 = (bf16[2048,384]{1,0:T(8,128)(2,1)}, f32[4096,128]{1,0:T(8,128)}, bf16[4096,384]{1,0:T(8,128)(2,1)}, bf16[4096,384]{1,0:T(8,128)(2,1)}, bf16[4096,128]{1,0:T(8,128)(2,1)}, /*index=5*/bf16[4096,128]{1,0:T(8,128)(2,1)}) custom-call(bf16[4096,2048]{1,0:T(8,128)(2,1)} %all-gather.2.cloned.1.call-done.cot, s32[4096,1]{1,0:T(8,128)} %copy.144.refs_16_.ids_ref, ...), custom_call_target="tpu_custom_call" | custom-call | bytes 3690000 | tf_op jit(solution)/shard_map/gates/pallas_call | solution.py:705
  411.5 6.0 convolution_convert_fusion
  427.1 67.4 %scan_back.1 = (f32[4096,128]{1,0:T(8,128)}, bf16[4096,128]{1,0:T(8,128)(2,1)}, f32[2,4,4,160,128]{4,3,2,1,0:T(8,128)}, f32[8,128]{1,0:T(8,128)}, f32[128,128]{1,0:T(8,128)}) custom-call(s32[3]{0:T(128)} %pad_add_fusion.place.core, s32[4096,1]{1,0:T(8,128)} %copy.144.refs_16_.ids_ref, s32[32,128]{1,0:T(8,128)} %reshape.1124.refs_17_.ids_rows, ...), custom_call_target="tpu_custom_call" | custom-call | bytes 3690000 | tf_op jit(solution)/shard_map/scan_back/pallas_call | solution.py:1134
  510.7 6.7 all-to-all-start.4
  517.4 5.6 fusion.62
  526.2 13.4 %convolution_convert_fusion.6 = bf16[2048,384]{1,0:T(8,128)(2,1)} fusion(bf16[4096,2048]{1,0:T(8,128)(2,1)} %all-gather.2.cloned.1.call-done.cot, bf16[4096,384]{1,0:T(8,128)(2,1)S(1)} %copy-done.88), kind=kOutput, calls=%fused_computation.17 | convolution fusion | flops 6443237376 | bytes 21495808 | tf_op jit(solution)/shard_map/dot_general | solution.py:479
  542.6 6.7 all-to-all-start.5
  549.3 4.7 fusion.60
  574.7 11.9 %conv_back.1 = (bf16[4096,384]{1,0:T(8,128)(2,1)}, bf16[4096,128]{1,0:T(8,128)(2,1)}, f32[8,128]{1,0:T(8,128)}) custom-call(s32[2]{0:T(128)} %lengths.5, s32[4096,1]{1,0:T(8,128)} %copy.144.refs_16_.ids_ref, bf16[2,4,4,160,128]{4,3,2,1,0:T(8,128)(2,1)} %maximum_select_fusion.1.feat_grad, f32[4096,128]{1,0:T(8,128)} %get-tuple-element.135.act_part, ...), custom_call_target="tpu_custom_call" | custom-call | bytes 3690000 | tf_op jit(solution)/shard_map/conv_back/pallas_call | solution.py:1230
  589.1 4.6 all-to-all-start.6
  635.1 5.0 copy.175
  642.0 5.7 fusion.65
  678.6 5.4 all-to-all-start.7
  716.2 17.5 %all-to-all-done.7 = bf16[8,256,384]{1,2,0:T(8,128)(2,1)} async-done(((bf16[8,256,384]{1,2,0:T(8,128)(2,1)}), bf16[8,256,384]{1,2,0:T(8,128)(2,1)}, u32[]{:S(2)}, u32[]{:S(2)}) %all-to-all-start.7) | async-done | bytes 1572896 | tf_op jit(solution)/shard_map/all_to_all | solution.py:1269
  746.2 6.7 all-to-all-done.8
  762.8 10.3 %copy.178 = f32[3,256,2,1024]{3,2,1,0:T(2,128)} copy(f32[3,256,2,1024]{1,3,0,2:T(8,128)} %maximum_convert_fusion) | data formatting | bytes 12582912
  773.1 4.7 collective-permute-done.51
  (474 shorter events, 302.3 us)
Async XLA Ops:
  67.3 75.8 %all-to-all-start = ((bf16[8,1552,128]{2,1,0:T(8,128)(2,1)}), bf16[8,1552,128]{2,1,0:T(8,128)(2,1)S(1)}, u32[]{:S(2)}, u32[]{:S(2)}) async-start(bf16[8,1552,128]{2,1,0:T(8,128)(2,1)} %pad_maximum_fusion), calls=%async_computation | async-start | bytes 6356992 | tf_op jit(solution)/shard_map/all_to_all | solution.py:1269
  70.9 308.8 %all-gather.2.cloned.1.call-start = ((), (), s32[]{:S(2)}) async-start(), calls=%async_computation.9 | async-start | bytes 17301504 | tf_op jit(solution)/shard_map/all_gather | solution.py:1467
  87.8 55.2 %collective-permute-start.10 = (bf16[2,2,2,128,512]{4,3,2,1,0:T(8,128)(2,1)}, bf16[2,2,2,128,512]{4,3,2,1,0:T(8,128)(2,1)}, u32[]{:S(2)}, u32[]{:S(2)}) collective-permute-start(bf16[2,2,2,128,512]{4,3,2,1,0:T(8,128)(2,1)} %maximum_select_fusion.2.refs_0_), channel_id=1, source_target_pairs={{0,4},{4,0},{1,5},{5,1},{2,6},{6,2},{3,7},{7,3},{8,12},{12,8},{9,1... | collective-permute-start | bytes 3145736 | tf_op jit(solution)/shard_map/ppermute | solution.py:1278
  87.8 56.8 %collective-permute-start.9 = (bf16[2,2,2,128,512]{4,3,2,1,0:T(8,128)(2,1)}, bf16[2,2,2,128,512]{4,3,2,1,0:T(8,128)(2,1)}, u32[]{:S(2)}, u32[]{:S(2)}) collective-permute-start(bf16[2,2,2,128,512]{4,3,2,1,0:T(8,128)(2,1)} %maximum_select_fusion.2.refs_0_), channel_id=1, source_target_pairs={{0,2},{1,3},{2,0},{3,1},{4,6},{5,7},{6,4},{7,5},{8,10},{9,11},{10,... | collective-permute-start | bytes 3145736 | tf_op jit(solution)/shard_map/ppermute | solution.py:1278
  92.1 32.7 %collective-permute-start.20 = (bf16[2,2,128,512]{3,2,1,0:T(8,128)(2,1)S(1)}, bf16[2,2,128,512]{3,2,1,0:T(8,128)(2,1)S(1)}, u32[]{:S(2)}, u32[]{:S(2)}) collective-permute-start(bf16[2,2,128,512]{3,2,1,0:T(8,128)(2,1)S(1)} %copy-done.72), channel_id=1, source_target_pairs={{0,2},{1,3},{2,0},{3,1},{4,6},{5,7},{6,4},{7,5},{8,10},{9,11},{10,... | collective-permute-start | bytes 1572872 | tf_op jit(solution)/shard_map/ppermute | solution.py:1278
  95.0 51.1 %collective-permute-start.14 = (bf16[2,2,2,128,512]{4,3,2,1,0:T(8,128)(2,1)}, bf16[2,2,2,128,512]{4,3,2,1,0:T(8,128)(2,1)}, u32[]{:S(2)}, u32[]{:S(2)}) collective-permute-start(bf16[2,2,2,128,512]{4,3,2,1,0:T(8,128)(2,1)} %maximum_select_fusion.3.refs_4_), channel_id=1, source_target_pairs={{0,4},{4,0},{1,5},{5,1},{2,6},{6,2},{3,7},{7,3},{8,12},{12,8},{9,1... | collective-permute-start | bytes 3145736 | tf_op jit(solution)/shard_map/ppermute | solution.py:1278
  103.6 42.5 %collective-permute-start.13 = (bf16[2,2,2,128,512]{4,3,2,1,0:T(8,128)(2,1)}, bf16[2,2,2,128,512]{4,3,2,1,0:T(8,128)(2,1)}, u32[]{:S(2)}, u32[]{:S(2)}) collective-permute-start(bf16[2,2,2,128,512]{4,3,2,1,0:T(8,128)(2,1)} %maximum_select_fusion.3.refs_4_), channel_id=1, source_target_pairs={{0,1},{1,0},{2,3},{3,2},{4,5},{5,4},{6,7},{7,6},{8,9},{9,8},{10,11... | collective-permute-start | bytes 3145736 | tf_op jit(solution)/shard_map/ppermute | solution.py:1278
  143.1 25.0 %collective-permute-start.17 = (bf16[2,2,2,128,512]{4,3,2,1,0:T(8,128)(2,1)}, bf16[2,2,2,128,512]{4,3,2,1,0:T(8,128)(2,1)}, u32[]{:S(2)}, u32[]{:S(2)}) collective-permute-start(bf16[2,2,2,128,512]{4,3,2,1,0:T(8,128)(2,1)} %maximum_select_fusion.4.refs_8_), channel_id=1, source_target_pairs={{0,2},{1,3},{2,0},{3,1},{4,6},{5,7},{6,4},{7,5},{8,10},{9,11},{10,... | collective-permute-start | bytes 3145736 | tf_op jit(solution)/shard_map/ppermute | solution.py:1278
  146.1 27.6 %collective-permute-start.22 = (bf16[2,2,2,128,512]{4,3,2,1,0:T(8,128)(2,1)}, bf16[2,2,2,128,512]{4,3,2,1,0:T(8,128)(2,1)}, u32[]{:S(2)}, u32[]{:S(2)}) collective-permute-start(bf16[2,2,2,128,512]{4,3,2,1,0:T(8,128)(2,1)} %maximum_select_fusion.5.refs_12_), channel_id=1, source_target_pairs={{0,4},{4,0},{1,5},{5,1},{2,6},{6,2},{3,7},{7,3},{8,12},{12,8},{9,1... | collective-permute-start | bytes 3145736 | tf_op jit(solution)/shard_map/ppermute | solution.py:1278
  146.1 27.6 %collective-permute-start.11 = (bf16[2,2,2,128,512]{4,3,2,1,0:T(8,128)(2,1)}, bf16[2,2,2,128,512]{4,3,2,1,0:T(8,128)(2,1)}, u32[]{:S(2)}, u32[]{:S(2)}) collective-permute-start(bf16[2,2,2,128,512]{4,3,2,1,0:T(8,128)(2,1)} %collective-permute-done.9.refs_1_), channel_id=1, source_target_pairs={{0,4},{4,0},{1,5},{5,1},{2,6},{6,2},{3,7},{7,3},{8,12},{12,8},{9,1... | collective-permute-start | bytes 3145736 | tf_op jit(solution)/shard_map/ppermute | solution.py:1278
  146.6 27.1 %collective-permute-start.15 = (bf16[2,2,2,128,512]{4,3,2,1,0:T(8,128)(2,1)}, bf16[2,2,2,128,512]{4,3,2,1,0:T(8,128)(2,1)}, u32[]{:S(2)}, u32[]{:S(2)}) collective-permute-start(bf16[2,2,2,128,512]{4,3,2,1,0:T(8,128)(2,1)} %collective-permute-done.13.refs_5_), channel_id=1, source_target_pairs={{0,4},{4,0},{1,5},{5,1},{2,6},{6,2},{3,7},{7,3},{8,12},{12,8},{9,1... | collective-permute-start | bytes 3145736 | tf_op jit(solution)/shard_map/ppermute | solution.py:1278
  205.9 48.6 %all-to-all-start.1 = ((f32[16,160,128]{2,1,0:T(8,128)}), f32[16,160,128]{2,1,0:T(8,128)S(1)}, u32[]{:S(2)}, u32[]{:S(2)}) async-start(f32[16,160,128]{2,1,0:T(8,128)} %bitcast.342), calls=%async_computation.1 | async-start | bytes 2621440 | tf_op jit(solution)/shard_map/all_to_all | solution.py:1269
  316.1 63.5 %all-to-all-start.3 = ((bf16[8,768,128]{2,1,0:T(8,128)(2,1)}), bf16[8,768,128]{2,1,0:T(8,128)(2,1)S(1)}, u32[]{:S(2)}, u32[]{:S(2)}) async-start(bf16[8,768,128]{2,1,0:T(8,128)(2,1)} %bitcast.43), calls=%async_computation.3 | async-start | bytes 3145728 | tf_op jit(solution)/shard_map/all_to_all | solution.py:1269
  423.1 71.3 %collective-permute-start.30 = (bf16[2,2,2,128,1024]{4,3,1,0,2:T(8,128)(2,1)}, bf16[2,2,2,128,1024]{4,3,1,0,2:T(8,128)(2,1)}, u32[]{:S(2)}, u32[]{:S(2)}) collective-permute-start(bf16[2,2,2,128,1024]{4,3,1,0,2:T(8,128)(2,1)} %copy_bitcast_fusion.1), channel_id=1, source_target_pairs={{0,1},{1,0},{2,3},{3,2},{4,5},{5,4},{6,7},{7,6},{8,9},{9,8},{10,11... | collective-permute-start | bytes 6291464 | tf_op jit(solution)/shard_map/ppermute | solution.py:1278
  426.3 68.2 %collective-permute-start.31 = (bf16[2,2,2,128,1024]{4,3,1,0,2:T(8,128)(2,1)}, bf16[2,2,2,128,1024]{4,3,1,0,2:T(8,128)(2,1)}, u32[]{:S(2)}, u32[]{:S(2)}) collective-permute-start(bf16[2,2,2,128,1024]{4,3,1,0,2:T(8,128)(2,1)} %copy_bitcast_fusion), channel_id=1, source_target_pairs={{0,2},{1,3},{2,0},{3,1},{4,6},{5,7},{6,4},{7,5},{8,10},{9,11},{10,... | collective-permute-start | bytes 6291464 | tf_op jit(solution)/shard_map/ppermute | solution.py:1278
  503.6 85.5 %collective-permute-start.32 = (bf16[2,2,128,1024]{3,2,1,0:T(8,128)(2,1)}, bf16[2,2,128,1024]{3,2,1,0:T(8,128)(2,1)}, u32[]{:S(2)}, u32[]{:S(2)}) collective-permute-start(bf16[2,2,128,1024]{3,2,1,0:T(8,128)(2,1)} %fusion.7), channel_id=1, source_target_pairs={{0,2},{1,3},{2,0},{3,1},{4,6},{5,7},{6,4},{7,5},{8,10},{9,11},{10,... | collective-permute-start | bytes 3145736 | tf_op jit(solution)/shard_map/ppermute | solution.py:1278
  507.9 66.8 %collective-permute-start.35 = (bf16[2,2,128,1024]{3,2,1,0:T(8,128)(2,1)}, bf16[2,2,128,1024]{3,2,1,0:T(8,128)(2,1)}, u32[]{:S(2)}, u32[]{:S(2)}) collective-permute-start(bf16[2,2,128,1024]{3,2,1,0:T(8,128)(2,1)} %fusion.6), channel_id=1, source_target_pairs={{0,1},{1,0},{2,3},{3,2},{4,5},{5,4},{6,7},{7,6},{8,9},{9,8},{10,11... | collective-permute-start | bytes 3145736 | tf_op jit(solution)/shard_map/ppermute | solution.py:1278
  510.7 29.8 %all-to-all-start.4 = ((bf16[16,160,128]{2,1,0:T(8,128)(2,1)}), bf16[16,160,128]{2,1,0:T(8,128)(2,1)}, u32[]{:S(2)}, u32[]{:S(2)}) async-start(bf16[16,160,128]{2,1,0:T(8,128)(2,1)} %bitcast.352), calls=%async_computation.4 | async-start | bytes 1310720 | tf_op jit(solution)/shard_map/all_to_all | solution.py:1269
  589.1 86.9 %all-to-all-start.6 = ((bf16[8,256,768]{1,2,0:T(8,128)(2,1)}), bf16[8,256,768]{1,2,0:T(8,128)(2,1)}, u32[]{:S(2)}, u32[]{:S(2)}) async-start(bf16[8,256,768]{1,2,0:T(8,128)(2,1)} %pad_maximum_fusion.1), calls=%async_computation.6 | async-start | bytes 6291456 | tf_op jit(solution)/shard_map/all_to_all | solution.py:1269
  619.3 42.9 %collective-permute-start.42 = (bf16[2,2,2,128,512]{4,3,1,0,2:T(8,128)(2,1)}, bf16[2,2,2,128,512]{4,3,1,0,2:T(8,128)(2,1)}, u32[]{:S(2)}, u32[]{:S(2)}) collective-permute-start(bf16[2,2,2,128,512]{4,3,1,0,2:T(8,128)(2,1)} %copy_bitcast_fusion.2), channel_id=1, source_target_pairs={{0,2},{1,3},{2,0},{3,1},{4,6},{5,7},{6,4},{7,5},{8,10},{9,11},{10,... | collective-permute-start | bytes 3145736 | tf_op jit(solution)/shard_map/ppermute | solution.py:1278
  621.6 43.6 %collective-permute-start.41 = (bf16[2,2,2,128,512]{4,3,1,0,2:T(8,128)(2,1)}, bf16[2,2,2,128,512]{4,3,1,0,2:T(8,128)(2,1)}, u32[]{:S(2)}, u32[]{:S(2)}) collective-permute-start(bf16[2,2,2,128,512]{4,3,1,0,2:T(8,128)(2,1)} %copy_bitcast_fusion.3), channel_id=1, source_target_pairs={{0,1},{1,0},{2,3},{3,2},{4,5},{5,4},{6,7},{7,6},{8,9},{9,8},{10,11... | collective-permute-start | bytes 3145736 | tf_op jit(solution)/shard_map/ppermute | solution.py:1278
  624.8 45.6 %collective-permute-start.39 = (bf16[2,2,2,128,512]{4,3,1,0,2:T(8,128)(2,1)}, bf16[2,2,2,128,512]{4,3,1,0,2:T(8,128)(2,1)}, u32[]{:S(2)}, u32[]{:S(2)}) collective-permute-start(bf16[2,2,2,128,512]{4,3,1,0,2:T(8,128)(2,1)} %copy_bitcast_fusion.5), channel_id=1, source_target_pairs={{0,1},{1,0},{2,3},{3,2},{4,5},{5,4},{6,7},{7,6},{8,9},{9,8},{10,11... | collective-permute-start | bytes 3145736 | tf_op jit(solution)/shard_map/ppermute | solution.py:1278
  625.8 47.4 %collective-permute-start.40 = (bf16[2,2,2,128,512]{4,3,1,0,2:T(8,128)(2,1)}, bf16[2,2,2,128,512]{4,3,1,0,2:T(8,128)(2,1)}, u32[]{:S(2)}, u32[]{:S(2)}) collective-permute-start(bf16[2,2,2,128,512]{4,3,1,0,2:T(8,128)(2,1)} %copy_bitcast_fusion.4), channel_id=1, source_target_pairs={{0,2},{1,3},{2,0},{3,1},{4,6},{5,7},{6,4},{7,5},{8,10},{9,11},{10,... | collective-permute-start | bytes 3145736 | tf_op jit(solution)/shard_map/ppermute | solution.py:1278
  628.0 48.0 %collective-permute-start.38 = (bf16[2,128,2048]{2,1,0:T(8,128)(2,1)}, bf16[2,128,2048]{2,1,0:T(8,128)(2,1)}, u32[]{:S(2)}, u32[]{:S(2)}) collective-permute-start(bf16[2,128,2048]{2,1,0:T(8,128)(2,1)} %fusion.25), channel_id=1, source_target_pairs={{0,8},{8,0},{16,24},{24,16},{1,9},{9,1},{17,25},{25,17},{2,10},{10... | collective-permute-start | bytes 3145736 | tf_op jit(solution)/shard_map/ppermute | solution.py:1278
  664.3 31.3 %collective-permute-start.49 = (bf16[2,2,128,512]{3,2,1,0:T(8,128)(2,1)}, bf16[2,2,128,512]{3,2,1,0:T(8,128)(2,1)}, u32[]{:S(2)}, u32[]{:S(2)}) collective-permute-start(bf16[2,2,128,512]{3,2,1,0:T(8,128)(2,1)} %fusion.30), channel_id=1, source_target_pairs={{0,1},{1,0},{2,3},{3,2},{4,5},{5,4},{6,7},{7,6},{8,9},{9,8},{10,11... | collective-permute-start | bytes 1572872 | tf_op jit(solution)/shard_map/ppermute | solution.py:1278
  667.2 27.1 %collective-permute-start.48 = (bf16[2,2,128,512]{3,2,1,0:T(8,128)(2,1)}, bf16[2,2,128,512]{3,2,1,0:T(8,128)(2,1)}, u32[]{:S(2)}, u32[]{:S(2)}) collective-permute-start(bf16[2,2,128,512]{3,2,1,0:T(8,128)(2,1)} %fusion.31), channel_id=1, source_target_pairs={{0,2},{1,3},{2,0},{3,1},{4,6},{5,7},{6,4},{7,5},{8,10},{9,11},{10,... | collective-permute-start | bytes 1572872 | tf_op jit(solution)/shard_map/ppermute | solution.py:1278
  672.4 27.1 %collective-permute-start.44 = (bf16[2,2,128,512]{3,2,1,0:T(8,128)(2,1)}, bf16[2,2,128,512]{3,2,1,0:T(8,128)(2,1)}, u32[]{:S(2)}, u32[]{:S(2)}) collective-permute-start(bf16[2,2,128,512]{3,2,1,0:T(8,128)(2,1)} %fusion.33), channel_id=1, source_target_pairs={{0,2},{1,3},{2,0},{3,1},{4,6},{5,7},{6,4},{7,5},{8,10},{9,11},{10,... | collective-permute-start | bytes 1572872 | tf_op jit(solution)/shard_map/ppermute | solution.py:1278
  675.1 25.5 %collective-permute-start.45 = (bf16[2,2,128,512]{3,2,1,0:T(8,128)(2,1)}, bf16[2,2,128,512]{3,2,1,0:T(8,128)(2,1)}, u32[]{:S(2)}, u32[]{:S(2)}) collective-permute-start(bf16[2,2,128,512]{3,2,1,0:T(8,128)(2,1)} %fusion.32), channel_id=1, source_target_pairs={{0,1},{1,0},{2,3},{3,2},{4,5},{5,4},{6,7},{7,6},{8,9},{9,8},{10,11... | collective-permute-start | bytes 1572872 | tf_op jit(solution)/shard_map/ppermute | solution.py:1278
  678.6 55.0 %all-to-all-start.7 = ((bf16[8,256,384]{1,2,0:T(8,128)(2,1)}), bf16[8,256,384]{1,2,0:T(8,128)(2,1)}, u32[]{:S(2)}, u32[]{:S(2)}) async-start(bf16[8,256,384]{1,2,0:T(8,128)(2,1)} %copy.169), calls=%async_computation.7 | async-start | bytes 3145728 | tf_op jit(solution)/shard_map/all_to_all | solution.py:1269
  686.4 98.3 %collective-permute-start.43 = (bf16[128,2048]{1,0:T(8,128)(2,1)}, bf16[128,2048]{1,0:T(8,128)(2,1)}, u32[]{:S(2)}, u32[]{:S(2)}) collective-permute-start(bf16[128,2048]{1,0:T(8,128)(2,1)} %fusion.28), channel_id=1, source_target_pairs={{0,16},{8,24},{16,0},{24,8},{1,17},{9,25},{17,1},{25,9},{2,18},{10... | collective-permute-start | bytes 1572872 | tf_op jit(solution)/shard_map/ppermute | solution.py:1278
  698.0 55.7 %collective-permute-start.50 = (bf16[2,128,1024]{2,1,0:T(8,128)(2,1)}, bf16[2,128,1024]{2,1,0:T(8,128)(2,1)}, u32[]{:S(2)}, u32[]{:S(2)}) collective-permute-start(bf16[2,128,1024]{2,1,0:T(8,128)(2,1)} %fusion.35), channel_id=1, source_target_pairs={{0,8},{8,0},{16,24},{24,16},{1,9},{9,1},{17,25},{25,17},{2,10},{10... | collective-permute-start | bytes 1572872 | tf_op jit(solution)/shard_map/ppermute | solution.py:1278
  702.9 50.8 %collective-permute-start.46 = (bf16[2,128,1024]{2,1,0:T(8,128)(2,1)}, bf16[2,128,1024]{2,1,0:T(8,128)(2,1)}, u32[]{:S(2)}, u32[]{:S(2)}) collective-permute-start(bf16[2,128,1024]{2,1,0:T(8,128)(2,1)} %fusion.34), channel_id=1, source_target_pairs={{0,8},{8,0},{16,24},{24,16},{1,9},{9,1},{17,25},{25,17},{2,10},{10... | collective-permute-start | bytes 1572872 | tf_op jit(solution)/shard_map/ppermute | solution.py:1278
  (122 other events, 1412.7 us)
Sparse Core Ops, SparseCore 0:
  200.0 165.3 all-gather.1

commit v5 on v4

--- a/solution.py
+++ b/solution.py
@@ -1560,13 +1560,12 @@
     inner_low, more_low = lax.optimization_barrier((by_holder(inner_low), more_low))
     inner_low = exchange(inner_low, SEQ)
     step_grad_low = held_back(step_grad_low, sent)
+    for parts in normed_sums.parts[2:]:
+        parts[-1] = held_back(parts[-1], [more_low])
     sent = normed_sums.stage(("y", "x"))
     branch.hold(sent)
     branch.stage(("zh", "zh"))
     output = (token_vals + branch.result()).astype(bf16)
-    gain_sum = held_back(inner_gain + gate_gain, sent)
-    gain_sum, inner_low = lax.optimization_barrier((gain_sum, inner_low))
-    grad_gain = jnp.sum(share(gain_sum, SEQ + ("mod",)), axis=0) / gain_vals
     inner_low = inner_low.reshape(seqs, slab, MODS, channels)
     more_low = more_low.reshape(seqs, slab, 2, MODS, channels)
     grad_gate = more_low[:, :, 0].transpose(2, 1, 0, 3)
@@ -1577,9 +1576,6 @@
     feat_late, out_low = held_back((feat_grad, more_low[:, :, 1]), sent)
     grad_out = out_low.transpose(2, 0, 3, 1)
     grad_out = grad_out.reshape(MODS, seqs * channels, slab).astype(f32)
-    normed_sums.hold([grad_in, grad_gain])
-    normed_sums.stage(("zh", "zh"))
-    normed_grad = normed_sums.result()
     step_t = feats[:, :, :, :R].transpose(3, 1, 0, 2, 4).reshape(R, -1)
     grad_step = dot(step_t, masked(step_grad_low, ids))
     grad_step = grad_step.reshape(R, MODS, channels).transpose(1, 0, 2)
@@ -1590,6 +1586,11 @@
     ]
     grad_param = dot(jnp.concatenate(feat_late, axis=0), act_low)
     grad_param = grad_param.reshape(MODS, features, channels).transpose(0, 2, 1)
+    normed_sums.hold([grad_out, grad_param])
+    normed_sums.stage(("zh", "zh"))
+    gain_sum, grad_in = lax.optimization_barrier((inner_gain + gate_gain, grad_in))
+    grad_gain = jnp.sum(share(gain_sum, SEQ + ("mod",)), axis=0) / gain_vals
+    normed_grad, grad_gain = lax.optimization_barrier((normed_sums.result(), grad_gain))
     hat_grad = normed_grad * gain_vals[None, :]
     token_grad = cotangent.astype(f32) + inverse * (
         hat_grad - normal_rows * jnp.mean(hat_grad * normal_rows, axis=1, keepdims=True)

time: 807 us -> 827 us (1.025)
  waiting for transfers between devices: 159 us -> 179 us
    ppermute x52, waiting for transfers between devices: 94.6 us -> 139 us  [flip(): lax.ppermute(value, axis, [(i, i ^ bit) for i in range(size)])]
    all_to_all x6, waiting for transfers between devices: 56.7 us -> 39.3 us  [exchange(): return lax.all_to_all(blocks, axes, 0, 0)]
    unnamed x210 -> x226, local copies, waits for them, and re-layouts: 21.1 us -> 20.3 us
  transfers between devices with their start and end apart: 61 -> 61, of which waited for: 22 -> 23; matrix products, arithmetic and copies ran while one was open for 30% -> 28% of each run, Pallas kernels for 19% -> 19%
where the time goes in v5:
time: 827 us; the launch traced here: 816 us
  Pallas kernels  202 us (24%)
  waiting for transfers between devices  179 us (22%)
  starting transfers between devices  98 us (12%)
  local copies, waits for them, and re-layouts  96.9 us (12%)
  other arithmetic  95.1 us (11%)
  matrix products  72.6 us (9%)
  blocking collectives  56.1 us (7%)
  between operations  15.9 us (2%)
    ppermute x52, waiting for transfers between devices, flip(): lax.ppermute(value, axis, [(i, i ^ bit) for i in range(size)])  139 us
    dot_general x17, matrix products, dot(): lax.dot_general(left, right, (((left_dim,), (right_dim,)), ((), ())), pre...  72.6 us
    pallas_call x1, Pallas kernels, scan_back(): pl.pallas_call(back_kernel, grid=(chunks,), in_specs=[pl.BlockSpec(memory...  67.3 us
    ppermute x52, starting transfers between devices, flip(): lax.ppermute(value, axis, [(i, i ^ bit) for i in range(size)])  58.1 us
    all_to_all x1, blocking collectives, share(): lax.all_to_all(jnp.broadcast_to(values, (size,) + values.shape), axes, 0, 0)  56.1 us
    pallas_call x1, Pallas kernels, scan(): pl.pallas_call(scan_kernel, grid=(length // steps,), in_specs=[pl.BlockSp...  53.8 us
    all_to_all x6, waiting for transfers between devices, exchange(): return lax.all_to_all(blocks, axes, 0, 0)  39.3 us
    all_to_all x6, starting transfers between devices, exchange(): return lax.all_to_all(blocks, axes, 0, 0)  30.7 us
  transfers between devices with their start and end apart: 61, of which 23 were waited for; matrix products, arithmetic and copies ran while one was open for 28% of the time, Pallas kernels for 19%

profile of v5, /device:TPU:0, one launch (start us, length us, event | category | flops | bytes accessed | tf_op | source)
XLA Modules:
  0.0 815.7 jit_solution(1174715708098385490)
XLA Ops:
  15.3 6.3 collective-permute-done
  25.8 5.1 collective-permute-done.1
  38.5 6.3 collective-permute-done.2
  76.6 8.9 %collective-permute-done.8 = bf16[2,2,128,512]{3,2,1,0:T(8,128)(2,1)} collective-permute-done((bf16[2,2,128,512]{3,2,1,0:T(8,128)(2,1)}, bf16[2,2,128,512]{3,2,1,0:T(8,128)(2,1)}, u32[]{:S(2)}, u32[]{:S(2)}) %collective-permute-start.8) | collective-permute-done | bytes 524320 | tf_op jit(solution)/shard_map/ppermute | solution.py:1278
  95.1 8.5 %collective-permute-done.16 = bf16[2,2,128,512]{3,2,1,0:T(8,128)(2,1)S(1)} collective-permute-done((bf16[2,2,128,512]{3,2,1,0:T(8,128)(2,1)S(1)}, bf16[2,2,128,512]{3,2,1,0:T(8,128)(2,1)S(1)}, u32[]{:S(2)}, u32[]{:S(2)}) %collective-permute-start.16) | collective-permute-done | bytes 524320 | tf_op jit(solution)/shard_map/ppermute | solution.py:1278
  106.2 18.6 %collective-permute-done.20 = bf16[2,2,128,512]{3,2,1,0:T(8,128)(2,1)S(1)} collective-permute-done((bf16[2,2,128,512]{3,2,1,0:T(8,128)(2,1)S(1)}, bf16[2,2,128,512]{3,2,1,0:T(8,128)(2,1)S(1)}, u32[]{:S(2)}, u32[]{:S(2)}) %collective-permute-start.20) | collective-permute-done | bytes 524320 | tf_op jit(solution)/shard_map/ppermute | solution.py:1278
  126.1 17.0 %all-to-all-done.refs_18_ = bf16[8,1552,128]{2,1,0:T(8,128)(2,1)S(1)} async-done(((bf16[8,1552,128]{2,1,0:T(8,128)(2,1)}), bf16[8,1552,128]{2,1,0:T(8,128)(2,1)S(1)}, u32[]{:S(2)}, u32[]{:S(2)}) %all-to-all-start) | async-done | bytes 3178528 | tf_op jit(solution)/shard_map/all_to_all | solution.py:1269
  146.7 21.4 %collective-permute-done.17.refs_9_ = bf16[2,2,2,128,512]{4,3,2,1,0:T(8,128)(2,1)} collective-permute-done((bf16[2,2,2,128,512]{4,3,2,1,0:T(8,128)(2,1)}, bf16[2,2,2,128,512]{4,3,2,1,0:T(8,128)(2,1)}, u32[]{:S(2)}, u32[]{:S(2)}) %collective-permute-start.17) | collective-permute-done | bytes 1048608 | tf_op jit(solution)/shard_map/ppermute | solution.py:1278
  173.8 26.1 %project.1 = (bf16[4096,512]{1,0:T(8,128)(2,1)}, bf16[4096,512]{1,0:T(8,128)(2,1)}, bf16[4096,512]{1,0:T(8,128)(2,1)}, bf16[4096,512]{1,0:T(8,128)(2,1)}, bf16[2...) custom-call(s32[2]{0:T(128)} %lengths.5, ...), custom_call_target="tpu_custom_call" | custom-call | bytes 3690000 | tf_op jit(solution)/shard_map/project/pallas_call | solution.py:597
  212.6 14.8 %modal_rows.1.pre = f32[4096,128]{1,0:T(8,128)} custom-call(bf16[4096,512]{1,0:T(8,128)(2,1)} %get-tuple-element.102.refs_0_, bf16[4096,512]{1,0:T(8,128)(2,1)} %get-tuple-element.103.refs_1_, bf16[4096,512]{1,0:T(8,128)(2,1)} %get-tuple-element.104.refs_2_, bf16[4096,512]{1,0:T(8,128)(2,1)} %get-tuple-element.105.refs_3_, s32[4096,1]{1,0:T(8,128)} %copy.146.refs_4_, ...), custom_call_target="tpu_custom_call" | custom-call | bytes 3690000 | tf_op jit(solution)/shard_map/modal_rows/pallas_call | solution.py:640
  227.4 5.9 side_by_side.2
  233.3 21.3 %all-to-all-done.1 = f32[16,160,128]{2,1,0:T(8,128)S(1)} async-done(((f32[16,160,128]{2,1,0:T(8,128)}), f32[16,160,128]{2,1,0:T(8,128)S(1)}, u32[]{:S(2)}, u32[]{:S(2)}) %all-to-all-start.1) | async-done | bytes 1310752 | tf_op jit(solution)/shard_map/all_to_all | solution.py:1269
  254.8 56.1 %all_to_all.46 = bf16[16,192,128]{2,1,0:T(8,128)(2,1)S(1)} all-to-all(bf16[16,192,128]{2,1,0:T(8,128)(2,1)S(1)} %broadcast_in_dim.129), channel_id=1, replica_groups=mesh['z'=4,'core'=2,'mod'=4] {'z','mod'}, dimensions={0} | all-to-all | bytes 1572864 | tf_op jit(solution)/shard_map/all_to_all | solution.py:1265
  316.3 6.8 all-to-all-start.3
  326.0 53.8 %scan.1 = (f32[32,2048,128]{2,1,0:T(8,128)}, f32[2048,128]{1,0:T(8,128)}, f32[4096,128]{1,0:T(8,128)}, f32[4096,128]{1,0:T(8,128)}, f32[4096,128]{1,0:T(8,128)},...) custom-call(s32[2]{0:T(128)} %lengths.5, s32[4096,1]{1,0:T(8,128)} %copy.144.refs_16_.ids_ref, ...), custom_call_target="tpu_custom_call" | custom-call | bytes 3690000 | tf_op jit(solution)/shard_map/scan/pallas_call | solution.py:926
  381.0 18.1 %gates.1 = (bf16[2048,384]{1,0:T(8,128)(2,1)}, f32[4096,128]{1,0:T(8,128)}, bf16[4096,384]{1,0:T(8,128)(2,1)}, bf16[4096,384]{1,0:T(8,128)(2,1)}, bf16[4096,128]{1,0:T(8,128)(2,1)}, /*index=5*/bf16[4096,128]{1,0:T(8,128)(2,1)}) custom-call(bf16[4096,2048]{1,0:T(8,128)(2,1)} %all-gather.2.cloned.1.call-done.cot, s32[4096,1]{1,0:T(8,128)} %copy.144.refs_16_.ids_ref, ...), custom_call_target="tpu_custom_call" | custom-call | bytes 3690000 | tf_op jit(solution)/shard_map/gates/pallas_call | solution.py:705
  411.6 6.0 convolution_convert_fusion
  427.2 67.3 %scan_back.1 = (f32[4096,128]{1,0:T(8,128)}, bf16[4096,128]{1,0:T(8,128)(2,1)}, f32[2,4,4,160,128]{4,3,2,1,0:T(8,128)}, f32[8,128]{1,0:T(8,128)}, f32[128,128]{1,0:T(8,128)}) custom-call(s32[3]{0:T(128)} %pad_add_fusion.place.core, s32[4096,1]{1,0:T(8,128)} %copy.144.refs_16_.ids_ref, s32[32,128]{1,0:T(8,128)} %reshape.1124.refs_17_.ids_rows, ...), custom_call_target="tpu_custom_call" | custom-call | bytes 3690000 | tf_op jit(solution)/shard_map/scan_back/pallas_call | solution.py:1134
  510.8 6.7 all-to-all-start.4
  517.5 5.6 fusion.62
  526.4 13.4 %convolution_convert_fusion.6 = bf16[2048,384]{1,0:T(8,128)(2,1)} fusion(bf16[4096,2048]{1,0:T(8,128)(2,1)} %all-gather.2.cloned.1.call-done.cot, bf16[4096,384]{1,0:T(8,128)(2,1)S(1)} %copy-done.95), kind=kOutput, calls=%fused_computation.17 | convolution fusion | flops 6443237376 | bytes 21495808 | tf_op jit(solution)/shard_map/dot_general | solution.py:479
  542.8 6.5 all-to-all-start.5
  549.4 4.7 fusion.60
  574.8 11.9 %conv_back.1 = (bf16[4096,384]{1,0:T(8,128)(2,1)}, bf16[4096,128]{1,0:T(8,128)(2,1)}, f32[8,128]{1,0:T(8,128)}) custom-call(s32[2]{0:T(128)} %lengths.5, s32[4096,1]{1,0:T(8,128)} %copy.144.refs_16_.ids_ref, bf16[2,4,4,160,128]{4,3,2,1,0:T(8,128)(2,1)} %maximum_select_fusion.1.feat_grad, f32[4096,128]{1,0:T(8,128)} %get-tuple-element.138.act_part, ...), custom_call_target="tpu_custom_call" | custom-call | bytes 3690000 | tf_op jit(solution)/shard_map/conv_back/pallas_call | solution.py:1230
  589.1 5.0 all-to-all-start.6
  637.6 5.5 multiply_reduce_fusion.7
  662.5 7.8 collective-permute-done.39
  677.7 7.0 collective-permute-done.44
  734.8 17.7 %collective-permute-done.50 = bf16[2,128,1024]{2,1,0:T(8,128)(2,1)} collective-permute-done((bf16[2,128,1024]{2,1,0:T(8,128)(2,1)}, bf16[2,128,1024]{2,1,0:T(8,128)(2,1)}, u32[]{:S(2)}, u32[]{:S(2)}) %collective-permute-start.50) | collective-permute-done | bytes 524320 | tf_op jit(solution)/shard_map/ppermute | solution.py:1278
  754.4 4.7 collective-permute-start.51
  767.5 16.3 %collective-permute-done.49 = bf16[128,1024]{1,0:T(8,128)(2,1)} collective-permute-done((bf16[128,1024]{1,0:T(8,128)(2,1)}, bf16[128,1024]{1,0:T(8,128)(2,1)}, u32[]{:S(2)}, u32[]{:S(2)}) %collective-permute-start.49) | collective-permute-done | bytes 262176 | tf_op jit(solution)/shard_map/ppermute | solution.py:1278
  791.8 10.3 %copy.178 = f32[3,256,2,1024]{3,2,1,0:T(2,128)} copy(f32[3,256,2,1024]{1,3,0,2:T(8,128)} %maximum_convert_fusion) | data formatting | bytes 12582912
  (491 shorter events, 308.3 us)
Async XLA Ops:
  67.3 75.8 %all-to-all-start = ((bf16[8,1552,128]{2,1,0:T(8,128)(2,1)}), bf16[8,1552,128]{2,1,0:T(8,128)(2,1)S(1)}, u32[]{:S(2)}, u32[]{:S(2)}) async-start(bf16[8,1552,128]{2,1,0:T(8,128)(2,1)} %pad_maximum_fusion), calls=%async_computation | async-start | bytes 6356992 | tf_op jit(solution)/shard_map/all_to_all | solution.py:1269
  70.9 308.9 %all-gather.2.cloned.1.call-start = ((), (), s32[]{:S(2)}) async-start(), calls=%async_computation.9 | async-start | bytes 17301504 | tf_op jit(solution)/shard_map/all_gather | solution.py:1467
  87.8 55.3 %collective-permute-start.10 = (bf16[2,2,2,128,512]{4,3,2,1,0:T(8,128)(2,1)}, bf16[2,2,2,128,512]{4,3,2,1,0:T(8,128)(2,1)}, u32[]{:S(2)}, u32[]{:S(2)}) collective-permute-start(bf16[2,2,2,128,512]{4,3,2,1,0:T(8,128)(2,1)} %maximum_select_fusion.2.refs_0_), channel_id=1, source_target_pairs={{0,4},{4,0},{1,5},{5,1},{2,6},{6,2},{3,7},{7,3},{8,12},{12,8},{9,1... | collective-permute-start | bytes 3145736 | tf_op jit(solution)/shard_map/ppermute | solution.py:1278
  87.8 56.8 %collective-permute-start.9 = (bf16[2,2,2,128,512]{4,3,2,1,0:T(8,128)(2,1)}, bf16[2,2,2,128,512]{4,3,2,1,0:T(8,128)(2,1)}, u32[]{:S(2)}, u32[]{:S(2)}) collective-permute-start(bf16[2,2,2,128,512]{4,3,2,1,0:T(8,128)(2,1)} %maximum_select_fusion.2.refs_0_), channel_id=1, source_target_pairs={{0,2},{1,3},{2,0},{3,1},{4,6},{5,7},{6,4},{7,5},{8,10},{9,11},{10,... | collective-permute-start | bytes 3145736 | tf_op jit(solution)/shard_map/ppermute | solution.py:1278
  92.1 32.7 %collective-permute-start.20 = (bf16[2,2,128,512]{3,2,1,0:T(8,128)(2,1)S(1)}, bf16[2,2,128,512]{3,2,1,0:T(8,128)(2,1)S(1)}, u32[]{:S(2)}, u32[]{:S(2)}) collective-permute-start(bf16[2,2,128,512]{3,2,1,0:T(8,128)(2,1)S(1)} %copy-done.72), channel_id=1, source_target_pairs={{0,2},{1,3},{2,0},{3,1},{4,6},{5,7},{6,4},{7,5},{8,10},{9,11},{10,... | collective-permute-start | bytes 1572872 | tf_op jit(solution)/shard_map/ppermute | solution.py:1278
  95.0 51.2 %collective-permute-start.14 = (bf16[2,2,2,128,512]{4,3,2,1,0:T(8,128)(2,1)}, bf16[2,2,2,128,512]{4,3,2,1,0:T(8,128)(2,1)}, u32[]{:S(2)}, u32[]{:S(2)}) collective-permute-start(bf16[2,2,2,128,512]{4,3,2,1,0:T(8,128)(2,1)} %maximum_select_fusion.3.refs_4_), channel_id=1, source_target_pairs={{0,4},{4,0},{1,5},{5,1},{2,6},{6,2},{3,7},{7,3},{8,12},{12,8},{9,1... | collective-permute-start | bytes 3145736 | tf_op jit(solution)/shard_map/ppermute | solution.py:1278
  103.6 42.6 %collective-permute-start.13 = (bf16[2,2,2,128,512]{4,3,2,1,0:T(8,128)(2,1)}, bf16[2,2,2,128,512]{4,3,2,1,0:T(8,128)(2,1)}, u32[]{:S(2)}, u32[]{:S(2)}) collective-permute-start(bf16[2,2,2,128,512]{4,3,2,1,0:T(8,128)(2,1)} %maximum_select_fusion.3.refs_4_), channel_id=1, source_target_pairs={{0,1},{1,0},{2,3},{3,2},{4,5},{5,4},{6,7},{7,6},{8,9},{9,8},{10,11... | collective-permute-start | bytes 3145736 | tf_op jit(solution)/shard_map/ppermute | solution.py:1278
  143.1 25.0 %collective-permute-start.17 = (bf16[2,2,2,128,512]{4,3,2,1,0:T(8,128)(2,1)}, bf16[2,2,2,128,512]{4,3,2,1,0:T(8,128)(2,1)}, u32[]{:S(2)}, u32[]{:S(2)}) collective-permute-start(bf16[2,2,2,128,512]{4,3,2,1,0:T(8,128)(2,1)} %maximum_select_fusion.4.refs_8_), channel_id=1, source_target_pairs={{0,2},{1,3},{2,0},{3,1},{4,6},{5,7},{6,4},{7,5},{8,10},{9,11},{10,... | collective-permute-start | bytes 3145736 | tf_op jit(solution)/shard_map/ppermute | solution.py:1278
  144.6 24.7 %collective-permute-start.21 = (bf16[2,2,2,128,512]{4,3,2,1,0:T(8,128)(2,1)}, bf16[2,2,2,128,512]{4,3,2,1,0:T(8,128)(2,1)}, u32[]{:S(2)}, u32[]{:S(2)}) collective-permute-start(bf16[2,2,2,128,512]{4,3,2,1,0:T(8,128)(2,1)} %maximum_select_fusion.5.refs_12_), channel_id=1, source_target_pairs={{0,1},{1,0},{2,3},{3,2},{4,5},{5,4},{6,7},{7,6},{8,9},{9,8},{10,11... | collective-permute-start | bytes 3145736 | tf_op jit(solution)/shard_map/ppermute | solution.py:1278
  146.1 27.7 %collective-permute-start.22 = (bf16[2,2,2,128,512]{4,3,2,1,0:T(8,128)(2,1)}, bf16[2,2,2,128,512]{4,3,2,1,0:T(8,128)(2,1)}, u32[]{:S(2)}, u32[]{:S(2)}) collective-permute-start(bf16[2,2,2,128,512]{4,3,2,1,0:T(8,128)(2,1)} %maximum_select_fusion.5.refs_12_), channel_id=1, source_target_pairs={{0,4},{4,0},{1,5},{5,1},{2,6},{6,2},{3,7},{7,3},{8,12},{12,8},{9,1... | collective-permute-start | bytes 3145736 | tf_op jit(solution)/shard_map/ppermute | solution.py:1278
  146.1 27.7 %collective-permute-start.11 = (bf16[2,2,2,128,512]{4,3,2,1,0:T(8,128)(2,1)}, bf16[2,2,2,128,512]{4,3,2,1,0:T(8,128)(2,1)}, u32[]{:S(2)}, u32[]{:S(2)}) collective-permute-start(bf16[2,2,2,128,512]{4,3,2,1,0:T(8,128)(2,1)} %collective-permute-done.9.refs_1_), channel_id=1, source_target_pairs={{0,4},{4,0},{1,5},{5,1},{2,6},{6,2},{3,7},{7,3},{8,12},{12,8},{9,1... | collective-permute-start | bytes 3145736 | tf_op jit(solution)/shard_map/ppermute | solution.py:1278
  146.6 27.2 %collective-permute-start.15 = (bf16[2,2,2,128,512]{4,3,2,1,0:T(8,128)(2,1)}, bf16[2,2,2,128,512]{4,3,2,1,0:T(8,128)(2,1)}, u32[]{:S(2)}, u32[]{:S(2)}) collective-permute-start(bf16[2,2,2,128,512]{4,3,2,1,0:T(8,128)(2,1)} %collective-permute-done.13.refs_5_), channel_id=1, source_target_pairs={{0,4},{4,0},{1,5},{5,1},{2,6},{6,2},{3,7},{7,3},{8,12},{12,8},{9,1... | collective-permute-start | bytes 3145736 | tf_op jit(solution)/shard_map/ppermute | solution.py:1278
  206.0 48.6 %all-to-all-start.1 = ((f32[16,160,128]{2,1,0:T(8,128)}), f32[16,160,128]{2,1,0:T(8,128)S(1)}, u32[]{:S(2)}, u32[]{:S(2)}) async-start(f32[16,160,128]{2,1,0:T(8,128)} %bitcast.342), calls=%async_computation.1 | async-start | bytes 2621440 | tf_op jit(solution)/shard_map/all_to_all | solution.py:1269
  316.3 63.6 %all-to-all-start.3 = ((bf16[8,768,128]{2,1,0:T(8,128)(2,1)}), bf16[8,768,128]{2,1,0:T(8,128)(2,1)S(1)}, u32[]{:S(2)}, u32[]{:S(2)}) async-start(bf16[8,768,128]{2,1,0:T(8,128)(2,1)} %bitcast.43), calls=%async_computation.3 | async-start | bytes 3145728 | tf_op jit(solution)/shard_map/all_to_all | solution.py:1269
  423.3 71.3 %collective-permute-start.30 = (bf16[2,2,2,128,1024]{4,3,1,0,2:T(8,128)(2,1)}, bf16[2,2,2,128,1024]{4,3,1,0,2:T(8,128)(2,1)}, u32[]{:S(2)}, u32[]{:S(2)}) collective-permute-start(bf16[2,2,2,128,1024]{4,3,1,0,2:T(8,128)(2,1)} %copy_bitcast_fusion.1), channel_id=1, source_target_pairs={{0,1},{1,0},{2,3},{3,2},{4,5},{5,4},{6,7},{7,6},{8,9},{9,8},{10,11... | collective-permute-start | bytes 6291464 | tf_op jit(solution)/shard_map/ppermute | solution.py:1278
  426.3 68.2 %collective-permute-start.31 = (bf16[2,2,2,128,1024]{4,3,1,0,2:T(8,128)(2,1)}, bf16[2,2,2,128,1024]{4,3,1,0,2:T(8,128)(2,1)}, u32[]{:S(2)}, u32[]{:S(2)}) collective-permute-start(bf16[2,2,2,128,1024]{4,3,1,0,2:T(8,128)(2,1)} %copy_bitcast_fusion), channel_id=1, source_target_pairs={{0,2},{1,3},{2,0},{3,1},{4,6},{5,7},{6,4},{7,5},{8,10},{9,11},{10,... | collective-permute-start | bytes 6291464 | tf_op jit(solution)/shard_map/ppermute | solution.py:1278
  503.8 85.3 %collective-permute-start.32 = (bf16[2,2,128,1024]{3,2,1,0:T(8,128)(2,1)}, bf16[2,2,128,1024]{3,2,1,0:T(8,128)(2,1)}, u32[]{:S(2)}, u32[]{:S(2)}) collective-permute-start(bf16[2,2,128,1024]{3,2,1,0:T(8,128)(2,1)} %fusion.7), channel_id=1, source_target_pairs={{0,2},{1,3},{2,0},{3,1},{4,6},{5,7},{6,4},{7,5},{8,10},{9,11},{10,... | collective-permute-start | bytes 3145736 | tf_op jit(solution)/shard_map/ppermute | solution.py:1278
  508.0 66.7 %collective-permute-start.35 = (bf16[2,2,128,1024]{3,2,1,0:T(8,128)(2,1)}, bf16[2,2,128,1024]{3,2,1,0:T(8,128)(2,1)}, u32[]{:S(2)}, u32[]{:S(2)}) collective-permute-start(bf16[2,2,128,1024]{3,2,1,0:T(8,128)(2,1)} %fusion.6), channel_id=1, source_target_pairs={{0,1},{1,0},{2,3},{3,2},{4,5},{5,4},{6,7},{7,6},{8,9},{9,8},{10,11... | collective-permute-start | bytes 3145736 | tf_op jit(solution)/shard_map/ppermute | solution.py:1278
  510.8 29.8 %all-to-all-start.4 = ((bf16[16,160,128]{2,1,0:T(8,128)(2,1)}), bf16[16,160,128]{2,1,0:T(8,128)(2,1)}, u32[]{:S(2)}, u32[]{:S(2)}) async-start(bf16[16,160,128]{2,1,0:T(8,128)(2,1)} %bitcast.352), calls=%async_computation.4 | async-start | bytes 1310720 | tf_op jit(solution)/shard_map/all_to_all | solution.py:1269
  589.1 99.9 %all-to-all-start.6 = ((bf16[8,256,768]{1,2,0:T(8,128)(2,1)}), bf16[8,256,768]{1,2,0:T(8,128)(2,1)}, u32[]{:S(2)}, u32[]{:S(2)}) async-start(bf16[8,256,768]{1,2,0:T(8,128)(2,1)} %pad_maximum_fusion.1), calls=%async_computation.6 | async-start | bytes 6291456 | tf_op jit(solution)/shard_map/all_to_all | solution.py:1269
  619.8 71.8 %collective-permute-start.42 = (bf16[2,2,2,128,512]{4,3,1,0,2:T(8,128)(2,1)}, bf16[2,2,2,128,512]{4,3,1,0,2:T(8,128)(2,1)}, u32[]{:S(2)}, u32[]{:S(2)}) collective-permute-start(bf16[2,2,2,128,512]{4,3,1,0,2:T(8,128)(2,1)} %copy_bitcast_fusion.2), channel_id=1, source_target_pairs={{0,2},{1,3},{2,0},{3,1},{4,6},{5,7},{6,4},{7,5},{8,10},{9,11},{10,... | collective-permute-start | bytes 3145736 | tf_op jit(solution)/shard_map/ppermute | solution.py:1278
  622.3 69.3 %collective-permute-start.41 = (bf16[2,2,2,128,512]{4,3,1,0,2:T(8,128)(2,1)}, bf16[2,2,2,128,512]{4,3,1,0,2:T(8,128)(2,1)}, u32[]{:S(2)}, u32[]{:S(2)}) collective-permute-start(bf16[2,2,2,128,512]{4,3,1,0,2:T(8,128)(2,1)} %copy_bitcast_fusion.3), channel_id=1, source_target_pairs={{0,1},{1,0},{2,3},{3,2},{4,5},{5,4},{6,7},{7,6},{8,9},{9,8},{10,11... | collective-permute-start | bytes 3145736 | tf_op jit(solution)/shard_map/ppermute | solution.py:1278
  625.8 44.5 %collective-permute-start.39 = (bf16[2,2,2,128,512]{4,3,1,0,2:T(8,128)(2,1)}, bf16[2,2,2,128,512]{4,3,1,0,2:T(8,128)(2,1)}, u32[]{:S(2)}, u32[]{:S(2)}) collective-permute-start(bf16[2,2,2,128,512]{4,3,1,0,2:T(8,128)(2,1)} %copy_bitcast_fusion.5), channel_id=1, source_target_pairs={{0,1},{1,0},{2,3},{3,2},{4,5},{5,4},{6,7},{7,6},{8,9},{9,8},{10,11... | collective-permute-start | bytes 3145736 | tf_op jit(solution)/shard_map/ppermute | solution.py:1278
  626.3 45.8 %collective-permute-start.40 = (bf16[2,2,2,128,512]{4,3,1,0,2:T(8,128)(2,1)}, bf16[2,2,2,128,512]{4,3,1,0,2:T(8,128)(2,1)}, u32[]{:S(2)}, u32[]{:S(2)}) collective-permute-start(bf16[2,2,2,128,512]{4,3,1,0,2:T(8,128)(2,1)} %copy_bitcast_fusion.4), channel_id=1, source_target_pairs={{0,2},{1,3},{2,0},{3,1},{4,6},{5,7},{6,4},{7,5},{8,10},{9,11},{10,... | collective-permute-start | bytes 3145736 | tf_op jit(solution)/shard_map/ppermute | solution.py:1278
  630.8 68.0 %collective-permute-start.38 = (bf16[2,128,2048]{2,1,0:T(8,128)(2,1)}, bf16[2,128,2048]{2,1,0:T(8,128)(2,1)}, u32[]{:S(2)}, u32[]{:S(2)}) collective-permute-start(bf16[2,128,2048]{2,1,0:T(8,128)(2,1)} %fusion.25), channel_id=1, source_target_pairs={{0,8},{8,0},{16,24},{24,16},{1,9},{9,1},{17,25},{25,17},{2,10},{10... | collective-permute-start | bytes 3145736 | tf_op jit(solution)/shard_map/ppermute | solution.py:1278
  687.7 44.5 %collective-permute-start.46 = (bf16[2,128,1024]{2,1,0:T(8,128)(2,1)}, bf16[2,128,1024]{2,1,0:T(8,128)(2,1)}, u32[]{:S(2)}, u32[]{:S(2)}) collective-permute-start(bf16[2,128,1024]{2,1,0:T(8,128)(2,1)} %fusion.34), channel_id=1, source_target_pairs={{0,8},{8,0},{16,24},{24,16},{1,9},{9,1},{17,25},{25,17},{2,10},{10... | collective-permute-start | bytes 1572872 | tf_op jit(solution)/shard_map/ppermute | solution.py:1278
  698.8 60.3 %all-to-all-start.7 = ((bf16[8,256,384]{1,2,0:T(8,128)(2,1)}), bf16[8,256,384]{1,2,0:T(8,128)(2,1)}, u32[]{:S(2)}, u32[]{:S(2)}) async-start(bf16[8,256,384]{1,2,0:T(8,128)(2,1)} %copy.171), calls=%async_computation.7 | async-start | bytes 3145728 | tf_op jit(solution)/shard_map/all_to_all | solution.py:1269
  705.8 98.9 %collective-permute-start.43 = (bf16[128,2048]{1,0:T(8,128)(2,1)}, bf16[128,2048]{1,0:T(8,128)(2,1)}, u32[]{:S(2)}, u32[]{:S(2)}) collective-permute-start(bf16[128,2048]{1,0:T(8,128)(2,1)} %fusion.28), channel_id=1, source_target_pairs={{0,16},{8,24},{16,0},{24,8},{1,17},{9,25},{17,1},{25,9},{2,18},{10... | collective-permute-start | bytes 1572872 | tf_op jit(solution)/shard_map/ppermute | solution.py:1278
  719.3 33.2 %collective-permute-start.50 = (bf16[2,128,1024]{2,1,0:T(8,128)(2,1)}, bf16[2,128,1024]{2,1,0:T(8,128)(2,1)}, u32[]{:S(2)}, u32[]{:S(2)}) collective-permute-start(bf16[2,128,1024]{2,1,0:T(8,128)(2,1)} %fusion.35), channel_id=1, source_target_pairs={{0,8},{8,0},{16,24},{24,16},{1,9},{9,1},{17,25},{25,17},{2,10},{10... | collective-permute-start | bytes 1572872 | tf_op jit(solution)/shard_map/ppermute | solution.py:1278
  734.2 49.6 %collective-permute-start.49 = (bf16[128,1024]{1,0:T(8,128)(2,1)}, bf16[128,1024]{1,0:T(8,128)(2,1)}, u32[]{:S(2)}, u32[]{:S(2)}) collective-permute-start(bf16[128,1024]{1,0:T(8,128)(2,1)} %fusion.46), channel_id=1, source_target_pairs={{0,16},{8,24},{16,0},{24,8},{1,17},{9,25},{17,1},{25,9},{2,18},{10... | collective-permute-start | bytes 786440 | tf_op jit(solution)/shard_map/ppermute | solution.py:1278
  754.4 35.0 %collective-permute-start.51 = (bf16[128,1024]{1,0:T(8,128)(2,1)}, bf16[128,1024]{1,0:T(8,128)(2,1)}, u32[]{:S(2)}, u32[]{:S(2)}) collective-permute-start(bf16[128,1024]{1,0:T(8,128)(2,1)} %fusion.44), channel_id=1, source_target_pairs={{0,16},{8,24},{16,0},{24,8},{1,17},{9,25},{17,1},{25,9},{2,18},{10... | collective-permute-start | bytes 786440 | tf_op jit(solution)/shard_map/ppermute | solution.py:1278
  764.9 37.3 %all-to-all-start.8 = ((f32[32,1,2048]{2,1,0:T(1,128)}), f32[32,1,2048]{2,1,0:T(1,128)S(1)}, u32[]{:S(2)}, u32[]{:S(2)}) async-start(f32[32,1,2048]{2,1,0:T(1,128)} %broadcast_in_dim.138), calls=%async_computation.8 | async-start | bytes 524288 | tf_op jit(solution)/shard_map/all_to_all | solution.py:1265
  (130 other events, 1627.2 us)
Sparse Core Ops, SparseCore 0:
  200.1 165.2 all-gather.1
